TPU v7x, 32 devices: a whole 2x2x4 slice. The times are simulated.
32 devices in a mesh: tp: 4 (over y, x), ep: 8 (over z, core).
Axes of the slice: x: 2, y: 2, z: 4, core: 2. Of those that a mesh axis runs over, the one named last changes fastest.
Arguments:
- tokens: bfloat16 [1024, 5120], P('ep', 'tp'), may hold values from -6 to 6
- cotangent: bfloat16 [1024, 5120], P('ep', 'tp'), may hold values from -6 to 6
- expert_ids: int32 [1024, 3], P('ep'), may hold values from 0 to 7, all different within a row; in each aligned block of 128 rows (0 to 127, 128 to 255, ...) at most 60 rows name the same one
- gate_weights: float32 [1024, 4], P('ep'), may hold values from 0.1 to 1
- shadow_mask: int32 [1024], P('ep'), may hold values 0 or 1
- w_gate: bfloat16 [8, 5120, 1536], P('ep', None, 'tp'), may hold values from -0.078125 to 0.078125
- w_up: bfloat16 [8, 5120, 1536], P('ep', None, 'tp'), may hold values from -0.078125 to 0.078125
- w_down: bfloat16 [8, 1536, 5120], P('ep', 'tp'), may hold values from -0.15625 to 0.15625
- s_gate: bfloat16 [5120, 1536], P('ep', 'tp'), may hold values from -0.078125 to 0.078125
- s_up: bfloat16 [5120, 1536], P('ep', 'tp'), may hold values from -0.078125 to 0.078125
- s_down: bfloat16 [1536, 5120], P('tp', 'ep'), may hold values from -0.15625 to 0.15625
Outputs:
- mixed: bfloat16 [1024, 5120], P('ep', 'tp')
- grad_gate: bfloat16 [8, 5120, 1536], P('ep', None, 'tp')
- grad_up: bfloat16 [8, 5120, 1536], P('ep', None, 'tp')
- grad_down: bfloat16 [8, 1536, 5120], P('ep', 'tp')
- grad_s_gate: bfloat16 [5120, 1536], P('ep', 'tp')
- grad_s_up: bfloat16 [5120, 1536], P('ep', 'tp')
- grad_s_down: bfloat16 [1536, 5120], P('tp', 'ep')
Inputs may be any that keep to these rules, and one draw needn't show every extreme that they name: `expert_ids`: each row names 3 different experts. Among the 128 rows of one device no expert is named more than 60 times, and in every draw some expert is named exactly 60 times by the rows of some device.
All inputs are finite; a program needn't handle non-finite values. No bound on the sum of `shadow_mask` on one device may be relied on, other than what follows from the above.
Results may differ from a plain program's by a relative error of at most 0.028.
Values may be sent and summed in bfloat16 or wider, within the bound.
No kernel may reach another device: no remote copies, remote signals or barrier semaphores. Data moves between devices by JAX's collectives and lax.ppermute only.
A program may use at most 192 MiB of HBM per device.

v0:
```python
import functools

import jax
import jax.numpy as jnp
from jax import lax
from jax.experimental import pallas as pl
from jax.experimental.pallas import tpu as pltpu
from jax.sharding import PartitionSpec as P


def contract_rows(left, right):
    return lax.dot_general(
        left, right, (((0,), (0,)), ((), ())), preferred_element_type=jnp.float32
    )


def split_parts(values):
    upper_part = values.astype(jnp.bfloat16)
    lower_part = (values - upper_part.astype(jnp.float32)).astype(jnp.bfloat16)
    return (upper_part, lower_part)


def weigh_rows(weight_table, rows):
    weight_upper, weight_lower = split_parts(weight_table)
    return jnp.dot(weight_upper, rows, preferred_element_type=jnp.float32) + jnp.dot(
        weight_lower, rows, preferred_element_type=jnp.float32
    )


def expert_pass(rows_x, rows_dout, weight_gate, weight_up, weight_down):
    pre_gate = jnp.dot(rows_x, weight_gate, preferred_element_type=jnp.float32)
    pre_up = jnp.dot(rows_x, weight_up, preferred_element_type=jnp.float32)
    sigmoid_gate = jax.nn.sigmoid(pre_gate)
    activated = pre_gate * sigmoid_gate
    hidden = (activated * pre_up).astype(jnp.bfloat16)
    partial_out = jnp.dot(hidden, weight_down, preferred_element_type=jnp.float32).astype(
        jnp.bfloat16
    )
    hidden_grad = lax.dot_general(
        rows_dout, weight_down, (((1,), (1,)), ((), ())), preferred_element_type=jnp.float32
    )
    grad_pre_gate = (
        hidden_grad * pre_up * sigmoid_gate * (1.0 + pre_gate * (1.0 - sigmoid_gate))
    ).astype(jnp.bfloat16)
    grad_pre_up = (hidden_grad * activated).astype(jnp.bfloat16)
    return (partial_out, hidden, grad_pre_gate, grad_pre_up)


def routed_shards(
    tokens,
    cotangent,
    expert_ids,
    gate_weights,
    shadow_mask,
    w_gate,
    w_up,
    w_down,
    s_gate,
    s_up,
    s_down,
):
    ep_count = lax.axis_size("ep")
    tok_count, top_count = expert_ids.shape
    quarter_width = tokens.shape[1]
    width = quarter_width * lax.axis_size("tp")
    expert_count = w_gate.shape[0] * ep_count
    capacity = (5 * tok_count * top_count + 4 * expert_count - 1) // (4 * expert_count)
    slot_count = expert_count * capacity
    picks_flat = expert_ids.reshape(-1)
    onehot = (picks_flat[:, None] == jnp.arange(expert_count, dtype=jnp.int32)[None, :]).astype(
        jnp.int32
    )
    slot_rank = jnp.sum((jnp.cumsum(onehot, axis=0) - onehot) * onehot, axis=1)
    slot_index = (picks_flat * capacity + slot_rank).reshape(tok_count, top_count)
    matches = jnp.arange(slot_count, dtype=jnp.int32)[:, None, None] == slot_index[None, :, :]
    dispatch = jnp.any(matches, axis=2).astype(jnp.bfloat16)
    weighting = jnp.sum(jnp.where(matches, gate_weights[None, :, :top_count], 0.0), axis=2)
    slot_gate = jnp.sum(weighting, axis=1)
    shadow_weight = gate_weights[:, top_count] * shadow_mask.astype(jnp.float32)
    x_full, dy_full = (
        lax.all_gather(tokens, "tp", axis=1, tiled=True),
        lax.all_gather(cotangent, "tp", axis=1, tiled=True),
    )
    rows_x = jnp.dot(dispatch, tokens, preferred_element_type=jnp.float32).astype(jnp.bfloat16)
    rows_dy = jnp.dot(dispatch, cotangent, preferred_element_type=jnp.float32)
    rows_dout = (slot_gate[:, None] * rows_dy).astype(jnp.bfloat16)
    recv_x, recv_dout = (
        lax.all_to_all(
            rows_x.reshape(ep_count, -1, quarter_width),
            "ep",
            split_axis=0,
            concat_axis=0,
            tiled=True,
        ),
        lax.all_to_all(
            rows_dout.reshape(ep_count, -1, quarter_width),
            "ep",
            split_axis=0,
            concat_axis=0,
            tiled=True,
        ),
    )
    expert_x, expert_dout = (
        lax.all_gather(recv_x.reshape(-1, quarter_width), "tp", axis=1, tiled=True),
        lax.all_gather(recv_dout.reshape(-1, quarter_width), "tp", axis=1, tiled=True),
    )
    partial_out, hidden, grad_pre_gate, grad_pre_up = expert_pass(
        expert_x, expert_dout, w_gate[0], w_up[0], w_down[0]
    )
    grad_gate = contract_rows(expert_x, grad_pre_gate).astype(jnp.bfloat16)[None]
    grad_up = contract_rows(expert_x, grad_pre_up).astype(jnp.bfloat16)[None]
    grad_down = contract_rows(hidden, expert_dout).astype(jnp.bfloat16)[None]
    full_gate, full_up, full_down = (
        lax.all_gather(s_gate, "ep", axis=0, tiled=True),
        lax.all_gather(s_up, "ep", axis=0, tiled=True),
        lax.all_gather(s_down, "ep", axis=1, tiled=True),
    )
    shadow_dout = (shadow_weight[:, None] * dy_full.astype(jnp.float32)).astype(jnp.bfloat16)
    shadow_out, shadow_hidden, shadow_gate_pre, shadow_up_pre = expert_pass(
        x_full, shadow_dout, full_gate, full_up, full_down
    )
    shadow_sums = lax.psum_scatter(
        jnp.concatenate(
            [
                contract_rows(x_full, shadow_gate_pre),
                contract_rows(x_full, shadow_up_pre),
                contract_rows(shadow_dout, shadow_hidden),
            ],
            axis=1,
        ).astype(jnp.bfloat16),
        "ep",
        scatter_dimension=0,
        tiled=True,
    ).astype(jnp.float32)
    hidden_part = s_gate.shape[1]
    grad_s_gate = shadow_sums[:, :hidden_part].astype(jnp.bfloat16)
    grad_s_up = shadow_sums[:, hidden_part : 2 * hidden_part].astype(jnp.bfloat16)
    grad_s_down = shadow_sums[:, 2 * hidden_part :].T.astype(jnp.bfloat16)
    back_rows = lax.all_to_all(
        partial_out.reshape(ep_count, -1, width), "ep", split_axis=0, concat_axis=0, tiled=True
    ).reshape(-1, width)
    term = weigh_rows(weighting.T, back_rows)
    term = term + shadow_weight[:, None] * shadow_out.astype(jnp.float32)
    mixed = lax.psum_scatter(term.astype(jnp.bfloat16), "tp", scatter_dimension=1, tiled=True)
    return (mixed, grad_gate, grad_up, grad_down, grad_s_gate, grad_s_up, grad_s_down)


ANY = pl.BlockSpec(memory_space=pl.ANY)
VMEM_LIMIT = 60 * 1024 * 1024
SHORT = pl.CostEstimate(flops=1, bytes_accessed=1, transcendentals=0)


def swap_pairs(count, bit):
    return [(i, i ^ bit) for i in range(count)]


def dot32(left, right):
    return jnp.dot(left, right, preferred_element_type=jnp.float32)


def contract_last(left, right):
    return lax.dot_general(
        left, right, (((1,), (1,)), ((), ())), preferred_element_type=jnp.float32
    )


def shape_of(*dims, dtype=jnp.bfloat16):
    return jax.ShapeDtypeStruct(dims, dtype)


def after(arrays, *earlier):
    def nothing(*refs):
        del refs

    count = len(arrays)
    return pl.pallas_call(
        nothing,
        out_shape=[jax.ShapeDtypeStruct(a.shape, a.dtype) for a in arrays],
        in_specs=[ANY] * (count + len(earlier)),
        out_specs=[ANY] * count,
        input_output_aliases={i: i for i in range(count)},
        compiler_params=pltpu.CompilerParams(vmem_limit_bytes=VMEM_LIMIT),
        cost_estimate=SHORT,
        name="after",
    )(*arrays, *earlier)


def kernel_call(body, grid, in_specs, out_specs, out_shape, operands, scratch, name, column=None, earlier=()):
    count = len(operands)

    def run(column_ref, *refs):
        del column_ref
        body(*refs[:count], *refs[count + len(earlier) :])

    column = jnp.zeros((1,), jnp.int32) if column is None else column.reshape(1).astype(jnp.int32)
    return pl.pallas_call(
        run,
        out_shape=out_shape,
        grid_spec=pltpu.PrefetchScalarGridSpec(
            num_scalar_prefetch=1,
            grid=grid,
            in_specs=list(in_specs) + [ANY] * len(earlier),
            out_specs=out_specs,
            scratch_shapes=scratch,
        ),
        compiler_params=pltpu.CompilerParams(vmem_limit_bytes=VMEM_LIMIT),
        cost_estimate=SHORT,
        name=name,
    )(column, *operands, *earlier)


def whole(array):
    return pl.BlockSpec(array.shape, lambda *_: (0,) * len(array.shape))


def join_plane(column, *pieces, earlier=()):
    rows, quarter = pieces[0].shape
    count = len(pieces)
    chunk = rows // 4

    def body(*refs):
        column_ref, sources, out = refs[0], refs[1 : 1 + count], refs[-1]
        for own_column in range(count):

            @pl.when(column_ref[0] == own_column)
            def _():
                for bit, source in enumerate(sources):
                    place = own_column ^ bit
                    out[:, place * quarter : (place + 1) * quarter] = source[...]

    return pl.pallas_call(
        body,
        out_shape=shape_of(rows, count * quarter),
        grid_spec=pltpu.PrefetchScalarGridSpec(
            num_scalar_prefetch=1,
            grid=(4,),
            in_specs=[pl.BlockSpec((chunk, quarter), lambda i, *_: (i, 0))] * count + [ANY] * len(earlier),
            out_specs=pl.BlockSpec((chunk, count * quarter), lambda i, *_: (i, 0)),
        ),
        compiler_params=pltpu.CompilerParams(vmem_limit_bytes=VMEM_LIMIT),
        cost_estimate=SHORT,
        name="join_plane",
    )(column.reshape(1).astype(jnp.int32), *pieces, *earlier)


def stack_pieces(pieces, earlier=()):
    rows, columns = pieces[0].shape
    count = len(pieces)

    def body(*refs):
        for i, ref in enumerate(refs[:count]):

            @pl.when(pl.program_id(0) == i)
            def _():
                refs[-1][...] = ref[...]

    return pl.pallas_call(
        body,
        out_shape=shape_of(count * rows, columns),
        grid=(count,),
        in_specs=[pl.BlockSpec((rows, columns), lambda i: (0, 0))] * count + [ANY] * len(earlier),
        out_specs=pl.BlockSpec((rows, columns), lambda i: (i, 0)),
        compiler_params=pltpu.CompilerParams(vmem_limit_bytes=VMEM_LIMIT),
        cost_estimate=SHORT,
        name="stack_pieces",
    )(*pieces, *earlier)


def on_piece(chip_ref, refs, use):
    step = pl.program_id(0)
    shift = chip_ref[0] ^ (step // 2)
    for i, ref in enumerate(refs):
        for core in range(2):

            @pl.when((shift == i) & (lax.rem(step, 2) == core))
            def _(ref=ref, core=core):
                use(ref.at[0, core])


def lay_out_shadow(pieces, down, units, chip, earlier=()):
    count = len(pieces)
    ep_count = 2 * count
    block_width = pieces[0].shape[3]
    apart = units + -units % 128
    all_units, width = down.shape

    def body(chip_ref, *refs):
        shadow_ref, out = refs[-2:]

        def use(ref):
            shadow_ref[...] = jnp.zeros_like(shadow_ref)
            shadow_ref[:units, :] = ref[:units, :]
            shadow_ref[apart : apart + units, :] = ref[units : 2 * units, :]
            out[units:, :] = jnp.zeros((apart - units, block_width), jnp.bfloat16)
            out[:units, :] = ref[2 * units : 3 * units, :]

        on_piece(chip_ref, refs[:count], use)

    return pl.pallas_call(
        body,
        out_shape=[shape_of(2 * apart, width), shape_of(all_units, width)],
        grid_spec=pltpu.PrefetchScalarGridSpec(
            num_scalar_prefetch=1,
            grid=(ep_count,),
            in_specs=[whole(p) for p in pieces] + [ANY] * (1 + len(earlier)),
            out_specs=[
                pl.BlockSpec((2 * apart, block_width), lambda e, *_: (0, e)),
                pl.BlockSpec((apart, block_width), lambda e, *_: (all_units // apart - 1, e)),
            ],
        ),
        input_output_aliases={1 + count: 1},
        compiler_params=pltpu.CompilerParams(vmem_limit_bytes=VMEM_LIMIT),
        cost_estimate=SHORT,
        name="lay_out_shadow",
    )(chip.reshape(1).astype(jnp.int32), *pieces, down, *earlier)


def lay_out_grads(pieces, units, chip, earlier=()):
    count = len(pieces)
    ep_count = 2 * count
    block_width = pieces[0].shape[3]
    hidden = ep_count * units

    def body(chip_ref, *refs):
        gate_ref, up_ref, down_ref, gate_t, up_t = refs[-5:]
        place = pl.ds(pl.multiple_of(pl.program_id(0) * units, 16), units)

        def use(ref):
            gate_t[place, :] = ref[:units, :]
            up_t[place, :] = ref[units : 2 * units, :]
            down_ref[place, :] = ref[2 * units :, :]

        on_piece(chip_ref, refs[:count], use)

        @pl.when(pl.program_id(0) == ep_count - 1)
        def _():
            gate_ref[...] = gate_t[...].T
            up_ref[...] = up_t[...].T

    return pl.pallas_call(
        body,
        out_shape=[shape_of(block_width, hidden), shape_of(block_width, hidden), shape_of(hidden, block_width)],
        grid_spec=pltpu.PrefetchScalarGridSpec(
            num_scalar_prefetch=1,
            grid=(ep_count,),
            in_specs=[whole(p) for p in pieces] + [ANY] * len(earlier),
            out_specs=[pl.BlockSpec((block_width, hidden), lambda *_: (0, 0))] * 2
            + [pl.BlockSpec((hidden, block_width), lambda *_: (0, 0))],
            scratch_shapes=[pltpu.VMEM((hidden, block_width), jnp.bfloat16)] * 2,
        ),
        compiler_params=pltpu.CompilerParams(vmem_limit_bytes=VMEM_LIMIT),
        cost_estimate=SHORT,
        name="lay_out_grads",
    )(chip.reshape(1).astype(jnp.int32), *pieces, *earlier)


def row_specs(groups, tile):
    def spec(index, rows):
        return pl.BlockSpec((rows, tile), lambda k, *_: (index, k))

    return [spec(index, rows) for _, index, rows in groups]


def apply_gate(pre_gate, pre_up):
    sigmoid_gate = jax.nn.sigmoid(pre_gate)
    activated = pre_gate * sigmoid_gate
    hidden = (activated * pre_up).astype(jnp.bfloat16)
    return hidden, pre_up * sigmoid_gate * (1.0 + pre_gate * (1.0 - sigmoid_gate)), activated


def clear_first(acc):
    @pl.when(pl.program_id(0) == 0)
    def _():
        acc[...] = jnp.zeros_like(acc)


def rows_operand(refs, groups, held):
    if len(groups) == 1:
        return refs[0][...]
    return stage_rows(refs, groups, held)


def forward_rows(groups, w_both, tile, transposed=False, earlier=()):
    rows = sum(g[2] for g in groups)
    if transposed:
        units, width = w_both.shape[0] // 2, w_both.shape[1]
        tile_spec = pl.BlockSpec((2 * units, tile), lambda k, *_: (0, k))
    else:
        width, units = w_both.shape[0], w_both.shape[1] // 2
        tile_spec = pl.BlockSpec((tile, 2 * units), lambda k, *_: (k, 0))
    steps = width // tile

    def body(*refs):
        n = len(groups)
        both_ref, hidden_ref, slope_ref, act_ref, acc, held = refs[n:]
        clear_first(acc)
        operand = rows_operand(refs[:n], groups, held)
        acc[...] += contract_last(operand, both_ref[...]) if transposed else dot32(operand, both_ref[...])

        @pl.when(pl.program_id(0) == steps - 1)
        def _():
            chunk = 128

            @pl.loop(0, rows // chunk)
            def _(i):
                part = pl.ds(pl.multiple_of(i * chunk, chunk), chunk)
                hidden, slope, act = apply_gate(acc[part, :units], acc[part, units:])
                hidden_ref[part, :] = hidden
                slope_ref[part, :] = slope.astype(jnp.bfloat16)
                act_ref[part, :] = act.astype(jnp.bfloat16)

    out_spec = pl.BlockSpec((rows, units), lambda *_: (0, 0))
    return kernel_call(
        body,
        (steps,),
        row_specs(groups, tile) + [tile_spec],
        [out_spec] * 3,
        [shape_of(rows, units)] * 3,
        [g[0] for g in groups] + [w_both],
        [pltpu.VMEM((rows, 2 * units), jnp.float32), pltpu.VMEM((rows, tile), jnp.bfloat16)],
        "forward_rows",
        earlier=earlier,
    )


def weigh_hidden(hidden_near, hidden_far, hidden_s, pieces, first_row, slot_rows, core, earlier=()):
    count = len(pieces)
    rows, units_s = hidden_s.shape
    units = hidden_near.shape[1]
    slots = [(s, 0) for s in list(range(1, count)) + [0]] + [(s, 1) for s in range(count)]

    def body(core_ref, *refs):
        near_ref, far_ref, s_ref, *piece_refs = refs[: 3 + count]
        out, w_ref, w_s_ref = refs[-3:]
        near, far = 0, 0
        for i, (slot, other) in enumerate(slots):
            part = pl.ds(i * slot_rows, slot_rows)
            table = piece_refs[slot][0, core_ref[0] ^ other, first_row : first_row + 16, :][:1].astype(jnp.float32)

            def column(j):
                both = table[:, j * slot_rows : (j + 1) * slot_rows]
                both = both + table[:, (j + 2) * slot_rows : (j + 3) * slot_rows]
                return jnp.broadcast_to(both, (slot_rows, slot_rows)).T[:, :1]

            weight, weight_s = column(0), column(1)
            w_ref[part, :] = weight
            w_s_ref[part, :] = weight_s
            if slot == 0:
                hidden = near_ref[near : near + slot_rows, :]
                near += slot_rows
            else:
                hidden = far_ref[far : far + slot_rows, :]
                far += slot_rows
            out[part, :units] = (hidden.astype(jnp.float32) * weight).astype(jnp.bfloat16)
            out[part, units:] = (s_ref[part, :].astype(jnp.float32) * weight_s).astype(jnp.bfloat16)

    return pl.pallas_call(
        body,
        out_shape=[
            shape_of(rows, units + units_s),
            shape_of(rows, 1, dtype=jnp.float32),
            shape_of(rows, 1, dtype=jnp.float32),
        ],
        grid_spec=pltpu.PrefetchScalarGridSpec(
            num_scalar_prefetch=1,
            grid=(1,),
            in_specs=[whole(a) for a in (hidden_near, hidden_far, hidden_s, *pieces)] + [ANY] * len(earlier),
            out_specs=[
                pl.BlockSpec((rows, units + units_s), lambda *_: (0, 0)),
                pl.BlockSpec((rows, 1), lambda *_: (0, 0)),
                pl.BlockSpec((rows, 1), lambda *_: (0, 0)),
            ],
        ),
        compiler_params=pltpu.CompilerParams(vmem_limit_bytes=VMEM_LIMIT),
        cost_estimate=SHORT,
        name="weigh_hidden",
    )(core.reshape(1).astype(jnp.int32), hidden_near, hidden_far, hidden_s, *pieces, *earlier)


def output_other(weighted, down, column, parts, slot_rows, quarter, earlier=()):
    rows, units = weighted.shape
    count = rows // 2 // parts

    def body(weighted_ref, down_ref, *outs):
        for i, out in enumerate(outs):
            first, last = slot_rows + i * count, slot_rows + (i + 1) * count
            kept = min(last, rows // 2) - first
            value = dot32(weighted_ref[first : first + kept, :], down_ref[...])
            out[:kept, :] = value.astype(jnp.bfloat16)
            if kept < count:
                value = dot32(weighted_ref[: count - kept, :], down_ref[...])
                out[kept:, :] = value.astype(jnp.bfloat16)

    return kernel_call(
        body,
        (4,),
        [
            pl.BlockSpec((rows // 2, units), lambda *_: (1, 0)),
            pl.BlockSpec((units, quarter), lambda q, column_ref: (0, column_ref[0] ^ q)),
        ],
        [pl.BlockSpec((count, quarter), lambda q, *_: (0, q))] * parts,
        [shape_of(count, 4 * quarter)] * parts,
        [weighted, down],
        [],
        "output_other",
        column=column,
        earlier=earlier,
    )


def output_own(weighted, got, down, column, quarter, earlier=()):
    count, units = got[0].shape[0], weighted.shape[1]
    parts = len(got)

    def body(weighted_ref, down_ref, *refs):
        for i in range(parts):
            value = dot32(weighted_ref[i * count : (i + 1) * count, :], down_ref[...])
            value = value + refs[i][...].astype(jnp.float32)
            for j, out in enumerate(refs[parts + 4 * i : parts + 4 * i + 4]):

                @pl.when(pl.program_id(0) == 3 - j)
                def _(out=out, value=value):
                    out[...] = value.astype(out.dtype)

    full = pl.BlockSpec((count, quarter), lambda *_: (0, 0))
    out = kernel_call(
        body,
        (4,),
        [
            pl.BlockSpec((parts * count, units), lambda *_: (0, 0)),
            pl.BlockSpec((units, quarter), lambda q, column_ref: (0, column_ref[0] ^ 3 ^ q)),
        ]
        + [pl.BlockSpec((count, quarter), lambda q, *_: (0, 3 - q))] * parts,
        [full] * (4 * parts),
        ([shape_of(count, quarter, dtype=jnp.float32)] + [shape_of(count, quarter)] * 3) * parts,
        [weighted, down] + list(got),
        [],
        "output_own",
        column=column,
        earlier=earlier,
    )
    return [out[4 * i : 4 * i + 4] for i in range(parts)]


def backward_rows(groups, down, parts, per_row, first_row, tile, earlier=()):
    slope_s, act_s, w_rows, w_shadow = per_row
    rows = sum(g[2] for g in groups)
    units_all, width = down.shape
    units_s = slope_s.shape[1]
    units = units_all - units_s
    steps = width // tile
    arrays = list({id(a): a for part in parts for a in part[:2]}.values())
    places = [[next(i for i, a in enumerate(arrays) if a is b) for b in part[:2]] for part in parts]

    def body(*refs):
        n, m = len(groups), len(arrays)
        down_ref = refs[n]
        array_refs = refs[n + 1 : n + 1 + m]
        slope_s_ref, act_s_ref, w_ref, w_s_ref, pre_ref, pre_s_ref, acc, held = refs[n + 1 + m :]
        clear_first(acc)
        acc[...] += contract_last(rows_operand(refs[:n], groups, held), down_ref[...])

        @pl.when(pl.program_id(0) == steps - 1)
        def _():
            chunk = 128
            start = 0
            for (_, _, count), (_, _, first), (slope_at, act_at) in zip(groups, parts, places):

                @pl.loop(0, count // chunk)
                def _(i, start=start, first=first, slope_ref=array_refs[slope_at], act_ref=array_refs[act_at]):
                    source = pl.ds(pl.multiple_of(first + i * chunk, chunk), chunk)
                    part = pl.ds(pl.multiple_of(start + i * chunk, chunk), chunk)
                    whole_part = pl.ds(pl.multiple_of(first_row + start + i * chunk, chunk), chunk)
                    grad = acc[part, :units] * w_ref[whole_part, :]
                    pre_ref[part, :units] = (grad * slope_ref[source, :]).astype(jnp.bfloat16)
                    pre_ref[part, units:] = (grad * act_ref[source, :]).astype(jnp.bfloat16)
                    grad = acc[part, units:] * w_s_ref[whole_part, :]
                    pre_s_ref[part, :units_s] = (grad * slope_s_ref[whole_part, :]).astype(jnp.bfloat16)
                    pre_s_ref[part, units_s:] = (grad * act_s_ref[whole_part, :]).astype(jnp.bfloat16)

                start += count

    extra = arrays + [slope_s, act_s, w_rows, w_shadow]
    return kernel_call(
        body,
        (steps,),
        row_specs(groups, tile) + [pl.BlockSpec((units_all, tile), lambda k, *_: (0, k))] + [whole(a) for a in extra],
        [pl.BlockSpec((rows, 2 * units), lambda *_: (0, 0)), pl.BlockSpec((rows, 2 * units_s), lambda *_: (0, 0))],
        [shape_of(rows, 2 * units), shape_of(rows, 2 * units_s)],
        [g[0] for g in groups] + [down] + extra,
        [pltpu.VMEM((rows, units_all), jnp.float32), pltpu.VMEM((rows, tile), jnp.bfloat16)],
        "backward_rows",
        earlier=earlier,
    )


def stage_rows(refs, groups, held):
    start = 0
    for ref, (_, _, count) in zip(refs, groups):
        held[pl.ds(start, count), :] = ref[...]
        start += count
    return held[...]


def shadow_grads(x_groups, dy_groups, pre_s, weighted, units, tile, earlier=()):
    rows, wide = weighted.shape[0], pre_s[0].shape[1]
    apart = wide // 2
    width = x_groups[0][0].shape[1]
    m = len(pre_s)

    def body(*refs):
        n = len(x_groups)
        pre_refs = refs[2 * n : 2 * n + m]
        hidden_ref, out, held, pre_t, hidden_t = refs[2 * n + m :]

        @pl.when(pl.program_id(0) == 0)
        def _():
            start = 0
            for ref in pre_refs:
                pre_t[:, start : start + ref.shape[0]] = ref[...].T
                start += ref.shape[0]
            hidden_t[...] = hidden_ref[...].T

        value = dot32(pre_t[...], stage_rows(refs[:n], x_groups, held))
        out[:units, :] = value[:units].astype(jnp.bfloat16)
        out[units : 2 * units, :] = value[apart : apart + units].astype(jnp.bfloat16)
        value = dot32(hidden_t[...], stage_rows(refs[n : 2 * n], dy_groups, held))
        out[2 * units :, :] = value[:units].astype(jnp.bfloat16)

    (out,) = kernel_call(
        body,
        (width // tile,),
        row_specs(x_groups, tile)
        + row_specs(dy_groups, tile)
        + [whole(p) for p in pre_s]
        + [pl.BlockSpec((rows, apart), lambda *_: (0, weighted.shape[1] // apart - 1))],
        [pl.BlockSpec((3 * units, tile), lambda k, *_: (0, k))],
        [shape_of(3 * units, width)],
        [g[0] for g in x_groups + dy_groups] + list(pre_s) + [weighted],
        [
            pltpu.VMEM((rows, tile), jnp.bfloat16),
            pltpu.VMEM((wide, rows), jnp.bfloat16),
            pltpu.VMEM((apart, rows), jnp.bfloat16),
        ],
        "shadow_grads",
        earlier=earlier,
    )
    return out


def input_grads(groups, pre, tile, earlier=()):
    both = pre[0].shape[1]
    rows = sum(p.shape[0] for p in pre)
    units = both // 2
    width = groups[0][0].shape[1]
    m = len(pre)

    def body(*refs):
        n = len(groups)
        gate_ref, up_ref, held, pre_held = refs[n + m :]

        @pl.when(pl.program_id(0) == 0)
        def _():
            start = 0
            for ref in refs[n : n + m]:
                pre_held[start : start + ref.shape[0], :] = ref[...]
                start += ref.shape[0]

        value = contract_rows(stage_rows(refs[:n], groups, held), pre_held[...])
        gate_ref[...] = value[:, :units].astype(jnp.bfloat16)
        up_ref[...] = value[:, units:].astype(jnp.bfloat16)

    return kernel_call(
        body,
        (width // tile,),
        row_specs(groups, tile) + [whole(p) for p in pre],
        [pl.BlockSpec((tile, units), lambda k, *_: (k, 0))] * 2,
        [shape_of(width, units)] * 2,
        [g[0] for g in groups] + list(pre),
        [pltpu.VMEM((rows, tile), jnp.bfloat16), pltpu.VMEM((rows, both), jnp.bfloat16)],
        "input_grads",
        earlier=earlier,
    )


def down_grad(groups, weighted, units, tile, earlier=()):
    rows = weighted.shape[0]
    width = groups[0][0].shape[1]

    def body(*refs):
        n = len(groups)
        hidden_ref, out, held, hidden_t = refs[n:]

        @pl.when(pl.program_id(0) == 0)
        def _():
            hidden_t[...] = hidden_ref[...].T

        out[...] = dot32(hidden_t[...], stage_rows(refs[:n], groups, held)).astype(jnp.bfloat16)

    (out,) = kernel_call(
        body,
        (width // tile,),
        row_specs(groups, tile) + [pl.BlockSpec((rows, units), lambda *_: (0, 0))],
        [pl.BlockSpec((units, tile), lambda k, *_: (0, k))],
        [shape_of(units, width)],
        [g[0] for g in groups] + [weighted],
        [pltpu.VMEM((rows, tile), jnp.bfloat16), pltpu.VMEM((units, rows), jnp.bfloat16)],
        "down_grad",
        earlier=earlier,
    )
    return out


def send_along_z(own):
    ep_count = lax.axis_size("ep")
    return [lax.ppermute(own, "ep", swap_pairs(ep_count, 2 * s)) for s in range(1, ep_count // 2)]


def swap_cores(block):
    return lax.ppermute(block, "ep", swap_pairs(lax.axis_size("ep"), 1))


def send_plane(*pieces):
    pieces = pieces * 3 if len(pieces) == 1 else pieces
    return [lax.ppermute(p, "tp", swap_pairs(lax.axis_size("tp"), bit)) for p, bit in zip(pieces, (1, 2, 3))]


def exchange_cores(blocks, cuts=1):
    ep_count, core = lax.axis_size("ep"), lax.axis_index("ep") % 2
    pairs = blocks.reshape(ep_count // 2, 2, *blocks.shape[1:])
    kept = jnp.where(core == 0, pairs[:, 0], pairs[:, 1])
    given = jnp.where(core == 0, pairs[:, 1], pairs[:, 0])
    return kept, [swap_cores(part) for part in jnp.split(given, cuts)]


def chip_pieces(kept, taken):
    ep_count, me = lax.axis_size("ep"), lax.axis_index("ep")
    chips, chip, core = ep_count // 2, me // 2, me % 2
    taken = jnp.concatenate(taken, axis=0)
    both = jnp.stack([jnp.where(core == 0, kept, taken), jnp.where(core == 0, taken, kept)], axis=1)
    return [lax.dynamic_index_in_dim(both, chip ^ shift, 0) for shift in range(chips)]


def send_piece(piece, shift):
    return lax.ppermute(piece, "ep", swap_pairs(lax.axis_size("ep"), 2 * shift))


def dense_shards(
    tokens,
    cotangent,
    expert_ids,
    gate_weights,
    shadow_mask,
    w_gate,
    w_up,
    w_down,
    s_gate,
    s_up,
    s_down,
):
    ep_count, tp_count = lax.axis_size("ep"), lax.axis_size("tp")
    ep_index, tp_index = lax.axis_index("ep"), lax.axis_index("tp")
    tok_count, top_count = expert_ids.shape
    quarter = tokens.shape[1]
    width = quarter * tp_count
    hidden_part = w_gate.shape[2]
    shadow_part = hidden_part // ep_count
    block_width = s_gate.shape[0]
    steps = ep_count // 2
    later = (steps - 1) * tok_count
    tile = width // 8
    along, across = swap_pairs(tp_count, 1), swap_pairs(tp_count, 2)

    picked = expert_ids[None, :, :] == jnp.arange(ep_count, dtype=jnp.int32)[:, None, None]
    table = jnp.sum(jnp.where(picked, gate_weights[None, :, :top_count], 0.0), axis=2)
    shadow_weight = gate_weights[:, top_count] * shadow_mask.astype(jnp.float32)
    table = jnp.concatenate([table, jnp.broadcast_to(shadow_weight[None], table.shape)], axis=1)
    table = jnp.concatenate(split_parts(table), axis=1)
    table = jnp.pad(table[:, None, :], ((0, 0), (0, 15), (0, block_width - table.shape[1])))
    shadow_blocks = jnp.concatenate(
        [
            s_gate.T.reshape(ep_count, shadow_part, block_width),
            s_up.T.reshape(ep_count, shadow_part, block_width),
            s_down.reshape(ep_count, shadow_part, block_width),
            table,
        ],
        axis=1,
    )

    x_z = send_along_z(tokens)
    near = stack_pieces([tokens, cotangent])
    near_x, near_y = send_plane(near, near)
    near_late = stack_pieces([tokens, cotangent], earlier=[x_z[0]])
    near_d = lax.ppermute(near_late, "tp", swap_pairs(tp_count, 3))
    w_both = jnp.concatenate([w_gate[0], w_up[0]], axis=1)
    near_x, near_y, near_d, *x_z = after([near_x, near_y, near_d, *x_z], w_both, shadow_blocks)

    x_piece = stack_pieces(x_z)
    x_plane = send_plane(x_piece)
    dy_z = send_along_z(cotangent)
    near_own = join_plane(tp_index, near, near_x, near_y, near_d)
    near_other = swap_cores(near_own)
    x_near = [(near_own, 0, tok_count), (near_other, 0, tok_count)]
    hidden_near, slope_near, act_near = forward_rows(x_near, w_both, 2 * tile)
    spare_rows = -shadow_part % 128 + shadow_part
    down = jnp.pad(w_down[0], ((0, spare_rows), (0, 0)))
    (shadow_blocks,) = after([shadow_blocks], x_z[0])
    shadow_kept, shadow_taken = exchange_cores(shadow_blocks)
    fenced = after([*x_plane, down, *shadow_taken, *dy_z], hidden_near)
    x_plane, down, shadow_taken, dy_z = fenced[:3], fenced[3], fenced[4:5], fenced[5:]

    dy_piece = stack_pieces(dy_z)
    dy_plane = send_plane(dy_piece)
    shadow_pieces = chip_pieces(shadow_kept, shadow_taken)
    for shift in range(1, steps - 1):
        shadow_pieces[shift] = send_piece(shadow_pieces[shift], shift)
    x_own = join_plane(tp_index, x_piece, *x_plane, earlier=[dy_piece])
    x_other = swap_cores(x_own)
    x_far = [(x_own, 0, later), (x_other, 0, later)]
    x_groups = [x_far[0], x_near[0], x_near[1], x_far[1]]
    hidden_far, slope_far, act_far = forward_rows(x_far, w_both, 2 * tile)
    shadow_pieces[-1:] = after(shadow_pieces[-1:], hidden_far)
    shadow_pieces[-1] = send_piece(shadow_pieces[-1], steps - 1)
    chip = ep_index // 2
    shadow_in, down = lay_out_shadow(shadow_pieces, down, shadow_part, chip, earlier=[hidden_far])
    hidden_s, slope_s, act_s = forward_rows(x_groups, shadow_in, 2 * tile, transposed=True)

    weighted, w_rows, w_shadow = weigh_hidden(
        hidden_near, hidden_far, hidden_s, shadow_pieces, 3 * shadow_part, tok_count, ep_index % 2
    )

    parts = 2 if steps % 2 == 0 else 1
    sent = output_other(weighted, down, tp_index, parts, tok_count, quarter)
    got = [swap_cores(array) for array in sent]
    dy_plane = after(dy_plane, *sent)

    dy_own = join_plane(tp_index, dy_piece, *dy_plane)
    dy_other = swap_cores(dy_own)
    dy_groups = [(dy_own, 0, later), (near_own, 1, tok_count), (near_other, 1, tok_count), (dy_other, 0, later)]
    segments = [
        (slope_far, act_far, 0),
        (slope_near, act_near, 0),
        (slope_near, act_near, tok_count),
        (slope_far, act_far, later),
    ]
    per_row = (slope_s, act_s, w_rows, w_shadow)
    pre_first, pre_s_first = backward_rows(dy_groups[:3], down, segments[:3], per_row, 0, 2 * tile)
    owns = output_own(weighted, got, down, tp_index, quarter, earlier=[pre_first])
    sums = [send_plane(*own[1:]) for own in owns]
    first_rows = sum(g[2] for g in dy_groups[:3])
    pre_last, pre_s_last = backward_rows(
        dy_groups[3:], down, segments[3:], per_row, first_rows, 2 * tile, earlier=[own[1] for own in owns]
    )
    pre, pre_s = [pre_first, pre_last], [pre_s_first, pre_s_last]
    grad_s = shadow_grads(x_groups, dy_groups, pre_s, weighted, shadow_part, tile)
    blocks = grad_s.reshape(3 * shadow_part, ep_count, block_width).transpose(1, 0, 2)
    grad_pieces = chip_pieces(*exchange_cores(blocks))

    def slot_rows(i):
        part = slice(i % (steps // parts) * tok_count, (i % (steps // parts) + 1) * tok_count)
        total = owns[i * parts // steps][0][part]
        for array in sums[i * parts // steps]:
            total = total + array[part].astype(jnp.float32)
        return total

    def send_rows(piece, i):
        return lax.ppermute(piece, "ep", swap_pairs(ep_count, 2 * (i + 1)))

    early = steps // parts if parts > 1 else 0
    sums[0] = after(sums[0], grad_s)
    rows = [slot_rows(i).astype(jnp.bfloat16) for i in range(early)]
    grad_down = down_grad(dy_groups, weighted, hidden_part, tile, earlier=[*rows, grad_pieces[0]])
    rows = [send_rows(piece, i) for i, piece in enumerate(rows)]
    fenced = after([*rows, *grad_pieces[1:]], grad_down)
    rows, grad_pieces[1:] = list(fenced[:early]), fenced[early:]
    grad_gate, grad_up = input_grads(x_groups, pre, tile, earlier=[grad_pieces[1]])
    for shift in range(1, steps - 1):
        grad_pieces[shift] = send_piece(grad_pieces[shift], shift)
    fenced = after([*sums[-1], *grad_pieces[1:]], grad_gate)
    sums[-1], grad_pieces[1:] = fenced[:3], fenced[3:]
    grad_pieces[-1] = send_piece(grad_pieces[-1], steps - 1)
    rows += [send_rows(slot_rows(i).astype(jnp.bfloat16), i) for i in range(early, steps - 1)]
    total = slot_rows(steps - 1)
    for piece in rows:
        total = total + piece.astype(jnp.float32)
    mixed = total.astype(jnp.bfloat16)

    grads_s = lay_out_grads(grad_pieces, shadow_part, chip)
    return (mixed, grad_gate[None], grad_up[None], grad_down[None], *grads_s)


def shards(tokens, cotangent, expert_ids, *others):
    tp_count, ep_count = lax.axis_size("tp"), lax.axis_size("ep")
    tok_count, top_count = expert_ids.shape
    rows = (5 * tok_count * top_count) // 4
    chips = ep_count // 2
    fits = tp_count == 4 and ep_count == 2 * chips and chips & (chips - 1) == 0 and tok_count % 128 == 0
    dense = fits and ep_count * tok_count <= 3 * rows
    return (dense_shards if dense else routed_shards)(tokens, cotangent, expert_ids, *others)


def solution(mesh):
    return jax.shard_map(
        shards,
        mesh=mesh,
        in_specs=(
            P("ep", "tp"),
            P("ep", "tp"),
            P("ep", None),
            P("ep", None),
            P("ep"),
            P("ep", None, "tp"),
            P("ep", None, "tp"),
            P("ep", "tp", None),
            P("ep", "tp"),
            P("ep", "tp"),
            P("tp", "ep"),
        ),
        out_specs=(
            P("ep", "tp"),
            P("ep", None, "tp"),
            P("ep", None, "tp"),
            P("ep", "tp", None),
            P("ep", "tp"),
            P("ep", "tp"),
            P("tp", "ep"),
        ),
        check_vma=False,
    )
```

profile of v0, /device:TPU:16, one launch (start us, length us, event | category | flops | bytes accessed | tf_op | source)
XLA Modules:
  0.0 309.7 jit_solution(8170289804349189839)
XLA Ops:
  9.1 7.1 %pad_maximum_fusion.refs_6_.refs_2_ = bf16[5120,768]{1,0:T(8,128)(2,1)} fusion(bf16[5120,384]{1,0:T(8,128)(2,1)} %bitcast.105, bf16[5120,384]{1,0:T(8,128)(2,1)} %bitcast.106), kind=kLoop, calls=%fused_computation | loop fusion | flops 15728640 | bytes 15728640 | tf_op jit(solution)/shard_map/concatenate | solution.py:795
  30.0 7.1 %collective-permute-done.5.refs_5_ = bf16[128,1280]{1,0:T(8,128)(2,1)} collective-permute-done((bf16[128,1280]{1,0:T(8,128)(2,1)}, bf16[128,1280]{1,0:T(8,128)(2,1)}, u32[]{:S(2)}, u32[]{:S(2)}) %collective-permute-start.5) | collective-permute-done | bytes 327712 | tf_op jit(solution)/shard_map/ppermute | solution.py:716
  39.4 4.1 %join_plane.3.refs_0_.refs_1_.refs_5_ = bf16[256,5120]{1,0:T(8,128)(2,1)} custom-call(s32[1]{0:T(128)} %bitcast.refs_0_.column_ref, bf16[256,1280]{1,0:T(8,128)(2,1)} %stack_pieces.4.refs_1_, bf16[256,1280]{1,0:T(8,128)(2,1)} %get-tuple-element.71.refs_2_, bf16[256,1280]{1,0:T(8,128)(2,1)} %get-tuple-element.72.refs_3_, ...), custom_call_target="tpu_custom_call" | custom-call | flops 1 | bytes 1 | tf_op jit(solution)/shard_map/join_plane/pallas_call | solution.py:231
  49.7 8.6 %collective-permute-done.11.refs_5_ = bf16[128,1280]{1,0:T(8,128)(2,1)S(1)} collective-permute-done((bf16[128,1280]{1,0:T(8,128)(2,1)S(1)}, bf16[128,1280]{1,0:T(8,128)(2,1)S(1)}, u32[]{:S(2)}, u32[]{:S(2)}) %collective-permute-start.11) | collective-permute-done | bytes 327712 | tf_op jit(solution)/shard_map/ppermute | solution.py:716
  63.1 5.1 %pad.9.refs_3_ = bf16[512,5120]{1,0:T(8,128)(2,1)} pad(bf16[384,5120]{1,0:T(8,128)(2,1)} %bitcast.103, bf16[]{:T(256)} %constant.71.clone.1), padding=0_128x0_0 | pad | bytes 9175042 | tf_op jit(solution)/shard_map/jit(_pad)/pad | solution.py:806
  68.2 6.9 %forward_rows.3 = (bf16[256,384]{1,0:T(8,128)(2,1)}, bf16[256,384]{1,0:T(8,128)(2,1)}, bf16[256,384]{1,0:T(8,128)(2,1)}) custom-call(s32[1]{0:T(128)} %constant.69.clone.1.column_ref, bf16[256,5120]{1,0:T(8,128)(2,1)} %join_plane.3.refs_0_.refs_1_.refs_5_, bf16[256,5120]{1,0:T(8,128)(2,1)} %copy-done, bf16[5120,768]{1,0:T(8,128)(2,1)} %pad_maximum_fusion.refs_6_.refs_2_), custom_call_target="tpu_custom_call" | custom-call | flops 1 | bytes 1 | tf_op jit(solution)/shard_map/forward_rows/pallas_call | solution.py:196
  78.7 15.5 %collective-permute-done.8.refs_1_ = bf16[384,1280]{1,0:T(8,128)(2,1)} collective-permute-done((bf16[384,1280]{1,0:T(8,128)(2,1)}, bf16[384,1280]{1,0:T(8,128)(2,1)}, u32[]{:S(2)}, u32[]{:S(2)}) %collective-permute-start.8) | collective-permute-done | bytes 983072 | tf_op jit(solution)/shard_map/ppermute | solution.py:725
  96.9 5.0 %join_plane.4.refs_0_ = bf16[384,5120]{1,0:T(8,128)(2,1)} custom-call(s32[1]{0:T(128)} %bitcast.refs_0_.column_ref, bf16[384,1280]{1,0:T(8,128)(2,1)} %stack_pieces.6.refs_1_, bf16[384,1280]{1,0:T(8,128)(2,1)} %get-tuple-element.78.refs_2_, bf16[384,1280]{1,0:T(8,128)(2,1)} %get-tuple-element.79.refs_3_, bf16[384,1280]{1,0:T(8,128)(2,1)} %get-tuple-element.80.refs_4_, ...), custom_call_target="tpu_custom_call" | custom-call | flops 1 | bytes 1 | tf_op jit(solution)/shard_map/join_plane/pallas_call | solution.py:231
  111.7 11.5 %forward_rows.4 = (bf16[768,384]{1,0:T(8,128)(2,1)}, bf16[768,384]{1,0:T(8,128)(2,1)}, bf16[768,384]{1,0:T(8,128)(2,1)}) custom-call(s32[1]{0:T(128)} %constant.69.clone.1.column_ref, bf16[384,5120]{1,0:T(8,128)(2,1)} %join_plane.4.refs_0_, bf16[384,5120]{1,0:T(8,128)(2,1)} %collective-permute-done.14.refs_1_.refs_3_, ...), custom_call_target="tpu_custom_call" | custom-call | flops 1 | bytes 1 | tf_op jit(solution)/shard_map/forward_rows/pallas_call | solution.py:196
  123.3 15.8 %collective-permute-done.16.refs_2_.refs_5_ = bf16[1,2,160,640]{3,2,1,0:T(8,128)(2,1)S(1)} collective-permute-done((bf16[1,2,160,640]{3,2,1,0:T(8,128)(2,1)S(1)}, bf16[1,2,160,640]{3,2,1,0:T(8,128)(2,1)S(1)}, u32[]{:S(2)}, u32[]{:S(2)}) %collective-permute-start.16) | collective-permute-done | bytes 409632 | tf_op jit(solution)/shard_map/ppermute | solution.py:745
  139.1 8.1 %collective-permute-done.17.refs_3_.refs_6_ = bf16[1,2,160,640]{3,2,1,0:T(8,128)(2,1)S(1)} collective-permute-done((bf16[1,2,160,640]{3,2,1,0:T(8,128)(2,1)}, bf16[1,2,160,640]{3,2,1,0:T(8,128)(2,1)S(1)}, u32[]{:S(2)}, u32[]{:S(2)}) %collective-permute-start.17) | collective-permute-done | bytes 409632 | tf_op jit(solution)/shard_map/ppermute | solution.py:745
  147.9 4.9 %lay_out_shadow.1 = (bf16[256,5120]{1,0:T(8,128)(2,1)}, bf16[512,5120]{1,0:T(8,128)(2,1)}) custom-call(s32[1]{0:T(128)} %bitcast.14.chip_ref, bf16[1,2,160,640]{3,2,1,0:T(8,128)(2,1)} %get-tuple-element.142.refs_0_.refs_3_, bf16[1,2,160,640]{3,2,1,0:T(8,128)(2,1)} %copy-done.13, ...), custom_call_target="tpu_custom_call", output_to_operand_aliasing={{1}: (5, {})} | custom-call | flops 1 | bytes 1 | tf_op jit(solution)/shard_map/lay_out_shadow/pallas_call | solution.py:299
  152.9 8.0 %forward_rows.5 = (bf16[1024,128]{1,0:T(8,128)(2,1)}, bf16[1024,128]{1,0:T(8,128)(2,1)}, bf16[1024,128]{1,0:T(8,128)(2,1)}) custom-call(s32[1]{0:T(128)} %constant.69.clone.1.column_ref, bf16[384,5120]{1,0:T(8,128)(2,1)} %join_plane.4.refs_0_, bf16[256,5120]{1,0:T(8,128)(2,1)} %join_plane.3.refs_0_.refs_1_.refs_5_, bf16[256,5120]{1,0:T(8,128)(2,1)} %copy-done, ...), custom_call_target="tpu_custom_call" | custom-call | flops 1 | bytes 1 | tf_op jit(solution)/shard_map/forward_rows/pallas_call | solution.py:196
  164.2 6.5 %output_other.1 = (bf16[256,5120]{1,0:T(8,128)(2,1)}, bf16[256,5120]{1,0:T(8,128)(2,1)}) custom-call(s32[1]{0:T(128)} %bitcast.refs_0_.column_ref, bf16[1024,512]{1,0:T(8,128)(2,1)} %get-tuple-element.89.refs_0_.refs_10_.refs_4_, bf16[512,5120]{1,0:T(8,128)(2,1)} %get-tuple-element.90.refs_1_.refs_3_), custom_call_target="tpu_custom_call" | custom-call | flops 1 | bytes 1 | tf_op jit(solution)/shard_map/output_other/pallas_call | solution.py:196
  170.8 4.7 %join_plane.5.refs_0_.refs_4_ = bf16[384,5120]{1,0:T(8,128)(2,1)} custom-call(s32[1]{0:T(128)} %bitcast.refs_0_.column_ref, bf16[384,1280]{1,0:T(8,128)(2,1)} %stack_pieces.7.refs_5_.refs_1_, bf16[384,1280]{1,0:T(8,128)(2,1)} %get-tuple-element.93.refs_2_, bf16[384,1280]{1,0:T(8,128)(2,1)} %get-tuple-element.94.refs_3_, ...), custom_call_target="tpu_custom_call" | custom-call | flops 1 | bytes 1 | tf_op jit(solution)/shard_map/join_plane/pallas_call | solution.py:231
  176.0 9.7 %backward_rows.2 = (bf16[640,768]{1,0:T(8,128)(2,1)}, bf16[640,256]{1,0:T(8,128)(2,1)}) custom-call(s32[1]{0:T(128)} %constant.69.clone.1.column_ref, bf16[384,5120]{1,0:T(8,128)(2,1)} %join_plane.5.refs_0_.refs_4_, bf16[256,5120]{1,0:T(8,128)(2,1)} %join_plane.3.refs_0_.refs_1_.refs_5_, bf16[256,5120]{1,0:T(8,128)(2,1)} %copy-done, ...), custom_call_target="tpu_custom_call" | custom-call | flops 1 | bytes 1 | tf_op jit(solution)/shard_map/backward_rows/pallas_call | solution.py:196
  186.0 4.1 %collective-permute-done.19.refs_3_ = bf16[256,5120]{1,0:T(8,128)(2,1)} collective-permute-done((bf16[256,5120]{1,0:T(8,128)(2,1)}, bf16[256,5120]{1,0:T(8,128)(2,1)}, u32[]{:S(2)}, u32[]{:S(2)}) %collective-permute-start.19) | collective-permute-done | bytes 2621472 | tf_op jit(solution)/shard_map/ppermute | solution.py:720
  190.1 10.5 %output_own.1 = (f32[256,1280]{1,0:T(8,128)}, bf16[256,1280]{1,0:T(8,128)(2,1)}, bf16[256,1280]{1,0:T(8,128)(2,1)}, bf16[256,1280]{1,0:T(8,128)(2,1)}, f32[256,1...) custom-call(s32[1]{0:T(128)} %bitcast.refs_0_.column_ref, ...), custom_call_target="tpu_custom_call" | custom-call | flops 1 | bytes 1 | tf_op jit(solution)/shard_map/output_own/pallas_call | solution.py:196
  206.0 7.7 %backward_rows.3 = (bf16[384,768]{1,0:T(8,128)(2,1)}, bf16[384,256]{1,0:T(8,128)(2,1)}) custom-call(s32[1]{0:T(128)} %constant.69.clone.1.column_ref, bf16[384,5120]{1,0:T(8,128)(2,1)} %copy-done.2, bf16[512,5120]{1,0:T(8,128)(2,1)} %get-tuple-element.90.refs_1_.refs_3_, bf16[768,384]{1,0:T(8,128)(2,1)} %get-tuple-element.96.refs_4_.refs_2_, ...), custom_call_target="tpu_custom_call" | custom-call | flops 1 | bytes 1 | tf_op jit(solution)/shard_map/backward_rows/pallas_call | solution.py:196
  213.7 13.1 %shadow_grads.1.refs_3_ = bf16[144,5120]{1,0:T(8,128)(2,1)} custom-call(s32[1]{0:T(128)} %constant.69.clone.1.column_ref, bf16[384,5120]{1,0:T(8,128)(2,1)} %join_plane.4.refs_0_, bf16[256,5120]{1,0:T(8,128)(2,1)} %join_plane.3.refs_0_.refs_1_.refs_5_, bf16[256,5120]{1,0:T(8,128)(2,1)} %copy-done, bf16[384,5120]{1,0:T(8,128)(2,1)} %collective-permute-done.14.refs_1_.refs_3_, ...), custom_call_target="tpu_custom_call" | custom-call | flops 1 | bytes 1 | tf_op jit(solution)/shard_map/shadow_grads/pallas_call | solution.py:196
  235.9 3.8 %collective-permute-start.31 = (bf16[128,1280]{1,0:T(8,128)(2,1)}, bf16[128,1280]{1,0:T(8,128)(2,1)S(1)}, u32[]{:S(2)}, u32[]{:S(2)}) collective-permute-start(bf16[128,1280]{1,0:T(8,128)(2,1)} %get-tuple-element.135.refs_6_), channel_id=1, source_target_pairs={{0,4},{1,5},{2,6},{3,7},{4,0},{5,1},{6,2},{7,3},{8,12},{9,13},{10,... | collective-permute-start | bytes 983048 | tf_op jit(solution)/shard_map/ppermute | solution.py:867
  242.2 11.4 %down_grad.1.refs_5_ = bf16[384,5120]{1,0:T(8,128)(2,1)} custom-call(s32[1]{0:T(128)} %constant.69.clone.1.column_ref, bf16[384,5120]{1,0:T(8,128)(2,1)} %join_plane.5.refs_0_.refs_4_, bf16[256,5120]{1,0:T(8,128)(2,1)} %join_plane.3.refs_0_.refs_1_.refs_5_, bf16[256,5120]{1,0:T(8,128)(2,1)} %copy-done, bf16[384,5120]{1,0:T(8,128)(2,1)} %copy-done.2, ...), custom_call_target="tpu_custom_call" | custom-call | flops 1 | bytes 1 | tf_op jit(solution)/shard_map/down_grad/pallas_call | solution.py:196
  257.5 14.4 %input_grads.1 = (bf16[5120,384]{1,0:T(8,128)(2,1)}, bf16[5120,384]{1,0:T(8,128)(2,1)}) custom-call(s32[1]{0:T(128)} %constant.69.clone.1.column_ref, bf16[384,5120]{1,0:T(8,128)(2,1)} %join_plane.4.refs_0_, bf16[256,5120]{1,0:T(8,128)(2,1)} %join_plane.3.refs_0_.refs_1_.refs_5_, bf16[256,5120]{1,0:T(8,128)(2,1)} %copy-done, ...), custom_call_target="tpu_custom_call" | custom-call | flops 1 | bytes 1 | tf_op jit(solution)/shard_map/input_grads/pallas_call | solution.py:196
  277.3 22.7 %collective-permute-done.35 = bf16[128,1280]{1,0:T(8,128)(2,1)S(1)} collective-permute-done((bf16[128,1280]{1,0:T(8,128)(2,1)S(1)}, bf16[128,1280]{1,0:T(8,128)(2,1)S(1)}, u32[]{:S(2)}, u32[]{:S(2)}) %collective-permute-start.35) | collective-permute-done | bytes 327712 | tf_op jit(solution)/shard_map/ppermute | solution.py:867
  (160 shorter events, 92.3 us)
Async XLA Ops:
  2.6 34.5 %collective-permute-start = (bf16[256,1280]{1,0:T(8,128)(2,1)}, bf16[256,1280]{1,0:T(8,128)(2,1)S(1)}, u32[]{:S(2)}, u32[]{:S(2)}) collective-permute-start(bf16[256,1280]{1,0:T(8,128)(2,1)} %stack_pieces.4.refs_1_), channel_id=1, source_target_pairs={{0,8},{8,0},{16,24},{24,16},{1,9},{9,1},{17,25},{25,17},{2,10},{10... | collective-permute-start | bytes 1966088 | tf_op jit(solution)/shard_map/ppermute | solution.py:725
  4.1 33.0 %collective-permute-start.1 = (bf16[256,1280]{1,0:T(8,128)(2,1)}, bf16[256,1280]{1,0:T(8,128)(2,1)S(1)}, u32[]{:S(2)}, u32[]{:S(2)}) collective-permute-start(bf16[256,1280]{1,0:T(8,128)(2,1)} %stack_pieces.4.refs_1_), channel_id=1, source_target_pairs={{0,16},{8,24},{16,0},{24,8},{1,17},{9,25},{17,1},{25,9},{2,18},{10... | collective-permute-start | bytes 1966088 | tf_op jit(solution)/shard_map/ppermute | solution.py:725
  7.2 22.9 %collective-permute-start.4 = (bf16[128,1280]{1,0:T(8,128)(2,1)}, bf16[128,1280]{1,0:T(8,128)(2,1)S(1)}, u32[]{:S(2)}, u32[]{:S(2)}) collective-permute-start(bf16[128,1280]{1,0:T(8,128)(2,1)} %refs_0_.3), channel_id=1, source_target_pairs={{0,4},{1,5},{2,6},{3,7},{4,0},{5,1},{6,2},{7,3},{8,12},{9,13},{10,... | collective-permute-start | bytes 983048 | tf_op jit(solution)/shard_map/ppermute | solution.py:716
  7.5 29.6 %collective-permute-start.5 = (bf16[128,1280]{1,0:T(8,128)(2,1)}, bf16[128,1280]{1,0:T(8,128)(2,1)}, u32[]{:S(2)}, u32[]{:S(2)}) collective-permute-start(bf16[128,1280]{1,0:T(8,128)(2,1)} %refs_0_.3), channel_id=1, source_target_pairs={{0,6},{1,7},{2,4},{3,5},{4,2},{5,3},{6,0},{7,1},{8,14},{9,15},{10,... | collective-permute-start | bytes 983048 | tf_op jit(solution)/shard_map/ppermute | solution.py:716
  48.7 30.0 %collective-permute-start.7 = (bf16[384,1280]{1,0:T(8,128)(2,1)}, bf16[384,1280]{1,0:T(8,128)(2,1)}, u32[]{:S(2)}, u32[]{:S(2)}) collective-permute-start(bf16[384,1280]{1,0:T(8,128)(2,1)} %stack_pieces.6.refs_1_), channel_id=1, source_target_pairs={{0,8},{8,0},{16,24},{24,16},{1,9},{9,1},{17,25},{25,17},{2,10},{10... | collective-permute-start | bytes 2949128 | tf_op jit(solution)/shard_map/ppermute | solution.py:725
  49.2 44.9 %collective-permute-start.8 = (bf16[384,1280]{1,0:T(8,128)(2,1)}, bf16[384,1280]{1,0:T(8,128)(2,1)}, u32[]{:S(2)}, u32[]{:S(2)}) collective-permute-start(bf16[384,1280]{1,0:T(8,128)(2,1)} %stack_pieces.6.refs_1_), channel_id=1, source_target_pairs={{0,16},{8,24},{16,0},{24,8},{1,17},{9,25},{17,1},{25,9},{2,18},{10... | collective-permute-start | bytes 2949128 | tf_op jit(solution)/shard_map/ppermute | solution.py:725
  58.3 35.8 %collective-permute-start.9 = (bf16[384,1280]{1,0:T(8,128)(2,1)}, bf16[384,1280]{1,0:T(8,128)(2,1)}, u32[]{:S(2)}, u32[]{:S(2)}) collective-permute-start(bf16[384,1280]{1,0:T(8,128)(2,1)} %stack_pieces.6.refs_1_), channel_id=1, source_target_pairs={{0,24},{8,16},{16,8},{24,0},{1,25},{9,17},{17,9},{25,1},{2,26},{10... | collective-permute-start | bytes 2949128 | tf_op jit(solution)/shard_map/ppermute | solution.py:725
  101.9 68.8 %collective-permute-start.20 = (bf16[384,1280]{1,0:T(8,128)(2,1)S(1)}, bf16[384,1280]{1,0:T(8,128)(2,1)}, u32[]{:S(2)}, u32[]{:S(2)}) collective-permute-start(bf16[384,1280]{1,0:T(8,128)(2,1)S(1)} %copy-done.3), channel_id=1, source_target_pairs={{0,8},{8,0},{16,24},{24,16},{1,9},{9,1},{17,25},{25,17},{2,10},{10... | collective-permute-start | bytes 2949128 | tf_op jit(solution)/shard_map/ppermute | solution.py:725
  103.5 67.3 %collective-permute-start.21 = (bf16[384,1280]{1,0:T(8,128)(2,1)S(1)}, bf16[384,1280]{1,0:T(8,128)(2,1)}, u32[]{:S(2)}, u32[]{:S(2)}) collective-permute-start(bf16[384,1280]{1,0:T(8,128)(2,1)S(1)} %copy-done.3), channel_id=1, source_target_pairs={{0,16},{8,24},{16,0},{24,8},{1,17},{9,25},{17,1},{25,9},{2,18},{10... | collective-permute-start | bytes 2949128 | tf_op jit(solution)/shard_map/ppermute | solution.py:725
  103.9 66.8 %collective-permute-start.22 = (bf16[384,1280]{1,0:T(8,128)(2,1)S(1)}, bf16[384,1280]{1,0:T(8,128)(2,1)}, u32[]{:S(2)}, u32[]{:S(2)}) collective-permute-start(bf16[384,1280]{1,0:T(8,128)(2,1)S(1)} %copy-done.3), channel_id=1, source_target_pairs={{0,24},{8,16},{16,8},{24,0},{1,25},{9,17},{17,9},{25,1},{2,26},{10... | collective-permute-start | bytes 2949128 | tf_op jit(solution)/shard_map/ppermute | solution.py:725
  109.0 30.1 %collective-permute-start.16 = (bf16[1,2,160,640]{3,2,1,0:T(8,128)(2,1)S(1)}, bf16[1,2,160,640]{3,2,1,0:T(8,128)(2,1)S(1)}, u32[]{:S(2)}, u32[]{:S(2)}) collective-permute-start(bf16[1,2,160,640]{3,2,1,0:T(8,128)(2,1)S(1)} %get-tuple-element.144), channel_id=1, source_target_pairs={{0,4},{1,5},{2,6},{3,7},{4,0},{5,1},{6,2},{7,3},{8,12},{9,13},{10,... | collective-permute-start | bytes 1228808 | tf_op jit(solution)/shard_map/ppermute | solution.py:745
  123.2 24.0 %collective-permute-start.17 = (bf16[1,2,160,640]{3,2,1,0:T(8,128)(2,1)}, bf16[1,2,160,640]{3,2,1,0:T(8,128)(2,1)S(1)}, u32[]{:S(2)}, u32[]{:S(2)}) collective-permute-start(bf16[1,2,160,640]{3,2,1,0:T(8,128)(2,1)} %after.11), channel_id=1, source_target_pairs={{0,6},{1,7},{2,4},{3,5},{4,2},{5,3},{6,0},{7,1},{8,14},{9,15},{10,... | collective-permute-start | bytes 1228808 | tf_op jit(solution)/shard_map/ppermute | solution.py:745
  175.5 28.6 %collective-permute-start.29 = (bf16[384,5120]{1,0:T(8,128)(2,1)}, bf16[384,5120]{1,0:T(8,128)(2,1)S(1)}, u32[]{:S(2)}, u32[]{:S(2)}) collective-permute-start(bf16[384,5120]{1,0:T(8,128)(2,1)} %join_plane.5.refs_0_.refs_4_), channel_id=1, source_target_pairs={{0,1},{1,0},{2,3},{3,2},{4,5},{5,4},{6,7},{7,6},{8,9},{9,8},{10,11... | collective-permute-start | bytes 11796488 | tf_op jit(solution)/shard_map/ppermute | solution.py:720
  200.6 30.2 %collective-permute-start.26 = (bf16[256,1280]{1,0:T(8,128)(2,1)}, bf16[256,1280]{1,0:T(8,128)(2,1)}, u32[]{:S(2)}, u32[]{:S(2)}) collective-permute-start(bf16[256,1280]{1,0:T(8,128)(2,1)} %get-tuple-element.110.refs_8_), channel_id=1, source_target_pairs={{0,8},{8,0},{16,24},{24,16},{1,9},{9,1},{17,25},{25,17},{2,10},{10... | collective-permute-start | bytes 1966088 | tf_op jit(solution)/shard_map/ppermute | solution.py:725
  202.1 30.8 %collective-permute-start.27 = (bf16[256,1280]{1,0:T(8,128)(2,1)}, bf16[256,1280]{1,0:T(8,128)(2,1)}, u32[]{:S(2)}, u32[]{:S(2)}) collective-permute-start(bf16[256,1280]{1,0:T(8,128)(2,1)} %get-tuple-element.111), channel_id=1, source_target_pairs={{0,16},{8,24},{16,0},{24,8},{1,17},{9,25},{17,1},{25,9},{2,18},{10... | collective-permute-start | bytes 1966088 | tf_op jit(solution)/shard_map/ppermute | solution.py:725
  202.5 30.4 %collective-permute-start.28 = (bf16[256,1280]{1,0:T(8,128)(2,1)}, bf16[256,1280]{1,0:T(8,128)(2,1)}, u32[]{:S(2)}, u32[]{:S(2)}) collective-permute-start(bf16[256,1280]{1,0:T(8,128)(2,1)} %get-tuple-element.112), channel_id=1, source_target_pairs={{0,24},{8,16},{16,8},{24,0},{1,25},{9,17},{17,9},{25,1},{2,26},{10... | collective-permute-start | bytes 1966088 | tf_op jit(solution)/shard_map/ppermute | solution.py:725
  229.3 42.6 %collective-permute-start.23 = (bf16[256,1280]{1,0:T(8,128)(2,1)}, bf16[256,1280]{1,0:T(8,128)(2,1)S(1)}, u32[]{:S(2)}, u32[]{:S(2)}) collective-permute-start(bf16[256,1280]{1,0:T(8,128)(2,1)} %get-tuple-element.106.refs_9_), channel_id=1, source_target_pairs={{0,8},{8,0},{16,24},{24,16},{1,9},{9,1},{17,25},{25,17},{2,10},{10... | collective-permute-start | bytes 1966088 | tf_op jit(solution)/shard_map/ppermute | solution.py:725
  230.8 41.1 %collective-permute-start.24 = (bf16[256,1280]{1,0:T(8,128)(2,1)}, bf16[256,1280]{1,0:T(8,128)(2,1)S(1)}, u32[]{:S(2)}, u32[]{:S(2)}) collective-permute-start(bf16[256,1280]{1,0:T(8,128)(2,1)} %get-tuple-element.107), channel_id=1, source_target_pairs={{0,16},{8,24},{16,0},{24,8},{1,17},{9,25},{17,1},{25,9},{2,18},{10... | collective-permute-start | bytes 1966088 | tf_op jit(solution)/shard_map/ppermute | solution.py:725
  232.9 39.0 %collective-permute-start.25 = (bf16[256,1280]{1,0:T(8,128)(2,1)}, bf16[256,1280]{1,0:T(8,128)(2,1)S(1)}, u32[]{:S(2)}, u32[]{:S(2)}) collective-permute-start(bf16[256,1280]{1,0:T(8,128)(2,1)} %get-tuple-element.108), channel_id=1, source_target_pairs={{0,24},{8,16},{16,8},{24,0},{1,25},{9,17},{17,9},{25,1},{2,26},{10... | collective-permute-start | bytes 1966088 | tf_op jit(solution)/shard_map/ppermute | solution.py:725
  235.9 17.7 %collective-permute-start.30 = (bf16[128,1280]{1,0:T(8,128)(2,1)}, bf16[128,1280]{1,0:T(8,128)(2,1)S(1)}, u32[]{:S(2)}, u32[]{:S(2)}) collective-permute-start(bf16[128,1280]{1,0:T(8,128)(2,1)} %get-tuple-element.136.refs_5_), channel_id=1, source_target_pairs={{0,2},{1,3},{2,0},{3,1},{4,6},{5,7},{6,4},{7,5},{8,10},{9,11},{10,... | collective-permute-start | bytes 983048 | tf_op jit(solution)/shard_map/ppermute | solution.py:867
  235.9 18.2 %collective-permute-start.31 = (bf16[128,1280]{1,0:T(8,128)(2,1)}, bf16[128,1280]{1,0:T(8,128)(2,1)S(1)}, u32[]{:S(2)}, u32[]{:S(2)}) collective-permute-start(bf16[128,1280]{1,0:T(8,128)(2,1)} %get-tuple-element.135.refs_6_), channel_id=1, source_target_pairs={{0,4},{1,5},{2,6},{3,7},{4,0},{5,1},{6,2},{7,3},{8,12},{9,13},{10,... | collective-permute-start | bytes 983048 | tf_op jit(solution)/shard_map/ppermute | solution.py:867
  254.8 18.0 %collective-permute-start.34 = (bf16[1,2,144,640]{3,2,1,0:T(8,128)(2,1)}, bf16[1,2,144,640]{3,2,1,0:T(8,128)(2,1)S(1)}, u32[]{:S(2)}, u32[]{:S(2)}) collective-permute-start(bf16[1,2,144,640]{3,2,1,0:T(8,128)(2,1)} %get-tuple-element.119), channel_id=1, source_target_pairs={{0,4},{1,5},{2,6},{3,7},{4,0},{5,1},{6,2},{7,3},{8,12},{9,13},{10,... | collective-permute-start | bytes 1105928 | tf_op jit(solution)/shard_map/ppermute | solution.py:745
  275.2 24.8 %collective-permute-start.35 = (bf16[128,1280]{1,0:T(8,128)(2,1)S(1)}, bf16[128,1280]{1,0:T(8,128)(2,1)S(1)}, u32[]{:S(2)}, u32[]{:S(2)}) collective-permute-start(bf16[128,1280]{1,0:T(8,128)(2,1)S(1)} %add_convert_fusion.1), channel_id=1, source_target_pairs={{0,6},{1,7},{2,4},{3,5},{4,2},{5,3},{6,0},{7,1},{8,14},{9,15},{10,... | collective-permute-start | bytes 983048 | tf_op jit(solution)/shard_map/ppermute | solution.py:867
  276.0 29.6 %collective-permute-start.36 = (bf16[1,2,144,640]{3,2,1,0:T(8,128)(2,1)}, bf16[1,2,144,640]{3,2,1,0:T(8,128)(2,1)S(1)}, u32[]{:S(2)}, u32[]{:S(2)}) collective-permute-start(bf16[1,2,144,640]{3,2,1,0:T(8,128)(2,1)} %get-tuple-element.131), channel_id=1, source_target_pairs={{0,6},{1,7},{2,4},{3,5},{4,2},{5,3},{6,0},{7,1},{8,14},{9,15},{10,... | collective-permute-start | bytes 1105928 | tf_op jit(solution)/shard_map/ppermute | solution.py:745
  (43 other events, 381.4 us)
where the time goes:
time: 312 us; the launch traced here: 310 us
  Pallas kernels  135 us (43%)
  waiting for transfers between devices  101 us (32%)
  starting transfers between devices  34.2 us (11%)
  other arithmetic  23.5 us (8%)
  local copies, waits for them, and re-layouts  15.7 us (5%)
    pallas_call x10, Pallas kernels, kernel_call(): pl.pallas_call(run, out_shape=out_shape, grid_spec=pltpu.PrefetchScalarGr...  99.8 us
    ppermute x6, waiting for transfers between devices, send_piece(): return lax.ppermute(piece, 'ep', swap_pairs(lax.axis_size('ep'), 2 * shift))  28 us
    ppermute x6, waiting for transfers between devices, send_along_z(): lax.ppermute(own, 'ep', swap_pairs(ep_count, 2 * s))  24.9 us
    ppermute x3, waiting for transfers between devices, send_rows(): return lax.ppermute(piece, 'ep', swap_pairs(ep_count, 2 * (i + 1)))  23.1 us
    ppermute x14, waiting for transfers between devices, send_plane(): lax.ppermute(p, 'tp', swap_pairs(lax.axis_size('tp'), bit))  17.2 us
    pallas_call x3, Pallas kernels, join_plane(): pl.pallas_call(body, out_shape=shape_of(rows, count * quarter), grid_spec...  13.9 us
    ppermute x14, starting transfers between devices, send_plane(): lax.ppermute(p, 'tp', swap_pairs(lax.axis_size('tp'), bit))  13.5 us
    pallas_call x4, Pallas kernels, stack_pieces(): pl.pallas_call(body, out_shape=shape_of(count * rows, columns), grid=(cou...  9.26 us
  transfers between devices with their start and end apart: 37, of which 17 were waited for; matrix products, arithmetic and copies ran while one was open for 10% of the time, Pallas kernels for 36%

commit v1 on v0

--- a/solution.py
+++ b/solution.py
@@ -482,14 +482,13 @@
     count = rows // 2 // parts
 
     def body(weighted_ref, down_ref, *outs):
+        value = dot32(weighted_ref[...], down_ref[...]).astype(jnp.bfloat16)
         for i, out in enumerate(outs):
             first, last = slot_rows + i * count, slot_rows + (i + 1) * count
             kept = min(last, rows // 2) - first
-            value = dot32(weighted_ref[first : first + kept, :], down_ref[...])
-            out[:kept, :] = value.astype(jnp.bfloat16)
+            out[:kept, :] = value[first : first + kept]
             if kept < count:
-                value = dot32(weighted_ref[: count - kept, :], down_ref[...])
-                out[kept:, :] = value.astype(jnp.bfloat16)
+                out[kept:, :] = value[: count - kept]
 
     return kernel_call(
         body,
@@ -513,9 +512,9 @@
     parts = len(got)
 
     def body(weighted_ref, down_ref, *refs):
+        product = dot32(weighted_ref[...], down_ref[...])
         for i in range(parts):
-            value = dot32(weighted_ref[i * count : (i + 1) * count, :], down_ref[...])
-            value = value + refs[i][...].astype(jnp.float32)
+            value = product[i * count : (i + 1) * count] + refs[i][...].astype(jnp.float32)
             for j, out in enumerate(refs[parts + 4 * i : parts + 4 * i + 4]):
 
                 @pl.when(pl.program_id(0) == 3 - j)
@@ -602,7 +601,7 @@
     return held[...]
 
 
-def shadow_grads(x_groups, dy_groups, pre_s, weighted, units, tile, earlier=()):
+def shadow_grads(x_groups, dy_groups, pre_s, weighted, units, block, tile, earlier=()):
     rows, wide = weighted.shape[0], pre_s[0].shape[1]
     apart = wide // 2
     width = x_groups[0][0].shape[1]
@@ -621,11 +620,14 @@
                 start += ref.shape[0]
             hidden_t[...] = hidden_ref[...].T
 
-        value = dot32(pre_t[...], stage_rows(refs[:n], x_groups, held))
-        out[:units, :] = value[:units].astype(jnp.bfloat16)
-        out[units : 2 * units, :] = value[apart : apart + units].astype(jnp.bfloat16)
-        value = dot32(hidden_t[...], stage_rows(refs[n : 2 * n], dy_groups, held))
-        out[2 * units :, :] = value[:units].astype(jnp.bfloat16)
+        value = dot32(pre_t[...], stage_rows(refs[:n], x_groups, held)).astype(jnp.bfloat16)
+        for i in range(tile // block):
+            part = slice(i * block, (i + 1) * block)
+            out[i, :units, :] = value[:units, part]
+            out[i, units : 2 * units, :] = value[apart : apart + units, part]
+        value = dot32(hidden_t[...], stage_rows(refs[n : 2 * n], dy_groups, held)).astype(jnp.bfloat16)
+        for i in range(tile // block):
+            out[i, 2 * units :, :] = value[:units, i * block : (i + 1) * block]
 
     (out,) = kernel_call(
         body,
@@ -634,8 +636,8 @@
         + row_specs(dy_groups, tile)
         + [whole(p) for p in pre_s]
         + [pl.BlockSpec((rows, apart), lambda *_: (0, weighted.shape[1] // apart - 1))],
-        [pl.BlockSpec((3 * units, tile), lambda k, *_: (0, k))],
-        [shape_of(3 * units, width)],
+        [pl.BlockSpec((tile // block, 3 * units, block), lambda k, *_: (k, 0, 0))],
+        [shape_of(width // block, 3 * units, block)],
         [g[0] for g in x_groups + dy_groups] + list(pre_s) + [weighted],
         [
             pltpu.VMEM((rows, tile), jnp.bfloat16),
@@ -852,9 +854,8 @@
         dy_groups[3:], down, segments[3:], per_row, first_rows, 2 * tile, earlier=[own[1] for own in owns]
     )
     pre, pre_s = [pre_first, pre_last], [pre_s_first, pre_s_last]
-    grad_s = shadow_grads(x_groups, dy_groups, pre_s, weighted, shadow_part, tile)
-    blocks = grad_s.reshape(3 * shadow_part, ep_count, block_width).transpose(1, 0, 2)
-    grad_pieces = chip_pieces(*exchange_cores(blocks))
+    grad_s = shadow_grads(x_groups, dy_groups, pre_s, weighted, shadow_part, block_width, 2 * tile)
+    grad_pieces = chip_pieces(*exchange_cores(grad_s))
 
     def slot_rows(i):
         part = slice(i % (steps // parts) * tok_count, (i % (steps // parts) + 1) * tok_count)
@@ -869,11 +870,11 @@
     early = steps // parts if parts > 1 else 0
     sums[0] = after(sums[0], grad_s)
     rows = [slot_rows(i).astype(jnp.bfloat16) for i in range(early)]
-    grad_down = down_grad(dy_groups, weighted, hidden_part, tile, earlier=[*rows, grad_pieces[0]])
+    grad_down = down_grad(dy_groups, weighted, hidden_part, 2 * tile, earlier=[*rows, grad_pieces[0]])
     rows = [send_rows(piece, i) for i, piece in enumerate(rows)]
     fenced = after([*rows, *grad_pieces[1:]], grad_down)
     rows, grad_pieces[1:] = list(fenced[:early]), fenced[early:]
-    grad_gate, grad_up = input_grads(x_groups, pre, tile, earlier=[grad_pieces[1]])
+    grad_gate, grad_up = input_grads(x_groups, pre, 2 * tile, earlier=[grad_pieces[1]])
     for shift in range(1, steps - 1):
         grad_pieces[shift] = send_piece(grad_pieces[shift], shift)
     fenced = after([*sums[-1], *grad_pieces[1:]], grad_gate)

time: 312 us -> 307 us (0.984)
  Pallas kernels: 135 us -> 129 us
    pallas_call x10, Pallas kernels: 99.8 us -> 94 us  [kernel_call(): pl.pallas_call(run, out_shape=out_shape, grid_spec=pltpu.PrefetchScalarGr...]
    unnamed x60 -> x68, local copies, waits for them, and re-layouts: 6.51 us -> 7.22 us
  transfers between devices with their start and end apart: 37 -> 37, of which waited for: 17 -> 16; matrix products, arithmetic and copies ran while one was open for 10% -> 10% of each run, Pallas kernels for 36% -> 35%
where the time goes in v1:
time: 307 us; the launch traced here: 305 us
  Pallas kernels  129 us (42%)
  waiting for transfers between devices  102 us (33%)
  starting transfers between devices  34.3 us (11%)
  other arithmetic  23.8 us (8%)
  local copies, waits for them, and re-layouts  14.9 us (5%)
    pallas_call x10, Pallas kernels, kernel_call(): pl.pallas_call(run, out_shape=out_shape, grid_spec=pltpu.PrefetchScalarGr...  94 us
    ppermute x6, waiting for transfers between devices, send_piece(): return lax.ppermute(piece, 'ep', swap_pairs(lax.axis_size('ep'), 2 * shift))  27.3 us
    ppermute x6, waiting for transfers between devices, send_along_z(): lax.ppermute(own, 'ep', swap_pairs(ep_count, 2 * s))  24.8 us
    ppermute x3, waiting for transfers between devices, send_rows(): return lax.ppermute(piece, 'ep', swap_pairs(ep_count, 2 * (i + 1)))  22.4 us
    ppermute x14, waiting for transfers between devices, send_plane(): lax.ppermute(p, 'tp', swap_pairs(lax.axis_size('tp'), bit))  19.7 us
    pallas_call x3, Pallas kernels, join_plane(): pl.pallas_call(body, out_shape=shape_of(rows, count * quarter), grid_spec...  13.9 us
    ppermute x14, starting transfers between devices, send_plane(): lax.ppermute(p, 'tp', swap_pairs(lax.axis_size('tp'), bit))  13.5 us
    pallas_call x4, Pallas kernels, stack_pieces(): pl.pallas_call(body, out_shape=shape_of(count * rows, columns), grid=(cou...  9.28 us
  transfers between devices with their start and end apart: 37, of which 16 were waited for; matrix products, arithmetic and copies ran while one was open for 10% of the time, Pallas kernels for 35%

profile of v1, /device:TPU:16, one launch (start us, length us, event | category | flops | bytes accessed | tf_op | source)
XLA Modules:
  0.0 304.8 jit_solution(909308671656313068)
XLA Ops:
  9.1 7.1 %pad_maximum_fusion.refs_6_.refs_2_ = bf16[5120,768]{1,0:T(8,128)(2,1)} fusion(bf16[5120,384]{1,0:T(8,128)(2,1)} %bitcast.98, bf16[5120,384]{1,0:T(8,128)(2,1)} %bitcast.99), kind=kLoop, calls=%fused_computation | loop fusion | flops 15728640 | bytes 15728640 | tf_op jit(solution)/shard_map/concatenate | solution.py:797
  30.0 7.1 %collective-permute-done.5.refs_5_ = bf16[128,1280]{1,0:T(8,128)(2,1)} collective-permute-done((bf16[128,1280]{1,0:T(8,128)(2,1)}, bf16[128,1280]{1,0:T(8,128)(2,1)}, u32[]{:S(2)}, u32[]{:S(2)}) %collective-permute-start.5) | collective-permute-done | bytes 327712 | tf_op jit(solution)/shard_map/ppermute | solution.py:718
  39.4 4.1 %join_plane.3.refs_0_.refs_1_.refs_5_ = bf16[256,5120]{1,0:T(8,128)(2,1)} custom-call(s32[1]{0:T(128)} %bitcast.refs_0_.column_ref, bf16[256,1280]{1,0:T(8,128)(2,1)} %stack_pieces.4.refs_1_, bf16[256,1280]{1,0:T(8,128)(2,1)} %get-tuple-element.71.refs_2_, bf16[256,1280]{1,0:T(8,128)(2,1)} %get-tuple-element.72.refs_3_, ...), custom_call_target="tpu_custom_call" | custom-call | flops 1 | bytes 1 | tf_op jit(solution)/shard_map/join_plane/pallas_call | solution.py:231
  49.7 8.6 %collective-permute-done.11.refs_5_ = bf16[128,1280]{1,0:T(8,128)(2,1)S(1)} collective-permute-done((bf16[128,1280]{1,0:T(8,128)(2,1)S(1)}, bf16[128,1280]{1,0:T(8,128)(2,1)S(1)}, u32[]{:S(2)}, u32[]{:S(2)}) %collective-permute-start.11) | collective-permute-done | bytes 327712 | tf_op jit(solution)/shard_map/ppermute | solution.py:718
  63.1 5.1 %pad.9.refs_3_ = bf16[512,5120]{1,0:T(8,128)(2,1)} pad(bf16[384,5120]{1,0:T(8,128)(2,1)} %bitcast.96, bf16[]{:T(256)} %constant.71.clone.1), padding=0_128x0_0 | pad | bytes 9175042 | tf_op jit(solution)/shard_map/jit(_pad)/pad | solution.py:808
  68.2 7.0 %forward_rows.3 = (bf16[256,384]{1,0:T(8,128)(2,1)}, bf16[256,384]{1,0:T(8,128)(2,1)}, bf16[256,384]{1,0:T(8,128)(2,1)}) custom-call(s32[1]{0:T(128)} %constant.69.clone.1.column_ref, bf16[256,5120]{1,0:T(8,128)(2,1)} %join_plane.3.refs_0_.refs_1_.refs_5_, bf16[256,5120]{1,0:T(8,128)(2,1)} %copy-done, bf16[5120,768]{1,0:T(8,128)(2,1)} %pad_maximum_fusion.refs_6_.refs_2_), custom_call_target="tpu_custom_call" | custom-call | flops 1 | bytes 1 | tf_op jit(solution)/shard_map/forward_rows/pallas_call | solution.py:196
  78.7 15.5 %collective-permute-done.8.refs_1_ = bf16[384,1280]{1,0:T(8,128)(2,1)} collective-permute-done((bf16[384,1280]{1,0:T(8,128)(2,1)}, bf16[384,1280]{1,0:T(8,128)(2,1)}, u32[]{:S(2)}, u32[]{:S(2)}) %collective-permute-start.8) | collective-permute-done | bytes 983072 | tf_op jit(solution)/shard_map/ppermute | solution.py:727
  96.9 5.0 %join_plane.4.refs_0_ = bf16[384,5120]{1,0:T(8,128)(2,1)} custom-call(s32[1]{0:T(128)} %bitcast.refs_0_.column_ref, bf16[384,1280]{1,0:T(8,128)(2,1)} %stack_pieces.6.refs_1_, bf16[384,1280]{1,0:T(8,128)(2,1)} %get-tuple-element.78.refs_2_, bf16[384,1280]{1,0:T(8,128)(2,1)} %get-tuple-element.79.refs_3_, bf16[384,1280]{1,0:T(8,128)(2,1)} %get-tuple-element.80.refs_4_, ...), custom_call_target="tpu_custom_call" | custom-call | flops 1 | bytes 1 | tf_op jit(solution)/shard_map/join_plane/pallas_call | solution.py:231
  111.7 11.5 %forward_rows.4 = (bf16[768,384]{1,0:T(8,128)(2,1)}, bf16[768,384]{1,0:T(8,128)(2,1)}, bf16[768,384]{1,0:T(8,128)(2,1)}) custom-call(s32[1]{0:T(128)} %constant.69.clone.1.column_ref, bf16[384,5120]{1,0:T(8,128)(2,1)} %join_plane.4.refs_0_, bf16[384,5120]{1,0:T(8,128)(2,1)} %collective-permute-done.14.refs_1_.refs_3_, ...), custom_call_target="tpu_custom_call" | custom-call | flops 1 | bytes 1 | tf_op jit(solution)/shard_map/forward_rows/pallas_call | solution.py:196
  123.3 15.8 %collective-permute-done.16.refs_2_.refs_5_ = bf16[1,2,160,640]{3,2,1,0:T(8,128)(2,1)S(1)} collective-permute-done((bf16[1,2,160,640]{3,2,1,0:T(8,128)(2,1)S(1)}, bf16[1,2,160,640]{3,2,1,0:T(8,128)(2,1)S(1)}, u32[]{:S(2)}, u32[]{:S(2)}) %collective-permute-start.16) | collective-permute-done | bytes 409632 | tf_op jit(solution)/shard_map/ppermute | solution.py:747
  139.1 8.1 %collective-permute-done.17.refs_3_.refs_6_ = bf16[1,2,160,640]{3,2,1,0:T(8,128)(2,1)S(1)} collective-permute-done((bf16[1,2,160,640]{3,2,1,0:T(8,128)(2,1)}, bf16[1,2,160,640]{3,2,1,0:T(8,128)(2,1)S(1)}, u32[]{:S(2)}, u32[]{:S(2)}) %collective-permute-start.17) | collective-permute-done | bytes 409632 | tf_op jit(solution)/shard_map/ppermute | solution.py:747
  148.0 4.9 %lay_out_shadow.1 = (bf16[256,5120]{1,0:T(8,128)(2,1)}, bf16[512,5120]{1,0:T(8,128)(2,1)}) custom-call(s32[1]{0:T(128)} %bitcast.14.chip_ref, bf16[1,2,160,640]{3,2,1,0:T(8,128)(2,1)} %get-tuple-element.142.refs_0_.refs_3_, bf16[1,2,160,640]{3,2,1,0:T(8,128)(2,1)} %copy-done.14, ...), custom_call_target="tpu_custom_call", output_to_operand_aliasing={{1}: (5, {})} | custom-call | flops 1 | bytes 1 | tf_op jit(solution)/shard_map/lay_out_shadow/pallas_call | solution.py:299
  152.9 8.0 %forward_rows.5 = (bf16[1024,128]{1,0:T(8,128)(2,1)}, bf16[1024,128]{1,0:T(8,128)(2,1)}, bf16[1024,128]{1,0:T(8,128)(2,1)}) custom-call(s32[1]{0:T(128)} %constant.69.clone.1.column_ref, bf16[384,5120]{1,0:T(8,128)(2,1)} %join_plane.4.refs_0_, bf16[256,5120]{1,0:T(8,128)(2,1)} %join_plane.3.refs_0_.refs_1_.refs_5_, bf16[256,5120]{1,0:T(8,128)(2,1)} %copy-done, ...), custom_call_target="tpu_custom_call" | custom-call | flops 1 | bytes 1 | tf_op jit(solution)/shard_map/forward_rows/pallas_call | solution.py:196
  164.3 6.9 %output_other.1 = (bf16[256,5120]{1,0:T(8,128)(2,1)}, bf16[256,5120]{1,0:T(8,128)(2,1)}) custom-call(s32[1]{0:T(128)} %bitcast.refs_0_.column_ref, bf16[1024,512]{1,0:T(8,128)(2,1)} %get-tuple-element.89.refs_0_.refs_10_.refs_4_, bf16[512,5120]{1,0:T(8,128)(2,1)} %get-tuple-element.90.refs_1_.refs_3_), custom_call_target="tpu_custom_call" | custom-call | flops 1 | bytes 1 | tf_op jit(solution)/shard_map/output_other/pallas_call | solution.py:196
  171.2 4.7 %join_plane.5.refs_0_.refs_4_ = bf16[384,5120]{1,0:T(8,128)(2,1)} custom-call(s32[1]{0:T(128)} %bitcast.refs_0_.column_ref, bf16[384,1280]{1,0:T(8,128)(2,1)} %stack_pieces.7.refs_5_.refs_1_, bf16[384,1280]{1,0:T(8,128)(2,1)} %get-tuple-element.93.refs_2_, bf16[384,1280]{1,0:T(8,128)(2,1)} %get-tuple-element.94.refs_3_, ...), custom_call_target="tpu_custom_call" | custom-call | flops 1 | bytes 1 | tf_op jit(solution)/shard_map/join_plane/pallas_call | solution.py:231
  176.4 9.7 %backward_rows.2 = (bf16[640,768]{1,0:T(8,128)(2,1)}, bf16[640,256]{1,0:T(8,128)(2,1)}) custom-call(s32[1]{0:T(128)} %constant.69.clone.1.column_ref, bf16[384,5120]{1,0:T(8,128)(2,1)} %join_plane.5.refs_0_.refs_4_, bf16[256,5120]{1,0:T(8,128)(2,1)} %join_plane.3.refs_0_.refs_1_.refs_5_, bf16[256,5120]{1,0:T(8,128)(2,1)} %copy-done, ...), custom_call_target="tpu_custom_call" | custom-call | flops 1 | bytes 1 | tf_op jit(solution)/shard_map/backward_rows/pallas_call | solution.py:196
  186.4 4.1 %collective-permute-done.19.refs_3_ = bf16[256,5120]{1,0:T(8,128)(2,1)} collective-permute-done((bf16[256,5120]{1,0:T(8,128)(2,1)}, bf16[256,5120]{1,0:T(8,128)(2,1)}, u32[]{:S(2)}, u32[]{:S(2)}) %collective-permute-start.19) | collective-permute-done | bytes 2621472 | tf_op jit(solution)/shard_map/ppermute | solution.py:722
  190.5 10.2 %output_own.1 = (f32[256,1280]{1,0:T(8,128)}, bf16[256,1280]{1,0:T(8,128)(2,1)}, bf16[256,1280]{1,0:T(8,128)(2,1)}, bf16[256,1280]{1,0:T(8,128)(2,1)}, f32[256,1...) custom-call(s32[1]{0:T(128)} %bitcast.refs_0_.column_ref, ...), custom_call_target="tpu_custom_call" | custom-call | flops 1 | bytes 1 | tf_op jit(solution)/shard_map/output_own/pallas_call | solution.py:196
  206.1 7.7 %backward_rows.3 = (bf16[384,768]{1,0:T(8,128)(2,1)}, bf16[384,256]{1,0:T(8,128)(2,1)}) custom-call(s32[1]{0:T(128)} %constant.69.clone.1.column_ref, bf16[384,5120]{1,0:T(8,128)(2,1)} %copy-done.2, bf16[512,5120]{1,0:T(8,128)(2,1)} %get-tuple-element.90.refs_1_.refs_3_, bf16[768,384]{1,0:T(8,128)(2,1)} %get-tuple-element.96.refs_4_.refs_2_, ...), custom_call_target="tpu_custom_call" | custom-call | flops 1 | bytes 1 | tf_op jit(solution)/shard_map/backward_rows/pallas_call | solution.py:196
  213.8 11.1 %shadow_grads.1.refs_3_ = bf16[8,144,640]{2,1,0:T(8,128)(2,1)} custom-call(s32[1]{0:T(128)} %constant.69.clone.1.column_ref, bf16[384,5120]{1,0:T(8,128)(2,1)} %join_plane.4.refs_0_, bf16[256,5120]{1,0:T(8,128)(2,1)} %join_plane.3.refs_0_.refs_1_.refs_5_, bf16[256,5120]{1,0:T(8,128)(2,1)} %copy-done, ...), custom_call_target="tpu_custom_call" | custom-call | flops 1 | bytes 1 | tf_op jit(solution)/shard_map/shadow_grads/pallas_call | solution.py:196
  229.2 4.2 %collective-permute-done.27.refs_1_ = bf16[256,1280]{1,0:T(8,128)(2,1)} collective-permute-done((bf16[256,1280]{1,0:T(8,128)(2,1)}, bf16[256,1280]{1,0:T(8,128)(2,1)}, u32[]{:S(2)}, u32[]{:S(2)}) %collective-permute-start.27) | collective-permute-done | bytes 655392 | tf_op jit(solution)/shard_map/ppermute | solution.py:727
  241.7 9.1 %down_grad.1.refs_5_ = bf16[384,5120]{1,0:T(8,128)(2,1)} custom-call(s32[1]{0:T(128)} %constant.69.clone.1.column_ref, bf16[384,5120]{1,0:T(8,128)(2,1)} %join_plane.5.refs_0_.refs_4_, bf16[256,5120]{1,0:T(8,128)(2,1)} %join_plane.3.refs_0_.refs_1_.refs_5_, bf16[256,5120]{1,0:T(8,128)(2,1)} %copy-done, bf16[384,5120]{1,0:T(8,128)(2,1)} %copy-done.2, ...), custom_call_target="tpu_custom_call" | custom-call | flops 1 | bytes 1 | tf_op jit(solution)/shard_map/down_grad/pallas_call | solution.py:196
  255.7 12.9 %input_grads.1 = (bf16[5120,384]{1,0:T(8,128)(2,1)}, bf16[5120,384]{1,0:T(8,128)(2,1)}) custom-call(s32[1]{0:T(128)} %constant.69.clone.1.column_ref, bf16[384,5120]{1,0:T(8,128)(2,1)} %join_plane.4.refs_0_, bf16[256,5120]{1,0:T(8,128)(2,1)} %join_plane.3.refs_0_.refs_1_.refs_5_, bf16[256,5120]{1,0:T(8,128)(2,1)} %copy-done, ...), custom_call_target="tpu_custom_call" | custom-call | flops 1 | bytes 1 | tf_op jit(solution)/shard_map/input_grads/pallas_call | solution.py:196
  273.8 21.1 %collective-permute-done.35 = bf16[128,1280]{1,0:T(8,128)(2,1)S(1)} collective-permute-done((bf16[128,1280]{1,0:T(8,128)(2,1)S(1)}, bf16[128,1280]{1,0:T(8,128)(2,1)S(1)}, u32[]{:S(2)}, u32[]{:S(2)}) %collective-permute-start.35) | collective-permute-done | bytes 327712 | tf_op jit(solution)/shard_map/ppermute | solution.py:868
  (167 shorter events, 94.3 us)
Async XLA Ops:
  2.6 34.5 %collective-permute-start = (bf16[256,1280]{1,0:T(8,128)(2,1)}, bf16[256,1280]{1,0:T(8,128)(2,1)S(1)}, u32[]{:S(2)}, u32[]{:S(2)}) collective-permute-start(bf16[256,1280]{1,0:T(8,128)(2,1)} %stack_pieces.4.refs_1_), channel_id=1, source_target_pairs={{0,8},{8,0},{16,24},{24,16},{1,9},{9,1},{17,25},{25,17},{2,10},{10... | collective-permute-start | bytes 1966088 | tf_op jit(solution)/shard_map/ppermute | solution.py:727
  4.1 33.0 %collective-permute-start.1 = (bf16[256,1280]{1,0:T(8,128)(2,1)}, bf16[256,1280]{1,0:T(8,128)(2,1)S(1)}, u32[]{:S(2)}, u32[]{:S(2)}) collective-permute-start(bf16[256,1280]{1,0:T(8,128)(2,1)} %stack_pieces.4.refs_1_), channel_id=1, source_target_pairs={{0,16},{8,24},{16,0},{24,8},{1,17},{9,25},{17,1},{25,9},{2,18},{10... | collective-permute-start | bytes 1966088 | tf_op jit(solution)/shard_map/ppermute | solution.py:727
  7.2 22.9 %collective-permute-start.4 = (bf16[128,1280]{1,0:T(8,128)(2,1)}, bf16[128,1280]{1,0:T(8,128)(2,1)S(1)}, u32[]{:S(2)}, u32[]{:S(2)}) collective-permute-start(bf16[128,1280]{1,0:T(8,128)(2,1)} %refs_0_.3), channel_id=1, source_target_pairs={{0,4},{1,5},{2,6},{3,7},{4,0},{5,1},{6,2},{7,3},{8,12},{9,13},{10,... | collective-permute-start | bytes 983048 | tf_op jit(solution)/shard_map/ppermute | solution.py:718
  7.5 29.6 %collective-permute-start.5 = (bf16[128,1280]{1,0:T(8,128)(2,1)}, bf16[128,1280]{1,0:T(8,128)(2,1)}, u32[]{:S(2)}, u32[]{:S(2)}) collective-permute-start(bf16[128,1280]{1,0:T(8,128)(2,1)} %refs_0_.3), channel_id=1, source_target_pairs={{0,6},{1,7},{2,4},{3,5},{4,2},{5,3},{6,0},{7,1},{8,14},{9,15},{10,... | collective-permute-start | bytes 983048 | tf_op jit(solution)/shard_map/ppermute | solution.py:718
  43.6 17.7 %collective-permute-start.6 = (bf16[256,5120]{1,0:T(8,128)(2,1)}, bf16[256,5120]{1,0:T(8,128)(2,1)S(1)}, u32[]{:S(2)}, u32[]{:S(2)}) collective-permute-start(bf16[256,5120]{1,0:T(8,128)(2,1)} %join_plane.3.refs_0_.refs_1_.refs_5_), channel_id=1, source_target_pairs={{0,1},{1,0},{2,3},{3,2},{4,5},{5,4},{6,7},{7,6},{8,9},{9,8},{10,11... | collective-permute-start | bytes 7864328 | tf_op jit(solution)/shard_map/ppermute | solution.py:722
  48.7 30.0 %collective-permute-start.7 = (bf16[384,1280]{1,0:T(8,128)(2,1)}, bf16[384,1280]{1,0:T(8,128)(2,1)}, u32[]{:S(2)}, u32[]{:S(2)}) collective-permute-start(bf16[384,1280]{1,0:T(8,128)(2,1)} %stack_pieces.6.refs_1_), channel_id=1, source_target_pairs={{0,8},{8,0},{16,24},{24,16},{1,9},{9,1},{17,25},{25,17},{2,10},{10... | collective-permute-start | bytes 2949128 | tf_op jit(solution)/shard_map/ppermute | solution.py:727
  49.2 44.9 %collective-permute-start.8 = (bf16[384,1280]{1,0:T(8,128)(2,1)}, bf16[384,1280]{1,0:T(8,128)(2,1)}, u32[]{:S(2)}, u32[]{:S(2)}) collective-permute-start(bf16[384,1280]{1,0:T(8,128)(2,1)} %stack_pieces.6.refs_1_), channel_id=1, source_target_pairs={{0,16},{8,24},{16,0},{24,8},{1,17},{9,25},{17,1},{25,9},{2,18},{10... | collective-permute-start | bytes 2949128 | tf_op jit(solution)/shard_map/ppermute | solution.py:727
  58.3 35.8 %collective-permute-start.9 = (bf16[384,1280]{1,0:T(8,128)(2,1)}, bf16[384,1280]{1,0:T(8,128)(2,1)}, u32[]{:S(2)}, u32[]{:S(2)}) collective-permute-start(bf16[384,1280]{1,0:T(8,128)(2,1)} %stack_pieces.6.refs_1_), channel_id=1, source_target_pairs={{0,24},{8,16},{16,8},{24,0},{1,25},{9,17},{17,9},{25,1},{2,26},{10... | collective-permute-start | bytes 2949128 | tf_op jit(solution)/shard_map/ppermute | solution.py:727
  61.2 17.4 %collective-permute-start.10 = (bf16[4,160,640]{2,1,0:T(8,128)(2,1)}, bf16[4,160,640]{2,1,0:T(8,128)(2,1)S(1)}, u32[]{:S(2)}, u32[]{:S(2)}) collective-permute-start(bf16[4,160,640]{2,1,0:T(8,128)(2,1)} %select_bitcast_fusion), channel_id=1, source_target_pairs={{0,1},{1,0},{2,3},{3,2},{4,5},{5,4},{6,7},{7,6},{8,9},{9,8},{10,11... | collective-permute-start | bytes 2457608 | tf_op jit(solution)/shard_map/ppermute | solution.py:722
  61.3 17.4 %collective-permute-start.13 = (bf16[128,1280]{1,0:T(8,128)(2,1)}, bf16[128,1280]{1,0:T(8,128)(2,1)S(1)}, u32[]{:S(2)}, u32[]{:S(2)}) collective-permute-start(bf16[128,1280]{1,0:T(8,128)(2,1)} %refs_1_.3), channel_id=1, source_target_pairs={{0,6},{1,7},{2,4},{3,5},{4,2},{5,3},{6,0},{7,1},{8,14},{9,15},{10,... | collective-permute-start | bytes 983048 | tf_op jit(solution)/shard_map/ppermute | solution.py:718
  101.9 69.2 %collective-permute-start.20 = (bf16[384,1280]{1,0:T(8,128)(2,1)S(1)}, bf16[384,1280]{1,0:T(8,128)(2,1)}, u32[]{:S(2)}, u32[]{:S(2)}) collective-permute-start(bf16[384,1280]{1,0:T(8,128)(2,1)S(1)} %copy-done.4), channel_id=1, source_target_pairs={{0,8},{8,0},{16,24},{24,16},{1,9},{9,1},{17,25},{25,17},{2,10},{10... | collective-permute-start | bytes 2949128 | tf_op jit(solution)/shard_map/ppermute | solution.py:727
  103.5 67.7 %collective-permute-start.21 = (bf16[384,1280]{1,0:T(8,128)(2,1)S(1)}, bf16[384,1280]{1,0:T(8,128)(2,1)}, u32[]{:S(2)}, u32[]{:S(2)}) collective-permute-start(bf16[384,1280]{1,0:T(8,128)(2,1)S(1)} %copy-done.4), channel_id=1, source_target_pairs={{0,16},{8,24},{16,0},{24,8},{1,17},{9,25},{17,1},{25,9},{2,18},{10... | collective-permute-start | bytes 2949128 | tf_op jit(solution)/shard_map/ppermute | solution.py:727
  104.0 67.2 %collective-permute-start.22 = (bf16[384,1280]{1,0:T(8,128)(2,1)S(1)}, bf16[384,1280]{1,0:T(8,128)(2,1)}, u32[]{:S(2)}, u32[]{:S(2)}) collective-permute-start(bf16[384,1280]{1,0:T(8,128)(2,1)S(1)} %copy-done.4), channel_id=1, source_target_pairs={{0,24},{8,16},{16,8},{24,0},{1,25},{9,17},{17,9},{25,1},{2,26},{10... | collective-permute-start | bytes 2949128 | tf_op jit(solution)/shard_map/ppermute | solution.py:727
  109.0 30.1 %collective-permute-start.16 = (bf16[1,2,160,640]{3,2,1,0:T(8,128)(2,1)S(1)}, bf16[1,2,160,640]{3,2,1,0:T(8,128)(2,1)S(1)}, u32[]{:S(2)}, u32[]{:S(2)}) collective-permute-start(bf16[1,2,160,640]{3,2,1,0:T(8,128)(2,1)S(1)} %get-tuple-element.144), channel_id=1, source_target_pairs={{0,4},{1,5},{2,6},{3,7},{4,0},{5,1},{6,2},{7,3},{8,12},{9,13},{10,... | collective-permute-start | bytes 1228808 | tf_op jit(solution)/shard_map/ppermute | solution.py:747
  123.2 24.0 %collective-permute-start.17 = (bf16[1,2,160,640]{3,2,1,0:T(8,128)(2,1)}, bf16[1,2,160,640]{3,2,1,0:T(8,128)(2,1)S(1)}, u32[]{:S(2)}, u32[]{:S(2)}) collective-permute-start(bf16[1,2,160,640]{3,2,1,0:T(8,128)(2,1)} %after.11), channel_id=1, source_target_pairs={{0,6},{1,7},{2,4},{3,5},{4,2},{5,3},{6,0},{7,1},{8,14},{9,15},{10,... | collective-permute-start | bytes 1228808 | tf_op jit(solution)/shard_map/ppermute | solution.py:747
  175.9 28.3 %collective-permute-start.29 = (bf16[384,5120]{1,0:T(8,128)(2,1)}, bf16[384,5120]{1,0:T(8,128)(2,1)S(1)}, u32[]{:S(2)}, u32[]{:S(2)}) collective-permute-start(bf16[384,5120]{1,0:T(8,128)(2,1)} %join_plane.5.refs_0_.refs_4_), channel_id=1, source_target_pairs={{0,1},{1,0},{2,3},{3,2},{4,5},{5,4},{6,7},{7,6},{8,9},{9,8},{10,11... | collective-permute-start | bytes 11796488 | tf_op jit(solution)/shard_map/ppermute | solution.py:722
  200.7 28.1 %collective-permute-start.26 = (bf16[256,1280]{1,0:T(8,128)(2,1)}, bf16[256,1280]{1,0:T(8,128)(2,1)}, u32[]{:S(2)}, u32[]{:S(2)}) collective-permute-start(bf16[256,1280]{1,0:T(8,128)(2,1)} %get-tuple-element.110.refs_8_), channel_id=1, source_target_pairs={{0,8},{8,0},{16,24},{24,16},{1,9},{9,1},{17,25},{25,17},{2,10},{10... | collective-permute-start | bytes 1966088 | tf_op jit(solution)/shard_map/ppermute | solution.py:727
  202.2 31.2 %collective-permute-start.27 = (bf16[256,1280]{1,0:T(8,128)(2,1)}, bf16[256,1280]{1,0:T(8,128)(2,1)}, u32[]{:S(2)}, u32[]{:S(2)}) collective-permute-start(bf16[256,1280]{1,0:T(8,128)(2,1)} %get-tuple-element.111), channel_id=1, source_target_pairs={{0,16},{8,24},{16,0},{24,8},{1,17},{9,25},{17,1},{25,9},{2,18},{10... | collective-permute-start | bytes 1966088 | tf_op jit(solution)/shard_map/ppermute | solution.py:727
  202.6 30.8 %collective-permute-start.28 = (bf16[256,1280]{1,0:T(8,128)(2,1)}, bf16[256,1280]{1,0:T(8,128)(2,1)}, u32[]{:S(2)}, u32[]{:S(2)}) collective-permute-start(bf16[256,1280]{1,0:T(8,128)(2,1)} %get-tuple-element.112), channel_id=1, source_target_pairs={{0,24},{8,16},{16,8},{24,0},{1,25},{9,17},{17,9},{25,1},{2,26},{10... | collective-permute-start | bytes 1966088 | tf_op jit(solution)/shard_map/ppermute | solution.py:727
  227.2 41.4 %collective-permute-start.23 = (bf16[256,1280]{1,0:T(8,128)(2,1)}, bf16[256,1280]{1,0:T(8,128)(2,1)S(1)}, u32[]{:S(2)}, u32[]{:S(2)}) collective-permute-start(bf16[256,1280]{1,0:T(8,128)(2,1)} %get-tuple-element.106.refs_9_), channel_id=1, source_target_pairs={{0,8},{8,0},{16,24},{24,16},{1,9},{9,1},{17,25},{25,17},{2,10},{10... | collective-permute-start | bytes 1966088 | tf_op jit(solution)/shard_map/ppermute | solution.py:727
  228.7 39.9 %collective-permute-start.24 = (bf16[256,1280]{1,0:T(8,128)(2,1)}, bf16[256,1280]{1,0:T(8,128)(2,1)S(1)}, u32[]{:S(2)}, u32[]{:S(2)}) collective-permute-start(bf16[256,1280]{1,0:T(8,128)(2,1)} %get-tuple-element.107), channel_id=1, source_target_pairs={{0,16},{8,24},{16,0},{24,8},{1,17},{9,25},{17,1},{25,9},{2,18},{10... | collective-permute-start | bytes 1966088 | tf_op jit(solution)/shard_map/ppermute | solution.py:727
  233.4 35.2 %collective-permute-start.25 = (bf16[256,1280]{1,0:T(8,128)(2,1)}, bf16[256,1280]{1,0:T(8,128)(2,1)S(1)}, u32[]{:S(2)}, u32[]{:S(2)}) collective-permute-start(bf16[256,1280]{1,0:T(8,128)(2,1)} %get-tuple-element.108), channel_id=1, source_target_pairs={{0,24},{8,16},{16,8},{24,0},{1,25},{9,17},{17,9},{25,1},{2,26},{10... | collective-permute-start | bytes 1966088 | tf_op jit(solution)/shard_map/ppermute | solution.py:727
  271.7 23.2 %collective-permute-start.35 = (bf16[128,1280]{1,0:T(8,128)(2,1)S(1)}, bf16[128,1280]{1,0:T(8,128)(2,1)S(1)}, u32[]{:S(2)}, u32[]{:S(2)}) collective-permute-start(bf16[128,1280]{1,0:T(8,128)(2,1)S(1)} %add_convert_fusion.1), channel_id=1, source_target_pairs={{0,6},{1,7},{2,4},{3,5},{4,2},{5,3},{6,0},{7,1},{8,14},{9,15},{10,... | collective-permute-start | bytes 983048 | tf_op jit(solution)/shard_map/ppermute | solution.py:868
  272.9 27.7 %collective-permute-start.36 = (bf16[1,2,144,640]{3,2,1,0:T(8,128)(2,1)}, bf16[1,2,144,640]{3,2,1,0:T(8,128)(2,1)S(1)}, u32[]{:S(2)}, u32[]{:S(2)}) collective-permute-start(bf16[1,2,144,640]{3,2,1,0:T(8,128)(2,1)} %get-tuple-element.131), channel_id=1, source_target_pairs={{0,6},{1,7},{2,4},{3,5},{4,2},{5,3},{6,0},{7,1},{8,14},{9,15},{10,... | collective-permute-start | bytes 1105928 | tf_op jit(solution)/shard_map/ppermute | solution.py:747
  (47 other events, 402.4 us)

commit v2 on v1

--- a/solution.py
+++ b/solution.py
@@ -215,18 +215,23 @@
 
 def join_plane(column, *pieces, earlier=()):
     rows, quarter = pieces[0].shape
-    count = len(pieces)
+    count, halves = 4, len(pieces) - 3
     chunk = rows // 4
-
-    def body(*refs):
-        column_ref, sources, out = refs[0], refs[1 : 1 + count], refs[-1]
+    per = 4 // halves
+
+    def body(column_ref, *refs):
+        out = refs[-1]
         for own_column in range(count):
-
-            @pl.when(column_ref[0] == own_column)
-            def _():
-                for bit, source in enumerate(sources):
-                    place = own_column ^ bit
-                    out[:, place * quarter : (place + 1) * quarter] = source[...]
+            for j, from_diagonal in enumerate(refs[3 : 3 + halves]):
+
+                @pl.when((column_ref[0] == own_column) & (pl.program_id(0) // per == j))
+                def _(from_diagonal=from_diagonal, own_column=own_column):
+                    for bit, source in enumerate(refs[:3] + (from_diagonal,)):
+                        place = own_column ^ bit
+                        out[:, place * quarter : (place + 1) * quarter] = source[...]
+
+    def diagonal_spec(j):
+        return pl.BlockSpec((chunk, quarter), lambda i, *_: (jnp.clip(i - j * per, 0, per - 1), 0))
 
     return pl.pallas_call(
         body,
@@ -234,7 +239,9 @@
         grid_spec=pltpu.PrefetchScalarGridSpec(
             num_scalar_prefetch=1,
             grid=(4,),
-            in_specs=[pl.BlockSpec((chunk, quarter), lambda i, *_: (i, 0))] * count + [ANY] * len(earlier),
+            in_specs=[pl.BlockSpec((chunk, quarter), lambda i, *_: (i, 0))] * 3
+            + [diagonal_spec(j) for j in range(halves)]
+            + [ANY] * len(earlier),
             out_specs=pl.BlockSpec((chunk, count * quarter), lambda i, *_: (i, 0)),
         ),
         compiler_params=pltpu.CompilerParams(vmem_limit_bytes=VMEM_LIMIT),
@@ -725,6 +732,12 @@
 def send_plane(*pieces):
     pieces = pieces * 3 if len(pieces) == 1 else pieces
     return [lax.ppermute(p, "tp", swap_pairs(lax.axis_size("tp"), bit)) for p, bit in zip(pieces, (1, 2, 3))]
+
+
+def send_diagonal(from_x, from_y):
+    along, across = [swap_pairs(lax.axis_size("tp"), bit) for bit in (1, 2)]
+    half = from_x.shape[0] // 2
+    return [lax.ppermute(from_x[:half], "tp", across), lax.ppermute(from_y[half:], "tp", along)]
 
 
 def exchange_cores(blocks, cuts=1):
@@ -792,15 +805,18 @@
     x_z = send_along_z(tokens)
     near = stack_pieces([tokens, cotangent])
     near_x, near_y = send_plane(near, near)
-    near_late = stack_pieces([tokens, cotangent], earlier=[x_z[0]])
-    near_d = lax.ppermute(near_late, "tp", swap_pairs(tp_count, 3))
+    near_x, near_y = after([near_x, near_y], x_z[0])
+    near_d = send_diagonal(near_x, near_y)
     w_both = jnp.concatenate([w_gate[0], w_up[0]], axis=1)
-    near_x, near_y, near_d, *x_z = after([near_x, near_y, near_d, *x_z], w_both, shadow_blocks)
+    fenced = after([*near_d, *x_z], w_both, shadow_blocks)
+    near_d, x_z = fenced[:2], fenced[2:]
 
     x_piece = stack_pieces(x_z)
-    x_plane = send_plane(x_piece)
+    x_plane = send_plane(x_piece, x_piece)
     dy_z = send_along_z(cotangent)
-    near_own = join_plane(tp_index, near, near_x, near_y, near_d)
+    x_plane = after(x_plane, *dy_z[:2])
+    x_plane = [*x_plane, *send_diagonal(*x_plane)]
+    near_own = join_plane(tp_index, near, near_x, near_y, *near_d)
     near_other = swap_cores(near_own)
     x_near = [(near_own, 0, tok_count), (near_other, 0, tok_count)]
     hidden_near, slope_near, act_near = forward_rows(x_near, w_both, 2 * tile)
@@ -808,8 +824,8 @@
     down = jnp.pad(w_down[0], ((0, spare_rows), (0, 0)))
     (shadow_blocks,) = after([shadow_blocks], x_z[0])
     shadow_kept, shadow_taken = exchange_cores(shadow_blocks)
-    fenced = after([*x_plane, down, *shadow_taken, *dy_z], hidden_near)
-    x_plane, down, shadow_taken, dy_z = fenced[:3], fenced[3], fenced[4:5], fenced[5:]
+    fenced = after([*x_plane[2:], down, *shadow_taken, *dy_z], hidden_near)
+    x_plane[2:], down, shadow_taken, dy_z = fenced[:2], fenced[2], fenced[3:4], fenced[4:]
 
     dy_piece = stack_pieces(dy_z)
     dy_plane = send_plane(dy_piece)

time: 307 us -> 301 us (0.980)
  waiting for transfers between devices: 102 us -> 84.5 us
  local copies, waits for them, and re-layouts: 14.9 us -> 23.7 us
  starting transfers between devices: 34.3 us -> 39.6 us
    ppermute x14 -> x13, waiting for transfers between devices: 19.7 us -> 7.94 us  [send_plane(): lax.ppermute(p, 'tp', swap_pairs(lax.axis_size('tp'), bit))]
    slice x0 -> x4, local copies, waits for them, and re-layouts: none -> 6.39 us  [the longest x2 3.56 us: send_diagonal(): from_y[half:]]
    ppermute x14 -> x13, starting transfers between devices: 13.5 us -> 19 us  [send_plane(): lax.ppermute(p, 'tp', swap_pairs(lax.axis_size('tp'), bit))]
    ppermute x1 -> x4, starting transfers between devices: 0.48 us -> 4.65 us  [the longest x2 2.63 us: send_diagonal(): lax.ppermute(from_y[half:], 'tp', along)]
    unnamed x68 -> x70, local copies, waits for them, and re-layouts: 7.22 us -> 10.6 us
    pallas_call x4 -> x3, Pallas kernels: 9.28 us -> 7.32 us  [stack_pieces(): pl.pallas_call(body, out_shape=shape_of(count * rows, columns), grid=(cou...]
  transfers between devices with their start and end apart: 37 -> 39, of which waited for: 16 -> 17; matrix products, arithmetic and copies ran while one was open for 10% -> 12% of each run, Pallas kernels for 35% -> 35%
where the time goes in v2:
time: 301 us; the launch traced here: 300 us
  Pallas kernels  127 us (42%)
  waiting for transfers between devices  84.5 us (28%)
  starting transfers between devices  39.6 us (13%)
  other arithmetic  23.8 us (8%)
  local copies, waits for them, and re-layouts  23.7 us (8%)
    pallas_call x10, Pallas kernels, kernel_call(): pl.pallas_call(run, out_shape=out_shape, grid_spec=pltpu.PrefetchScalarGr...  94.1 us
    ppermute x6, waiting for transfers between devices, send_piece(): return lax.ppermute(piece, 'ep', swap_pairs(lax.axis_size('ep'), 2 * shift))  26.9 us
    ppermute x6, waiting for transfers between devices, send_along_z(): lax.ppermute(own, 'ep', swap_pairs(ep_count, 2 * s))  22.4 us
    ppermute x3, waiting for transfers between devices, send_rows(): return lax.ppermute(piece, 'ep', swap_pairs(ep_count, 2 * (i + 1)))  20.8 us
    ppermute x13, starting transfers between devices, send_plane(): lax.ppermute(p, 'tp', swap_pairs(lax.axis_size('tp'), bit))  19 us
    pallas_call x3, Pallas kernels, join_plane(): pl.pallas_call(body, out_shape=shape_of(rows, count * quarter), grid_spec...  14 us
    unnamed x70, local copies, waits for them, and re-layouts  10.6 us
    ppermute x13, waiting for transfers between devices, send_plane(): lax.ppermute(p, 'tp', swap_pairs(lax.axis_size('tp'), bit))  7.94 us
  transfers between devices with their start and end apart: 39, of which 17 were waited for; matrix products, arithmetic and copies ran while one was open for 12% of the time, Pallas kernels for 35%

profile of v2, /device:TPU:16, one launch (start us, length us, event | category | flops | bytes accessed | tf_op | source)
XLA Modules:
  0.0 299.8 jit_solution(4605011362483361566)
XLA Ops:
  9.1 7.1 %pad_maximum_fusion.refs_5_.refs_2_ = bf16[5120,768]{1,0:T(8,128)(2,1)} fusion(bf16[5120,384]{1,0:T(8,128)(2,1)} %bitcast.98, bf16[5120,384]{1,0:T(8,128)(2,1)} %bitcast.99), kind=kLoop, calls=%fused_computation | loop fusion | flops 15728640 | bytes 15728640 | tf_op jit(solution)/shard_map/concatenate | solution.py:810
  30.7 6.3 %collective-permute-done.6.refs_4_ = bf16[128,1280]{1,0:T(8,128)(2,1)S(1)} collective-permute-done((bf16[128,1280]{1,0:T(8,128)(2,1)}, bf16[128,1280]{1,0:T(8,128)(2,1)S(1)}, u32[]{:S(2)}, u32[]{:S(2)}) %collective-permute-start.6) | collective-permute-done | bytes 327712 | tf_op jit(solution)/shard_map/ppermute | solution.py:725
  38.6 4.3 %join_plane.3.refs_0_.refs_1_.refs_5_ = bf16[256,5120]{1,0:T(8,128)(2,1)} custom-call(s32[1]{0:T(128)} %bitcast.column_ref, bf16[256,1280]{1,0:T(8,128)(2,1)} %stack_pieces.3.refs_0_, bf16[256,1280]{1,0:T(8,128)(2,1)} %get-tuple-element.73.refs_1_, bf16[256,1280]{1,0:T(8,128)(2,1)} %get-tuple-element.74.refs_2_, ...), custom_call_target="tpu_custom_call" | custom-call | flops 1 | bytes 1 | tf_op jit(solution)/shard_map/join_plane/pallas_call | solution.py:236
  50.7 9.2 %collective-permute-done.10.refs_2_.refs_4_ = bf16[128,1280]{1,0:T(8,128)(2,1)} collective-permute-done((bf16[128,1280]{1,0:T(8,128)(2,1)}, bf16[128,1280]{1,0:T(8,128)(2,1)}, u32[]{:S(2)}, u32[]{:S(2)}) %collective-permute-start.10) | collective-permute-done | bytes 327712 | tf_op jit(solution)/shard_map/ppermute | solution.py:725
  63.3 6.6 %collective-permute-done.8.refs_0_ = bf16[384,1280]{1,0:T(8,128)(2,1)} collective-permute-done((bf16[384,1280]{1,0:T(8,128)(2,1)}, bf16[384,1280]{1,0:T(8,128)(2,1)}, u32[]{:S(2)}, u32[]{:S(2)}) %collective-permute-start.8) | collective-permute-done | bytes 983072 | tf_op jit(solution)/shard_map/ppermute | solution.py:734
  76.3 5.2 %pad.9.refs_2_ = bf16[512,5120]{1,0:T(8,128)(2,1)} pad(bf16[384,5120]{1,0:T(8,128)(2,1)} %bitcast.96, bf16[]{:T(256)} %constant.71.clone.1), padding=0_128x0_0 | pad | bytes 9175042 | tf_op jit(solution)/shard_map/jit(_pad)/pad | solution.py:824
  83.0 7.0 %forward_rows.3 = (bf16[256,384]{1,0:T(8,128)(2,1)}, bf16[256,384]{1,0:T(8,128)(2,1)}, bf16[256,384]{1,0:T(8,128)(2,1)}) custom-call(s32[1]{0:T(128)} %constant.69.clone.1.column_ref, bf16[256,5120]{1,0:T(8,128)(2,1)} %join_plane.3.refs_0_.refs_1_.refs_5_, bf16[256,5120]{1,0:T(8,128)(2,1)} %copy-done, bf16[5120,768]{1,0:T(8,128)(2,1)} %pad_maximum_fusion.refs_5_.refs_2_), custom_call_target="tpu_custom_call" | custom-call | flops 1 | bytes 1 | tf_op jit(solution)/shard_map/forward_rows/pallas_call | solution.py:196
  94.0 5.1 %join_plane.4.refs_0_ = bf16[384,5120]{1,0:T(8,128)(2,1)} custom-call(s32[1]{0:T(128)} %bitcast.column_ref, bf16[384,1280]{1,0:T(8,128)(2,1)} %stack_pieces.4.refs_0_, bf16[384,1280]{1,0:T(8,128)(2,1)} %get-tuple-element.81.refs_1_, bf16[384,1280]{1,0:T(8,128)(2,1)} %get-tuple-element.82.refs_2_, bf16[192,1280]{1,0:T(8,128)(2,1)} %get-tuple-element.83.refs_3_, ...), custom_call_target="tpu_custom_call" | custom-call | flops 1 | bytes 1 | tf_op jit(solution)/shard_map/join_plane/pallas_call | solution.py:236
  106.7 11.5 %forward_rows.4 = (bf16[768,384]{1,0:T(8,128)(2,1)}, bf16[768,384]{1,0:T(8,128)(2,1)}, bf16[768,384]{1,0:T(8,128)(2,1)}) custom-call(s32[1]{0:T(128)} %constant.69.clone.1.column_ref, bf16[384,5120]{1,0:T(8,128)(2,1)} %join_plane.4.refs_0_, bf16[384,5120]{1,0:T(8,128)(2,1)} %collective-permute-done.16.refs_1_.refs_3_, ...), custom_call_target="tpu_custom_call" | custom-call | flops 1 | bytes 1 | tf_op jit(solution)/shard_map/forward_rows/pallas_call | solution.py:196
  121.2 12.9 %collective-permute-done.18.refs_2_.refs_5_ = bf16[1,2,160,640]{3,2,1,0:T(8,128)(2,1)S(1)} collective-permute-done((bf16[1,2,160,640]{3,2,1,0:T(8,128)(2,1)S(1)}, bf16[1,2,160,640]{3,2,1,0:T(8,128)(2,1)S(1)}, u32[]{:S(2)}, u32[]{:S(2)}) %collective-permute-start.18) | collective-permute-done | bytes 409632 | tf_op jit(solution)/shard_map/ppermute | solution.py:760
  134.1 9.5 %collective-permute-done.19.refs_3_.refs_6_ = bf16[1,2,160,640]{3,2,1,0:T(8,128)(2,1)S(1)} collective-permute-done((bf16[1,2,160,640]{3,2,1,0:T(8,128)(2,1)}, bf16[1,2,160,640]{3,2,1,0:T(8,128)(2,1)S(1)}, u32[]{:S(2)}, u32[]{:S(2)}) %collective-permute-start.19) | collective-permute-done | bytes 409632 | tf_op jit(solution)/shard_map/ppermute | solution.py:760
  144.4 5.0 %lay_out_shadow.1 = (bf16[256,5120]{1,0:T(8,128)(2,1)}, bf16[512,5120]{1,0:T(8,128)(2,1)}) custom-call(s32[1]{0:T(128)} %bitcast.14.chip_ref, bf16[1,2,160,640]{3,2,1,0:T(8,128)(2,1)} %get-tuple-element.146.refs_0_.refs_3_, bf16[1,2,160,640]{3,2,1,0:T(8,128)(2,1)} %copy-done.14, ...), custom_call_target="tpu_custom_call", output_to_operand_aliasing={{1}: (5, {})} | custom-call | flops 1 | bytes 1 | tf_op jit(solution)/shard_map/lay_out_shadow/pallas_call | solution.py:306
  149.3 8.0 %forward_rows.5 = (bf16[1024,128]{1,0:T(8,128)(2,1)}, bf16[1024,128]{1,0:T(8,128)(2,1)}, bf16[1024,128]{1,0:T(8,128)(2,1)}) custom-call(s32[1]{0:T(128)} %constant.69.clone.1.column_ref, bf16[384,5120]{1,0:T(8,128)(2,1)} %join_plane.4.refs_0_, bf16[256,5120]{1,0:T(8,128)(2,1)} %join_plane.3.refs_0_.refs_1_.refs_5_, bf16[256,5120]{1,0:T(8,128)(2,1)} %copy-done, ...), custom_call_target="tpu_custom_call" | custom-call | flops 1 | bytes 1 | tf_op jit(solution)/shard_map/forward_rows/pallas_call | solution.py:196
  160.7 6.9 %output_other.1 = (bf16[256,5120]{1,0:T(8,128)(2,1)}, bf16[256,5120]{1,0:T(8,128)(2,1)}) custom-call(s32[1]{0:T(128)} %bitcast.column_ref, bf16[1024,512]{1,0:T(8,128)(2,1)} %get-tuple-element.93.refs_0_.refs_10_.refs_4_, bf16[512,5120]{1,0:T(8,128)(2,1)} %get-tuple-element.94.refs_1_.refs_3_), custom_call_target="tpu_custom_call" | custom-call | flops 1 | bytes 1 | tf_op jit(solution)/shard_map/output_other/pallas_call | solution.py:196
  167.6 4.7 %join_plane.5.refs_0_.refs_4_ = bf16[384,5120]{1,0:T(8,128)(2,1)} custom-call(s32[1]{0:T(128)} %bitcast.column_ref, bf16[384,1280]{1,0:T(8,128)(2,1)} %stack_pieces.5.refs_5_.refs_0_, bf16[384,1280]{1,0:T(8,128)(2,1)} %get-tuple-element.97.refs_1_, bf16[384,1280]{1,0:T(8,128)(2,1)} %get-tuple-element.98.refs_2_, bf16[384,1280]{1,0:T(8,128)(2,1)} %get-tuple-element.99.refs_3_), custom_call_target="tpu_custom_call" | custom-call | flops 1 | bytes 1 | tf_op jit(solution)/shard_map/join_plane/pallas_call | solution.py:236
  172.8 9.9 %backward_rows.2 = (bf16[640,768]{1,0:T(8,128)(2,1)}, bf16[640,256]{1,0:T(8,128)(2,1)}) custom-call(s32[1]{0:T(128)} %constant.69.clone.1.column_ref, bf16[384,5120]{1,0:T(8,128)(2,1)} %join_plane.5.refs_0_.refs_4_, bf16[256,5120]{1,0:T(8,128)(2,1)} %join_plane.3.refs_0_.refs_1_.refs_5_, bf16[256,5120]{1,0:T(8,128)(2,1)} %copy-done, ...), custom_call_target="tpu_custom_call" | custom-call | flops 1 | bytes 1 | tf_op jit(solution)/shard_map/backward_rows/pallas_call | solution.py:196
  182.8 4.1 %collective-permute-done.21.refs_3_ = bf16[256,5120]{1,0:T(8,128)(2,1)} collective-permute-done((bf16[256,5120]{1,0:T(8,128)(2,1)}, bf16[256,5120]{1,0:T(8,128)(2,1)}, u32[]{:S(2)}, u32[]{:S(2)}) %collective-permute-start.21) | collective-permute-done | bytes 2621472 | tf_op jit(solution)/shard_map/ppermute | solution.py:729
  186.9 10.1 %output_own.1 = (f32[256,1280]{1,0:T(8,128)}, bf16[256,1280]{1,0:T(8,128)(2,1)}, bf16[256,1280]{1,0:T(8,128)(2,1)}, bf16[256,1280]{1,0:T(8,128)(2,1)}, f32[256,1...) custom-call(s32[1]{0:T(128)} %bitcast.column_ref, ...), custom_call_target="tpu_custom_call" | custom-call | flops 1 | bytes 1 | tf_op jit(solution)/shard_map/output_own/pallas_call | solution.py:196
  202.4 7.7 %backward_rows.3 = (bf16[384,768]{1,0:T(8,128)(2,1)}, bf16[384,256]{1,0:T(8,128)(2,1)}) custom-call(s32[1]{0:T(128)} %constant.69.clone.1.column_ref, bf16[384,5120]{1,0:T(8,128)(2,1)} %copy-done.2, bf16[512,5120]{1,0:T(8,128)(2,1)} %get-tuple-element.94.refs_1_.refs_3_, bf16[768,384]{1,0:T(8,128)(2,1)} %get-tuple-element.100.refs_4_.refs_2_, ...), custom_call_target="tpu_custom_call" | custom-call | flops 1 | bytes 1 | tf_op jit(solution)/shard_map/backward_rows/pallas_call | solution.py:196
  210.1 11.1 %shadow_grads.1.refs_3_ = bf16[8,144,640]{2,1,0:T(8,128)(2,1)} custom-call(s32[1]{0:T(128)} %constant.69.clone.1.column_ref, bf16[384,5120]{1,0:T(8,128)(2,1)} %join_plane.4.refs_0_, bf16[256,5120]{1,0:T(8,128)(2,1)} %join_plane.3.refs_0_.refs_1_.refs_5_, bf16[256,5120]{1,0:T(8,128)(2,1)} %copy-done, ...), custom_call_target="tpu_custom_call" | custom-call | flops 1 | bytes 1 | tf_op jit(solution)/shard_map/shadow_grads/pallas_call | solution.py:196
  225.6 6.0 %collective-permute-start.27 = (bf16[256,1280]{1,0:T(8,128)(2,1)}, bf16[256,1280]{1,0:T(8,128)(2,1)S(1)}, u32[]{:S(2)}, u32[]{:S(2)}) collective-permute-start(bf16[256,1280]{1,0:T(8,128)(2,1)} %get-tuple-element.112), channel_id=1, source_target_pairs={{0,24},{8,16},{16,8},{24,0},{1,25},{9,17},{17,9},{25,1},{2,26},{10... | collective-permute-start | bytes 1966088 | tf_op jit(solution)/shard_map/ppermute | solution.py:734
  237.8 9.1 %down_grad.1.refs_5_ = bf16[384,5120]{1,0:T(8,128)(2,1)} custom-call(s32[1]{0:T(128)} %constant.69.clone.1.column_ref, bf16[384,5120]{1,0:T(8,128)(2,1)} %join_plane.5.refs_0_.refs_4_, bf16[256,5120]{1,0:T(8,128)(2,1)} %join_plane.3.refs_0_.refs_1_.refs_5_, bf16[256,5120]{1,0:T(8,128)(2,1)} %copy-done, bf16[384,5120]{1,0:T(8,128)(2,1)} %copy-done.2, ...), custom_call_target="tpu_custom_call" | custom-call | flops 1 | bytes 1 | tf_op jit(solution)/shard_map/down_grad/pallas_call | solution.py:196
  251.8 12.9 %input_grads.1 = (bf16[5120,384]{1,0:T(8,128)(2,1)}, bf16[5120,384]{1,0:T(8,128)(2,1)}) custom-call(s32[1]{0:T(128)} %constant.69.clone.1.column_ref, bf16[384,5120]{1,0:T(8,128)(2,1)} %join_plane.4.refs_0_, bf16[256,5120]{1,0:T(8,128)(2,1)} %join_plane.3.refs_0_.refs_1_.refs_5_, bf16[256,5120]{1,0:T(8,128)(2,1)} %copy-done, ...), custom_call_target="tpu_custom_call" | custom-call | flops 1 | bytes 1 | tf_op jit(solution)/shard_map/input_grads/pallas_call | solution.py:196
  269.9 20.7 %collective-permute-done.37 = bf16[128,1280]{1,0:T(8,128)(2,1)S(1)} collective-permute-done((bf16[128,1280]{1,0:T(8,128)(2,1)S(1)}, bf16[128,1280]{1,0:T(8,128)(2,1)S(1)}, u32[]{:S(2)}, u32[]{:S(2)}) %collective-permute-start.37) | collective-permute-done | bytes 327712 | tf_op jit(solution)/shard_map/ppermute | solution.py:884
  (178 shorter events, 98.1 us)
Async XLA Ops:
  2.6 16.8 %collective-permute-start = (bf16[256,1280]{1,0:T(8,128)(2,1)}, bf16[256,1280]{1,0:T(8,128)(2,1)S(1)}, u32[]{:S(2)}, u32[]{:S(2)}) collective-permute-start(bf16[256,1280]{1,0:T(8,128)(2,1)} %stack_pieces.3.refs_0_), channel_id=1, source_target_pairs={{0,8},{8,0},{16,24},{24,16},{1,9},{9,1},{17,25},{25,17},{2,10},{10... | collective-permute-start | bytes 1966088 | tf_op jit(solution)/shard_map/ppermute | solution.py:734
  7.2 23.5 %collective-permute-start.5 = (bf16[128,1280]{1,0:T(8,128)(2,1)}, bf16[128,1280]{1,0:T(8,128)(2,1)S(1)}, u32[]{:S(2)}, u32[]{:S(2)}) collective-permute-start(bf16[128,1280]{1,0:T(8,128)(2,1)} %refs_0_.1), channel_id=1, source_target_pairs={{0,4},{1,5},{2,6},{3,7},{4,0},{5,1},{6,2},{7,3},{8,12},{9,13},{10,... | collective-permute-start | bytes 983048 | tf_op jit(solution)/shard_map/ppermute | solution.py:725
  7.5 29.5 %collective-permute-start.6 = (bf16[128,1280]{1,0:T(8,128)(2,1)}, bf16[128,1280]{1,0:T(8,128)(2,1)S(1)}, u32[]{:S(2)}, u32[]{:S(2)}) collective-permute-start(bf16[128,1280]{1,0:T(8,128)(2,1)} %refs_0_.1), channel_id=1, source_target_pairs={{0,6},{1,7},{2,4},{3,5},{4,2},{5,3},{6,0},{7,1},{8,14},{9,15},{10,... | collective-permute-start | bytes 983048 | tf_op jit(solution)/shard_map/ppermute | solution.py:725
  42.8 38.6 %collective-permute-start.7 = (bf16[256,5120]{1,0:T(8,128)(2,1)}, bf16[256,5120]{1,0:T(8,128)(2,1)S(1)}, u32[]{:S(2)}, u32[]{:S(2)}) collective-permute-start(bf16[256,5120]{1,0:T(8,128)(2,1)} %join_plane.3.refs_0_.refs_1_.refs_5_), channel_id=1, source_target_pairs={{0,1},{1,0},{2,3},{3,2},{4,5},{5,4},{6,7},{7,6},{8,9},{9,8},{10,11... | collective-permute-start | bytes 7864328 | tf_op jit(solution)/shard_map/ppermute | solution.py:729
  45.5 24.5 %collective-permute-start.8 = (bf16[384,1280]{1,0:T(8,128)(2,1)}, bf16[384,1280]{1,0:T(8,128)(2,1)}, u32[]{:S(2)}, u32[]{:S(2)}) collective-permute-start(bf16[384,1280]{1,0:T(8,128)(2,1)} %stack_pieces.4.refs_0_), channel_id=1, source_target_pairs={{0,8},{8,0},{16,24},{24,16},{1,9},{9,1},{17,25},{25,17},{2,10},{10... | collective-permute-start | bytes 2949128 | tf_op jit(solution)/shard_map/ppermute | solution.py:734
  46.0 24.2 %collective-permute-start.9 = (bf16[384,1280]{1,0:T(8,128)(2,1)}, bf16[384,1280]{1,0:T(8,128)(2,1)}, u32[]{:S(2)}, u32[]{:S(2)}) collective-permute-start(bf16[384,1280]{1,0:T(8,128)(2,1)} %stack_pieces.4.refs_0_), channel_id=1, source_target_pairs={{0,16},{8,24},{16,0},{24,8},{1,17},{9,25},{17,1},{25,9},{2,18},{10... | collective-permute-start | bytes 2949128 | tf_op jit(solution)/shard_map/ppermute | solution.py:734
  46.4 16.9 %collective-permute-start.11 = (bf16[128,1280]{1,0:T(8,128)(2,1)}, bf16[128,1280]{1,0:T(8,128)(2,1)}, u32[]{:S(2)}, u32[]{:S(2)}) collective-permute-start(bf16[128,1280]{1,0:T(8,128)(2,1)} %refs_1_.1), channel_id=1, source_target_pairs={{0,4},{1,5},{2,6},{3,7},{4,0},{5,1},{6,2},{7,3},{8,12},{9,13},{10,... | collective-permute-start | bytes 983048 | tf_op jit(solution)/shard_map/ppermute | solution.py:725
  59.9 30.4 %collective-permute-start.14 = (bf16[4,160,640]{2,1,0:T(8,128)(2,1)}, bf16[4,160,640]{2,1,0:T(8,128)(2,1)S(1)}, u32[]{:S(2)}, u32[]{:S(2)}) collective-permute-start(bf16[4,160,640]{2,1,0:T(8,128)(2,1)} %select_bitcast_fusion), channel_id=1, source_target_pairs={{0,1},{1,0},{2,3},{3,2},{4,5},{5,4},{6,7},{7,6},{8,9},{9,8},{10,11... | collective-permute-start | bytes 2457608 | tf_op jit(solution)/shard_map/ppermute | solution.py:729
  72.0 18.3 %collective-permute-start.12 = (bf16[192,1280]{1,0:T(8,128)(2,1)}, bf16[192,1280]{1,0:T(8,128)(2,1)S(1)}, u32[]{:S(2)}, u32[]{:S(2)}) collective-permute-start(bf16[192,1280]{1,0:T(8,128)(2,1)} %slice.86), channel_id=1, source_target_pairs={{0,16},{8,24},{16,0},{24,8},{1,17},{9,25},{17,1},{25,9},{2,18},{10... | collective-permute-start | bytes 1474568 | tf_op jit(solution)/shard_map/ppermute | solution.py:740
  99.1 68.4 %collective-permute-start.22 = (bf16[384,1280]{1,0:T(8,128)(2,1)S(1)}, bf16[384,1280]{1,0:T(8,128)(2,1)}, u32[]{:S(2)}, u32[]{:S(2)}) collective-permute-start(bf16[384,1280]{1,0:T(8,128)(2,1)S(1)} %copy-done.4), channel_id=1, source_target_pairs={{0,8},{8,0},{16,24},{24,16},{1,9},{9,1},{17,25},{25,17},{2,10},{10... | collective-permute-start | bytes 2949128 | tf_op jit(solution)/shard_map/ppermute | solution.py:734
  99.8 67.8 %collective-permute-start.23 = (bf16[384,1280]{1,0:T(8,128)(2,1)S(1)}, bf16[384,1280]{1,0:T(8,128)(2,1)}, u32[]{:S(2)}, u32[]{:S(2)}) collective-permute-start(bf16[384,1280]{1,0:T(8,128)(2,1)S(1)} %copy-done.4), channel_id=1, source_target_pairs={{0,16},{8,24},{16,0},{24,8},{1,17},{9,25},{17,1},{25,9},{2,18},{10... | collective-permute-start | bytes 2949128 | tf_op jit(solution)/shard_map/ppermute | solution.py:734
  101.3 66.2 %collective-permute-start.24 = (bf16[384,1280]{1,0:T(8,128)(2,1)S(1)}, bf16[384,1280]{1,0:T(8,128)(2,1)}, u32[]{:S(2)}, u32[]{:S(2)}) collective-permute-start(bf16[384,1280]{1,0:T(8,128)(2,1)S(1)} %copy-done.4), channel_id=1, source_target_pairs={{0,24},{8,16},{16,8},{24,0},{1,25},{9,17},{17,9},{25,1},{2,26},{10... | collective-permute-start | bytes 2949128 | tf_op jit(solution)/shard_map/ppermute | solution.py:734
  106.2 27.9 %collective-permute-start.18 = (bf16[1,2,160,640]{3,2,1,0:T(8,128)(2,1)S(1)}, bf16[1,2,160,640]{3,2,1,0:T(8,128)(2,1)S(1)}, u32[]{:S(2)}, u32[]{:S(2)}) collective-permute-start(bf16[1,2,160,640]{3,2,1,0:T(8,128)(2,1)S(1)} %get-tuple-element.148), channel_id=1, source_target_pairs={{0,4},{1,5},{2,6},{3,7},{4,0},{5,1},{6,2},{7,3},{8,12},{9,13},{10,... | collective-permute-start | bytes 1228808 | tf_op jit(solution)/shard_map/ppermute | solution.py:760
  120.0 23.7 %collective-permute-start.19 = (bf16[1,2,160,640]{3,2,1,0:T(8,128)(2,1)}, bf16[1,2,160,640]{3,2,1,0:T(8,128)(2,1)S(1)}, u32[]{:S(2)}, u32[]{:S(2)}) collective-permute-start(bf16[1,2,160,640]{3,2,1,0:T(8,128)(2,1)} %after.15), channel_id=1, source_target_pairs={{0,6},{1,7},{2,4},{3,5},{4,2},{5,3},{6,0},{7,1},{8,14},{9,15},{10,... | collective-permute-start | bytes 1228808 | tf_op jit(solution)/shard_map/ppermute | solution.py:760
  172.3 28.2 %collective-permute-start.31 = (bf16[384,5120]{1,0:T(8,128)(2,1)}, bf16[384,5120]{1,0:T(8,128)(2,1)S(1)}, u32[]{:S(2)}, u32[]{:S(2)}) collective-permute-start(bf16[384,5120]{1,0:T(8,128)(2,1)} %join_plane.5.refs_0_.refs_4_), channel_id=1, source_target_pairs={{0,1},{1,0},{2,3},{3,2},{4,5},{5,4},{6,7},{7,6},{8,9},{9,8},{10,11... | collective-permute-start | bytes 11796488 | tf_op jit(solution)/shard_map/ppermute | solution.py:729
  197.0 27.0 %collective-permute-start.28 = (bf16[256,1280]{1,0:T(8,128)(2,1)}, bf16[256,1280]{1,0:T(8,128)(2,1)}, u32[]{:S(2)}, u32[]{:S(2)}) collective-permute-start(bf16[256,1280]{1,0:T(8,128)(2,1)} %get-tuple-element.114.refs_8_), channel_id=1, source_target_pairs={{0,8},{8,0},{16,24},{24,16},{1,9},{9,1},{17,25},{25,17},{2,10},{10... | collective-permute-start | bytes 1966088 | tf_op jit(solution)/shard_map/ppermute | solution.py:734
  197.5 28.1 %collective-permute-start.29 = (bf16[256,1280]{1,0:T(8,128)(2,1)}, bf16[256,1280]{1,0:T(8,128)(2,1)}, u32[]{:S(2)}, u32[]{:S(2)}) collective-permute-start(bf16[256,1280]{1,0:T(8,128)(2,1)} %get-tuple-element.115), channel_id=1, source_target_pairs={{0,16},{8,24},{16,0},{24,8},{1,17},{9,25},{17,1},{25,9},{2,18},{10... | collective-permute-start | bytes 1966088 | tf_op jit(solution)/shard_map/ppermute | solution.py:734
  199.0 32.6 %collective-permute-start.30 = (bf16[256,1280]{1,0:T(8,128)(2,1)}, bf16[256,1280]{1,0:T(8,128)(2,1)}, u32[]{:S(2)}, u32[]{:S(2)}) collective-permute-start(bf16[256,1280]{1,0:T(8,128)(2,1)} %get-tuple-element.116), channel_id=1, source_target_pairs={{0,24},{8,16},{16,8},{24,0},{1,25},{9,17},{17,9},{25,1},{2,26},{10... | collective-permute-start | bytes 1966088 | tf_op jit(solution)/shard_map/ppermute | solution.py:734
  223.6 41.1 %collective-permute-start.25 = (bf16[256,1280]{1,0:T(8,128)(2,1)}, bf16[256,1280]{1,0:T(8,128)(2,1)S(1)}, u32[]{:S(2)}, u32[]{:S(2)}) collective-permute-start(bf16[256,1280]{1,0:T(8,128)(2,1)} %get-tuple-element.110.refs_9_), channel_id=1, source_target_pairs={{0,8},{8,0},{16,24},{24,16},{1,9},{9,1},{17,25},{25,17},{2,10},{10... | collective-permute-start | bytes 1966088 | tf_op jit(solution)/shard_map/ppermute | solution.py:734
  224.0 40.6 %collective-permute-start.26 = (bf16[256,1280]{1,0:T(8,128)(2,1)}, bf16[256,1280]{1,0:T(8,128)(2,1)S(1)}, u32[]{:S(2)}, u32[]{:S(2)}) collective-permute-start(bf16[256,1280]{1,0:T(8,128)(2,1)} %get-tuple-element.111), channel_id=1, source_target_pairs={{0,16},{8,24},{16,0},{24,8},{1,17},{9,25},{17,1},{25,9},{2,18},{10... | collective-permute-start | bytes 1966088 | tf_op jit(solution)/shard_map/ppermute | solution.py:734
  225.6 39.1 %collective-permute-start.27 = (bf16[256,1280]{1,0:T(8,128)(2,1)}, bf16[256,1280]{1,0:T(8,128)(2,1)S(1)}, u32[]{:S(2)}, u32[]{:S(2)}) collective-permute-start(bf16[256,1280]{1,0:T(8,128)(2,1)} %get-tuple-element.112), channel_id=1, source_target_pairs={{0,24},{8,16},{16,8},{24,0},{1,25},{9,17},{17,9},{25,1},{2,26},{10... | collective-permute-start | bytes 1966088 | tf_op jit(solution)/shard_map/ppermute | solution.py:734
  247.8 17.0 %collective-permute-start.35 = (bf16[1,2,144,640]{3,2,1,0:T(8,128)(2,1)}, bf16[1,2,144,640]{3,2,1,0:T(8,128)(2,1)S(1)}, u32[]{:S(2)}, u32[]{:S(2)}) collective-permute-start(bf16[1,2,144,640]{3,2,1,0:T(8,128)(2,1)} %get-tuple-element.122.refs_6_), channel_id=1, source_target_pairs={{0,2},{1,3},{2,0},{3,1},{4,6},{5,7},{6,4},{7,5},{8,10},{9,11},{10,... | collective-permute-start | bytes 1105928 | tf_op jit(solution)/shard_map/ppermute | solution.py:760
  267.8 22.8 %collective-permute-start.37 = (bf16[128,1280]{1,0:T(8,128)(2,1)S(1)}, bf16[128,1280]{1,0:T(8,128)(2,1)S(1)}, u32[]{:S(2)}, u32[]{:S(2)}) collective-permute-start(bf16[128,1280]{1,0:T(8,128)(2,1)S(1)} %add_convert_fusion.1), channel_id=1, source_target_pairs={{0,6},{1,7},{2,4},{3,5},{4,2},{5,3},{6,0},{7,1},{8,14},{9,15},{10,... | collective-permute-start | bytes 983048 | tf_op jit(solution)/shard_map/ppermute | solution.py:884
  269.2 26.5 %collective-permute-start.38 = (bf16[1,2,144,640]{3,2,1,0:T(8,128)(2,1)}, bf16[1,2,144,640]{3,2,1,0:T(8,128)(2,1)S(1)}, u32[]{:S(2)}, u32[]{:S(2)}) collective-permute-start(bf16[1,2,144,640]{3,2,1,0:T(8,128)(2,1)} %get-tuple-element.135), channel_id=1, source_target_pairs={{0,6},{1,7},{2,4},{3,5},{4,2},{5,3},{6,0},{7,1},{8,14},{9,15},{10,... | collective-permute-start | bytes 1105928 | tf_op jit(solution)/shard_map/ppermute | solution.py:760
  (50 other events, 382.8 us)

commit v3 on v2

--- a/solution.py
+++ b/solution.py
@@ -814,23 +814,24 @@
     x_piece = stack_pieces(x_z)
     x_plane = send_plane(x_piece, x_piece)
     dy_z = send_along_z(cotangent)
-    x_plane = after(x_plane, *dy_z[:2])
-    x_plane = [*x_plane, *send_diagonal(*x_plane)]
     near_own = join_plane(tp_index, near, near_x, near_y, *near_d)
     near_other = swap_cores(near_own)
     x_near = [(near_own, 0, tok_count), (near_other, 0, tok_count)]
     hidden_near, slope_near, act_near = forward_rows(x_near, w_both, 2 * tile)
     spare_rows = -shadow_part % 128 + shadow_part
     down = jnp.pad(w_down[0], ((0, spare_rows), (0, 0)))
+    *x_plane, down = after([*x_plane, down], *dy_z[:2], hidden_near)
+    x_plane = [*x_plane, *send_diagonal(*x_plane)]
     (shadow_blocks,) = after([shadow_blocks], x_z[0])
     shadow_kept, shadow_taken = exchange_cores(shadow_blocks)
-    fenced = after([*x_plane[2:], down, *shadow_taken, *dy_z], hidden_near)
-    x_plane[2:], down, shadow_taken, dy_z = fenced[:2], fenced[2], fenced[3:4], fenced[4:]
+    shadow_pieces = chip_pieces(shadow_kept, shadow_taken)
+    shadow_pieces[1] = send_piece(shadow_pieces[1], 1)
+    fenced = after([*x_plane[2:], *shadow_pieces[1:], *dy_z])
+    x_plane[2:], shadow_pieces[1:], dy_z = fenced[:2], fenced[2 : 1 + steps], fenced[1 + steps :]
 
     dy_piece = stack_pieces(dy_z)
     dy_plane = send_plane(dy_piece)
-    shadow_pieces = chip_pieces(shadow_kept, shadow_taken)
-    for shift in range(1, steps - 1):
+    for shift in range(2, steps - 1):
         shadow_pieces[shift] = send_piece(shadow_pieces[shift], shift)
     x_own = join_plane(tp_index, x_piece, *x_plane, earlier=[dy_piece])
     x_other = swap_cores(x_own)

time: 301 us -> 302 us (level)
  waiting for transfers between devices: 84.5 us -> 78.6 us
  starting transfers between devices: 39.6 us -> 44.4 us
    ppermute x6, starting transfers between devices: 6.35 us -> 11.4 us  [send_piece(): return lax.ppermute(piece, 'ep', swap_pairs(lax.axis_size('ep'), 2 * shift))]
    ppermute x6, waiting for transfers between devices: 22.4 us -> 18.4 us  [send_along_z(): lax.ppermute(own, 'ep', swap_pairs(ep_count, 2 * s))]
    unnamed x70 -> x72, local copies, waits for them, and re-layouts: 10.6 us -> 12.7 us
  transfers between devices with their start and end apart: 39 -> 39, of which waited for: 17 -> 14; matrix products, arithmetic and copies ran while one was open for 12% -> 12% of each run, Pallas kernels for 35% -> 35%
where the time goes in v3:
time: 302 us; the launch traced here: 301 us
  Pallas kernels  127 us (42%)
  waiting for transfers between devices  78.6 us (26%)
  starting transfers between devices  44.4 us (15%)
  other arithmetic  25.8 us (9%)
  local copies, waits for them, and re-layouts  24.4 us (8%)
    pallas_call x10, Pallas kernels, kernel_call(): pl.pallas_call(run, out_shape=out_shape, grid_spec=pltpu.PrefetchScalarGr...  94 us
    ppermute x6, waiting for transfers between devices, send_piece(): return lax.ppermute(piece, 'ep', swap_pairs(lax.axis_size('ep'), 2 * shift))  27.7 us
    ppermute x3, waiting for transfers between devices, send_rows(): return lax.ppermute(piece, 'ep', swap_pairs(ep_count, 2 * (i + 1)))  20.8 us
    ppermute x6, waiting for transfers between devices, send_along_z(): lax.ppermute(own, 'ep', swap_pairs(ep_count, 2 * s))  18.4 us
    ppermute x13, starting transfers between devices, send_plane(): lax.ppermute(p, 'tp', swap_pairs(lax.axis_size('tp'), bit))  17.8 us
    pallas_call x3, Pallas kernels, join_plane(): pl.pallas_call(body, out_shape=shape_of(rows, count * quarter), grid_spec...  13.8 us
    unnamed x72, local copies, waits for them, and re-layouts  12.7 us
    ppermute x6, starting transfers between devices, send_piece(): return lax.ppermute(piece, 'ep', swap_pairs(lax.axis_size('ep'), 2 * shift))  11.4 us
  transfers between devices with their start and end apart: 39, of which 14 were waited for; matrix products, arithmetic and copies ran while one was open for 12% of the time, Pallas kernels for 35%

profile of v3, /device:TPU:16, one launch (start us, length us, event | category | flops | bytes accessed | tf_op | source)
XLA Modules:
  0.0 300.9 jit_solution(15520568486762433306)
XLA Ops:
  9.1 7.1 %pad_maximum_fusion.refs_5_.refs_2_ = bf16[5120,768]{1,0:T(8,128)(2,1)} fusion(bf16[5120,384]{1,0:T(8,128)(2,1)} %bitcast.98, bf16[5120,384]{1,0:T(8,128)(2,1)} %bitcast.99), kind=kLoop, calls=%fused_computation | loop fusion | flops 15728640 | bytes 15728640 | tf_op jit(solution)/shard_map/concatenate | solution.py:810
  30.7 6.3 %collective-permute-done.6.refs_4_ = bf16[128,1280]{1,0:T(8,128)(2,1)S(1)} collective-permute-done((bf16[128,1280]{1,0:T(8,128)(2,1)}, bf16[128,1280]{1,0:T(8,128)(2,1)S(1)}, u32[]{:S(2)}, u32[]{:S(2)}) %collective-permute-start.6) | collective-permute-done | bytes 327712 | tf_op jit(solution)/shard_map/ppermute | solution.py:725
  38.6 4.3 %join_plane.3.refs_0_.refs_1_.refs_5_ = bf16[256,5120]{1,0:T(8,128)(2,1)} custom-call(s32[1]{0:T(128)} %bitcast.column_ref, bf16[256,1280]{1,0:T(8,128)(2,1)} %stack_pieces.3.refs_0_, bf16[256,1280]{1,0:T(8,128)(2,1)} %get-tuple-element.75.refs_1_, bf16[256,1280]{1,0:T(8,128)(2,1)} %get-tuple-element.76.refs_2_, ...), custom_call_target="tpu_custom_call" | custom-call | flops 1 | bytes 1 | tf_op jit(solution)/shard_map/join_plane/pallas_call | solution.py:236
  51.3 5.3 %pad.9.refs_2_ = bf16[512,5120]{1,0:T(8,128)(2,1)} pad(bf16[384,5120]{1,0:T(8,128)(2,1)} %bitcast.96, bf16[]{:T(256)} %constant.71.clone.1), padding=0_128x0_0 | pad | bytes 9175042 | tf_op jit(solution)/shard_map/jit(_pad)/pad | solution.py:822
  60.3 6.9 %forward_rows.3 = (bf16[256,384]{1,0:T(8,128)(2,1)}, bf16[256,384]{1,0:T(8,128)(2,1)}, bf16[256,384]{1,0:T(8,128)(2,1)}) custom-call(s32[1]{0:T(128)} %constant.69.clone.1.column_ref, bf16[256,5120]{1,0:T(8,128)(2,1)} %join_plane.3.refs_0_.refs_1_.refs_5_, bf16[256,5120]{1,0:T(8,128)(2,1)} %copy-done, bf16[5120,768]{1,0:T(8,128)(2,1)} %pad_maximum_fusion.refs_5_.refs_2_), custom_call_target="tpu_custom_call" | custom-call | flops 1 | bytes 1 | tf_op jit(solution)/shard_map/forward_rows/pallas_call | solution.py:196
  67.3 5.1 %collective-permute-done.8.refs_0_ = bf16[384,1280]{1,0:T(8,128)(2,1)} collective-permute-done((bf16[384,1280]{1,0:T(8,128)(2,1)}, bf16[384,1280]{1,0:T(8,128)(2,1)}, u32[]{:S(2)}, u32[]{:S(2)}) %collective-permute-start.8) | collective-permute-done | bytes 983072 | tf_op jit(solution)/shard_map/ppermute | solution.py:734
  78.4 8.9 %collective-permute-done.16.refs_7_ = bf16[128,1280]{1,0:T(8,128)(2,1)S(1)} collective-permute-done((bf16[128,1280]{1,0:T(8,128)(2,1)}, bf16[128,1280]{1,0:T(8,128)(2,1)S(1)}, u32[]{:S(2)}, u32[]{:S(2)}) %collective-permute-start.16) | collective-permute-done | bytes 327712 | tf_op jit(solution)/shard_map/ppermute | solution.py:725
  94.1 4.8 %join_plane.4.refs_0_ = bf16[384,5120]{1,0:T(8,128)(2,1)} custom-call(s32[1]{0:T(128)} %bitcast.column_ref, bf16[384,1280]{1,0:T(8,128)(2,1)} %stack_pieces.4.refs_0_, bf16[384,1280]{1,0:T(8,128)(2,1)} %get-tuple-element.83.refs_1_, bf16[384,1280]{1,0:T(8,128)(2,1)} %get-tuple-element.84.refs_2_, bf16[192,1280]{1,0:T(8,128)(2,1)} %get-tuple-element.85.refs_3_, ...), custom_call_target="tpu_custom_call" | custom-call | flops 1 | bytes 1 | tf_op jit(solution)/shard_map/join_plane/pallas_call | solution.py:236
  102.4 6.7 %collective-permute-start.18 = (bf16[1,2,160,640]{3,2,1,0:T(8,128)(2,1)}, bf16[1,2,160,640]{3,2,1,0:T(8,128)(2,1)}, u32[]{:S(2)}, u32[]{:S(2)}) collective-permute-start(bf16[1,2,160,640]{3,2,1,0:T(8,128)(2,1)} %get-tuple-element.92), channel_id=1, source_target_pairs={{0,4},{1,5},{2,6},{3,7},{4,0},{5,1},{6,2},{7,3},{8,12},{9,13},{10,... | collective-permute-start | bytes 1228808 | tf_op jit(solution)/shard_map/ppermute | solution.py:760
  111.1 11.5 %forward_rows.4 = (bf16[768,384]{1,0:T(8,128)(2,1)}, bf16[768,384]{1,0:T(8,128)(2,1)}, bf16[768,384]{1,0:T(8,128)(2,1)}) custom-call(s32[1]{0:T(128)} %constant.69.clone.1.column_ref, bf16[384,5120]{1,0:T(8,128)(2,1)} %join_plane.4.refs_0_, bf16[384,5120]{1,0:T(8,128)(2,1)} %copy-done.1, bf16[5120,768]{1,0:T(8,128)(2,1)} %pad_maximum_fusion.refs_5_.refs_2_), custom_call_target="tpu_custom_call" | custom-call | flops 1 | bytes 1 | tf_op jit(solution)/shard_map/forward_rows/pallas_call | solution.py:196
  125.6 19.4 %collective-permute-done.19.refs_3_.refs_6_ = bf16[1,2,160,640]{3,2,1,0:T(8,128)(2,1)S(1)} collective-permute-done((bf16[1,2,160,640]{3,2,1,0:T(8,128)(2,1)}, bf16[1,2,160,640]{3,2,1,0:T(8,128)(2,1)S(1)}, u32[]{:S(2)}, u32[]{:S(2)}) %collective-permute-start.19) | collective-permute-done | bytes 409632 | tf_op jit(solution)/shard_map/ppermute | solution.py:760
  145.7 4.9 %lay_out_shadow.1 = (bf16[256,5120]{1,0:T(8,128)(2,1)}, bf16[512,5120]{1,0:T(8,128)(2,1)}) custom-call(s32[1]{0:T(128)} %bitcast.18.chip_ref, bf16[1,2,160,640]{3,2,1,0:T(8,128)(2,1)} %get-tuple-element.149.refs_0_.refs_3_, bf16[1,2,160,640]{3,2,1,0:T(8,128)(2,1)} %get-tuple-element.91.refs_1_.refs_4_, ...), custom_call_target="tpu_custom_call", output_to_operand_aliasing={{1}: (5, {})} | custom-call | flops 1 | bytes 1 | tf_op jit(solution)/shard_map/lay_out_shadow/pallas_call | solution.py:306
  150.6 8.0 %forward_rows.5 = (bf16[1024,128]{1,0:T(8,128)(2,1)}, bf16[1024,128]{1,0:T(8,128)(2,1)}, bf16[1024,128]{1,0:T(8,128)(2,1)}) custom-call(s32[1]{0:T(128)} %constant.69.clone.1.column_ref, bf16[384,5120]{1,0:T(8,128)(2,1)} %join_plane.4.refs_0_, bf16[256,5120]{1,0:T(8,128)(2,1)} %join_plane.3.refs_0_.refs_1_.refs_5_, bf16[256,5120]{1,0:T(8,128)(2,1)} %copy-done, ...), custom_call_target="tpu_custom_call" | custom-call | flops 1 | bytes 1 | tf_op jit(solution)/shard_map/forward_rows/pallas_call | solution.py:196
  162.0 6.9 %output_other.1 = (bf16[256,5120]{1,0:T(8,128)(2,1)}, bf16[256,5120]{1,0:T(8,128)(2,1)}) custom-call(s32[1]{0:T(128)} %bitcast.column_ref, bf16[1024,512]{1,0:T(8,128)(2,1)} %get-tuple-element.97.refs_0_.refs_10_.refs_4_, bf16[512,5120]{1,0:T(8,128)(2,1)} %get-tuple-element.98.refs_1_.refs_3_), custom_call_target="tpu_custom_call" | custom-call | flops 1 | bytes 1 | tf_op jit(solution)/shard_map/output_other/pallas_call | solution.py:196
  168.9 4.7 %join_plane.5.refs_0_.refs_4_ = bf16[384,5120]{1,0:T(8,128)(2,1)} custom-call(s32[1]{0:T(128)} %bitcast.column_ref, bf16[384,1280]{1,0:T(8,128)(2,1)} %stack_pieces.5.refs_5_.refs_0_, bf16[384,1280]{1,0:T(8,128)(2,1)} %get-tuple-element.101.refs_1_, bf16[384,1280]{1,0:T(8,128)(2,1)} %get-tuple-element.102.refs_2_, bf16[384,1280]{1,0:T(8,128)(2,1)} %get-tuple-element.103.refs_3_), custom_call_target="tpu_custom_call" | custom-call | flops 1 | bytes 1 | tf_op jit(solution)/shard_map/join_plane/pallas_call | solution.py:236
  174.2 9.8 %backward_rows.2 = (bf16[640,768]{1,0:T(8,128)(2,1)}, bf16[640,256]{1,0:T(8,128)(2,1)}) custom-call(s32[1]{0:T(128)} %constant.69.clone.1.column_ref, bf16[384,5120]{1,0:T(8,128)(2,1)} %join_plane.5.refs_0_.refs_4_, bf16[256,5120]{1,0:T(8,128)(2,1)} %join_plane.3.refs_0_.refs_1_.refs_5_, bf16[256,5120]{1,0:T(8,128)(2,1)} %copy-done, ...), custom_call_target="tpu_custom_call" | custom-call | flops 1 | bytes 1 | tf_op jit(solution)/shard_map/backward_rows/pallas_call | solution.py:196
  184.2 4.0 %collective-permute-done.21.refs_3_ = bf16[256,5120]{1,0:T(8,128)(2,1)} collective-permute-done((bf16[256,5120]{1,0:T(8,128)(2,1)}, bf16[256,5120]{1,0:T(8,128)(2,1)}, u32[]{:S(2)}, u32[]{:S(2)}) %collective-permute-start.21) | collective-permute-done | bytes 2621472 | tf_op jit(solution)/shard_map/ppermute | solution.py:729
  188.2 10.1 %output_own.1 = (f32[256,1280]{1,0:T(8,128)}, bf16[256,1280]{1,0:T(8,128)(2,1)}, bf16[256,1280]{1,0:T(8,128)(2,1)}, bf16[256,1280]{1,0:T(8,128)(2,1)}, f32[256,1...) custom-call(s32[1]{0:T(128)} %bitcast.column_ref, ...), custom_call_target="tpu_custom_call" | custom-call | flops 1 | bytes 1 | tf_op jit(solution)/shard_map/output_own/pallas_call | solution.py:196
  203.7 7.7 %backward_rows.3 = (bf16[384,768]{1,0:T(8,128)(2,1)}, bf16[384,256]{1,0:T(8,128)(2,1)}) custom-call(s32[1]{0:T(128)} %constant.69.clone.1.column_ref, bf16[384,5120]{1,0:T(8,128)(2,1)} %copy-done.3, bf16[512,5120]{1,0:T(8,128)(2,1)} %get-tuple-element.98.refs_1_.refs_3_, bf16[768,384]{1,0:T(8,128)(2,1)} %get-tuple-element.104.refs_4_.refs_2_, ...), custom_call_target="tpu_custom_call" | custom-call | flops 1 | bytes 1 | tf_op jit(solution)/shard_map/backward_rows/pallas_call | solution.py:196
  211.4 11.1 %shadow_grads.1.refs_3_ = bf16[8,144,640]{2,1,0:T(8,128)(2,1)} custom-call(s32[1]{0:T(128)} %constant.69.clone.1.column_ref, bf16[384,5120]{1,0:T(8,128)(2,1)} %join_plane.4.refs_0_, bf16[256,5120]{1,0:T(8,128)(2,1)} %join_plane.3.refs_0_.refs_1_.refs_5_, bf16[256,5120]{1,0:T(8,128)(2,1)} %copy-done, bf16[384,5120]{1,0:T(8,128)(2,1)} %copy-done.1, ...), custom_call_target="tpu_custom_call" | custom-call | flops 1 | bytes 1 | tf_op jit(solution)/shard_map/shadow_grads/pallas_call | solution.py:196
  228.1 4.8 %collective-permute-start.27 = (bf16[256,1280]{1,0:T(8,128)(2,1)}, bf16[256,1280]{1,0:T(8,128)(2,1)S(1)}, u32[]{:S(2)}, u32[]{:S(2)}) collective-permute-start(bf16[256,1280]{1,0:T(8,128)(2,1)} %get-tuple-element.116), channel_id=1, source_target_pairs={{0,24},{8,16},{16,8},{24,0},{1,25},{9,17},{17,9},{25,1},{2,26},{10... | collective-permute-start | bytes 1966088 | tf_op jit(solution)/shard_map/ppermute | solution.py:734
  239.2 9.1 %down_grad.1.refs_5_ = bf16[384,5120]{1,0:T(8,128)(2,1)} custom-call(s32[1]{0:T(128)} %constant.69.clone.1.column_ref, bf16[384,5120]{1,0:T(8,128)(2,1)} %join_plane.5.refs_0_.refs_4_, bf16[256,5120]{1,0:T(8,128)(2,1)} %join_plane.3.refs_0_.refs_1_.refs_5_, bf16[256,5120]{1,0:T(8,128)(2,1)} %copy-done, bf16[384,5120]{1,0:T(8,128)(2,1)} %copy-done.3, ...), custom_call_target="tpu_custom_call" | custom-call | flops 1 | bytes 1 | tf_op jit(solution)/shard_map/down_grad/pallas_call | solution.py:196
  252.7 12.9 %input_grads.1 = (bf16[5120,384]{1,0:T(8,128)(2,1)}, bf16[5120,384]{1,0:T(8,128)(2,1)}) custom-call(s32[1]{0:T(128)} %constant.69.clone.1.column_ref, bf16[384,5120]{1,0:T(8,128)(2,1)} %join_plane.4.refs_0_, bf16[256,5120]{1,0:T(8,128)(2,1)} %join_plane.3.refs_0_.refs_1_.refs_5_, bf16[256,5120]{1,0:T(8,128)(2,1)} %copy-done, bf16[384,5120]{1,0:T(8,128)(2,1)} %copy-done.1, ...), custom_call_target="tpu_custom_call" | custom-call | flops 1 | bytes 1 | tf_op jit(solution)/shard_map/input_grads/pallas_call | solution.py:196
  270.8 20.8 %collective-permute-done.37 = bf16[128,1280]{1,0:T(8,128)(2,1)S(1)} collective-permute-done((bf16[128,1280]{1,0:T(8,128)(2,1)S(1)}, bf16[128,1280]{1,0:T(8,128)(2,1)S(1)}, u32[]{:S(2)}, u32[]{:S(2)}) %collective-permute-start.37) | collective-permute-done | bytes 327712 | tf_op jit(solution)/shard_map/ppermute | solution.py:885
  (180 shorter events, 98.9 us)
Async XLA Ops:
  2.6 16.8 %collective-permute-start = (bf16[256,1280]{1,0:T(8,128)(2,1)}, bf16[256,1280]{1,0:T(8,128)(2,1)S(1)}, u32[]{:S(2)}, u32[]{:S(2)}) collective-permute-start(bf16[256,1280]{1,0:T(8,128)(2,1)} %stack_pieces.3.refs_0_), channel_id=1, source_target_pairs={{0,8},{8,0},{16,24},{24,16},{1,9},{9,1},{17,25},{25,17},{2,10},{10... | collective-permute-start | bytes 1966088 | tf_op jit(solution)/shard_map/ppermute | solution.py:734
  4.1 16.4 %collective-permute-start.1 = (bf16[256,1280]{1,0:T(8,128)(2,1)}, bf16[256,1280]{1,0:T(8,128)(2,1)S(1)}, u32[]{:S(2)}, u32[]{:S(2)}) collective-permute-start(bf16[256,1280]{1,0:T(8,128)(2,1)} %stack_pieces.3.refs_0_), channel_id=1, source_target_pairs={{0,16},{8,24},{16,0},{24,8},{1,17},{9,25},{17,1},{25,9},{2,18},{10... | collective-permute-start | bytes 1966088 | tf_op jit(solution)/shard_map/ppermute | solution.py:734
  7.2 23.5 %collective-permute-start.5 = (bf16[128,1280]{1,0:T(8,128)(2,1)}, bf16[128,1280]{1,0:T(8,128)(2,1)S(1)}, u32[]{:S(2)}, u32[]{:S(2)}) collective-permute-start(bf16[128,1280]{1,0:T(8,128)(2,1)} %refs_0_.1), channel_id=1, source_target_pairs={{0,4},{1,5},{2,6},{3,7},{4,0},{5,1},{6,2},{7,3},{8,12},{9,13},{10,... | collective-permute-start | bytes 983048 | tf_op jit(solution)/shard_map/ppermute | solution.py:725
  7.5 29.5 %collective-permute-start.6 = (bf16[128,1280]{1,0:T(8,128)(2,1)}, bf16[128,1280]{1,0:T(8,128)(2,1)S(1)}, u32[]{:S(2)}, u32[]{:S(2)}) collective-permute-start(bf16[128,1280]{1,0:T(8,128)(2,1)} %refs_0_.1), channel_id=1, source_target_pairs={{0,6},{1,7},{2,4},{3,5},{4,2},{5,3},{6,0},{7,1},{8,14},{9,15},{10,... | collective-permute-start | bytes 983048 | tf_op jit(solution)/shard_map/ppermute | solution.py:725
  48.4 24.0 %collective-permute-start.8 = (bf16[384,1280]{1,0:T(8,128)(2,1)}, bf16[384,1280]{1,0:T(8,128)(2,1)}, u32[]{:S(2)}, u32[]{:S(2)}) collective-permute-start(bf16[384,1280]{1,0:T(8,128)(2,1)} %stack_pieces.4.refs_0_), channel_id=1, source_target_pairs={{0,8},{8,0},{16,24},{24,16},{1,9},{9,1},{17,25},{25,17},{2,10},{10... | collective-permute-start | bytes 2949128 | tf_op jit(solution)/shard_map/ppermute | solution.py:734
  48.9 23.7 %collective-permute-start.9 = (bf16[384,1280]{1,0:T(8,128)(2,1)}, bf16[384,1280]{1,0:T(8,128)(2,1)}, u32[]{:S(2)}, u32[]{:S(2)}) collective-permute-start(bf16[384,1280]{1,0:T(8,128)(2,1)} %stack_pieces.4.refs_0_), channel_id=1, source_target_pairs={{0,16},{8,24},{16,0},{24,8},{1,17},{9,25},{17,1},{25,9},{2,18},{10... | collective-permute-start | bytes 2949128 | tf_op jit(solution)/shard_map/ppermute | solution.py:734
  49.3 17.9 %collective-permute-start.10 = (bf16[128,1280]{1,0:T(8,128)(2,1)}, bf16[128,1280]{1,0:T(8,128)(2,1)}, u32[]{:S(2)}, u32[]{:S(2)}) collective-permute-start(bf16[128,1280]{1,0:T(8,128)(2,1)} %refs_1_.1), channel_id=1, source_target_pairs={{0,2},{1,3},{2,0},{3,1},{4,6},{5,7},{6,4},{7,5},{8,10},{9,11},{10,... | collective-permute-start | bytes 983048 | tf_op jit(solution)/shard_map/ppermute | solution.py:725
  49.3 17.9 %collective-permute-start.11 = (bf16[128,1280]{1,0:T(8,128)(2,1)}, bf16[128,1280]{1,0:T(8,128)(2,1)}, u32[]{:S(2)}, u32[]{:S(2)}) collective-permute-start(bf16[128,1280]{1,0:T(8,128)(2,1)} %refs_1_.1), channel_id=1, source_target_pairs={{0,4},{1,5},{2,6},{3,7},{4,0},{5,1},{6,2},{7,3},{8,12},{9,13},{10,... | collective-permute-start | bytes 983048 | tf_op jit(solution)/shard_map/ppermute | solution.py:725
  73.7 16.6 %collective-permute-start.12 = (bf16[192,1280]{1,0:T(8,128)(2,1)S(1)}, bf16[192,1280]{1,0:T(8,128)(2,1)S(1)}, u32[]{:S(2)}, u32[]{:S(2)}) collective-permute-start(bf16[192,1280]{1,0:T(8,128)(2,1)S(1)} %slice.86), channel_id=1, source_target_pairs={{0,16},{8,24},{16,0},{24,8},{1,17},{9,25},{17,1},{25,9},{2,18},{10... | collective-permute-start | bytes 1474568 | tf_op jit(solution)/shard_map/ppermute | solution.py:740
  98.9 70.0 %collective-permute-start.22 = (bf16[384,1280]{1,0:T(8,128)(2,1)}, bf16[384,1280]{1,0:T(8,128)(2,1)}, u32[]{:S(2)}, u32[]{:S(2)}) collective-permute-start(bf16[384,1280]{1,0:T(8,128)(2,1)} %stack_pieces.5.refs_5_.refs_0_), channel_id=1, source_target_pairs={{0,8},{8,0},{16,24},{24,16},{1,9},{9,1},{17,25},{25,17},{2,10},{10... | collective-permute-start | bytes 2949128 | tf_op jit(solution)/shard_map/ppermute | solution.py:734
  99.4 69.5 %collective-permute-start.23 = (bf16[384,1280]{1,0:T(8,128)(2,1)}, bf16[384,1280]{1,0:T(8,128)(2,1)}, u32[]{:S(2)}, u32[]{:S(2)}) collective-permute-start(bf16[384,1280]{1,0:T(8,128)(2,1)} %stack_pieces.5.refs_5_.refs_0_), channel_id=1, source_target_pairs={{0,16},{8,24},{16,0},{24,8},{1,17},{9,25},{17,1},{25,9},{2,18},{10... | collective-permute-start | bytes 2949128 | tf_op jit(solution)/shard_map/ppermute | solution.py:734
  100.9 68.0 %collective-permute-start.24 = (bf16[384,1280]{1,0:T(8,128)(2,1)}, bf16[384,1280]{1,0:T(8,128)(2,1)}, u32[]{:S(2)}, u32[]{:S(2)}) collective-permute-start(bf16[384,1280]{1,0:T(8,128)(2,1)} %stack_pieces.5.refs_5_.refs_0_), channel_id=1, source_target_pairs={{0,24},{8,16},{16,8},{24,0},{1,25},{9,17},{17,9},{25,1},{2,26},{10... | collective-permute-start | bytes 2949128 | tf_op jit(solution)/shard_map/ppermute | solution.py:734
  102.4 23.2 %collective-permute-start.18 = (bf16[1,2,160,640]{3,2,1,0:T(8,128)(2,1)}, bf16[1,2,160,640]{3,2,1,0:T(8,128)(2,1)}, u32[]{:S(2)}, u32[]{:S(2)}) collective-permute-start(bf16[1,2,160,640]{3,2,1,0:T(8,128)(2,1)} %get-tuple-element.92), channel_id=1, source_target_pairs={{0,4},{1,5},{2,6},{3,7},{4,0},{5,1},{6,2},{7,3},{8,12},{9,13},{10,... | collective-permute-start | bytes 1228808 | tf_op jit(solution)/shard_map/ppermute | solution.py:760
  122.6 22.4 %collective-permute-start.19 = (bf16[1,2,160,640]{3,2,1,0:T(8,128)(2,1)}, bf16[1,2,160,640]{3,2,1,0:T(8,128)(2,1)S(1)}, u32[]{:S(2)}, u32[]{:S(2)}) collective-permute-start(bf16[1,2,160,640]{3,2,1,0:T(8,128)(2,1)} %after.15), channel_id=1, source_target_pairs={{0,6},{1,7},{2,4},{3,5},{4,2},{5,3},{6,0},{7,1},{8,14},{9,15},{10,... | collective-permute-start | bytes 1228808 | tf_op jit(solution)/shard_map/ppermute | solution.py:760
  173.6 28.2 %collective-permute-start.31 = (bf16[384,5120]{1,0:T(8,128)(2,1)}, bf16[384,5120]{1,0:T(8,128)(2,1)S(1)}, u32[]{:S(2)}, u32[]{:S(2)}) collective-permute-start(bf16[384,5120]{1,0:T(8,128)(2,1)} %join_plane.5.refs_0_.refs_4_), channel_id=1, source_target_pairs={{0,1},{1,0},{2,3},{3,2},{4,5},{5,4},{6,7},{7,6},{8,9},{9,8},{10,11... | collective-permute-start | bytes 11796488 | tf_op jit(solution)/shard_map/ppermute | solution.py:729
  198.3 27.1 %collective-permute-start.28 = (bf16[256,1280]{1,0:T(8,128)(2,1)}, bf16[256,1280]{1,0:T(8,128)(2,1)}, u32[]{:S(2)}, u32[]{:S(2)}) collective-permute-start(bf16[256,1280]{1,0:T(8,128)(2,1)} %get-tuple-element.118.refs_8_), channel_id=1, source_target_pairs={{0,8},{8,0},{16,24},{24,16},{1,9},{9,1},{17,25},{25,17},{2,10},{10... | collective-permute-start | bytes 1966088 | tf_op jit(solution)/shard_map/ppermute | solution.py:734
  198.9 29.2 %collective-permute-start.29 = (bf16[256,1280]{1,0:T(8,128)(2,1)}, bf16[256,1280]{1,0:T(8,128)(2,1)}, u32[]{:S(2)}, u32[]{:S(2)}) collective-permute-start(bf16[256,1280]{1,0:T(8,128)(2,1)} %get-tuple-element.119), channel_id=1, source_target_pairs={{0,16},{8,24},{16,0},{24,8},{1,17},{9,25},{17,1},{25,9},{2,18},{10... | collective-permute-start | bytes 1966088 | tf_op jit(solution)/shard_map/ppermute | solution.py:734
  200.4 32.5 %collective-permute-start.30 = (bf16[256,1280]{1,0:T(8,128)(2,1)}, bf16[256,1280]{1,0:T(8,128)(2,1)}, u32[]{:S(2)}, u32[]{:S(2)}) collective-permute-start(bf16[256,1280]{1,0:T(8,128)(2,1)} %get-tuple-element.120), channel_id=1, source_target_pairs={{0,24},{8,16},{16,8},{24,0},{1,25},{9,17},{17,9},{25,1},{2,26},{10... | collective-permute-start | bytes 1966088 | tf_op jit(solution)/shard_map/ppermute | solution.py:734
  224.9 40.7 %collective-permute-start.25 = (bf16[256,1280]{1,0:T(8,128)(2,1)}, bf16[256,1280]{1,0:T(8,128)(2,1)S(1)}, u32[]{:S(2)}, u32[]{:S(2)}) collective-permute-start(bf16[256,1280]{1,0:T(8,128)(2,1)} %get-tuple-element.114.refs_9_), channel_id=1, source_target_pairs={{0,8},{8,0},{16,24},{24,16},{1,9},{9,1},{17,25},{25,17},{2,10},{10... | collective-permute-start | bytes 1966088 | tf_op jit(solution)/shard_map/ppermute | solution.py:734
  225.4 40.2 %collective-permute-start.26 = (bf16[256,1280]{1,0:T(8,128)(2,1)}, bf16[256,1280]{1,0:T(8,128)(2,1)S(1)}, u32[]{:S(2)}, u32[]{:S(2)}) collective-permute-start(bf16[256,1280]{1,0:T(8,128)(2,1)} %get-tuple-element.115), channel_id=1, source_target_pairs={{0,16},{8,24},{16,0},{24,8},{1,17},{9,25},{17,1},{25,9},{2,18},{10... | collective-permute-start | bytes 1966088 | tf_op jit(solution)/shard_map/ppermute | solution.py:734
  228.1 37.6 %collective-permute-start.27 = (bf16[256,1280]{1,0:T(8,128)(2,1)}, bf16[256,1280]{1,0:T(8,128)(2,1)S(1)}, u32[]{:S(2)}, u32[]{:S(2)}) collective-permute-start(bf16[256,1280]{1,0:T(8,128)(2,1)} %get-tuple-element.116), channel_id=1, source_target_pairs={{0,24},{8,16},{16,8},{24,0},{1,25},{9,17},{17,9},{25,1},{2,26},{10... | collective-permute-start | bytes 1966088 | tf_op jit(solution)/shard_map/ppermute | solution.py:734
  249.2 16.5 %collective-permute-start.35 = (bf16[1,2,144,640]{3,2,1,0:T(8,128)(2,1)}, bf16[1,2,144,640]{3,2,1,0:T(8,128)(2,1)S(1)}, u32[]{:S(2)}, u32[]{:S(2)}) collective-permute-start(bf16[1,2,144,640]{3,2,1,0:T(8,128)(2,1)} %get-tuple-element.126.refs_6_), channel_id=1, source_target_pairs={{0,2},{1,3},{2,0},{3,1},{4,6},{5,7},{6,4},{7,5},{8,10},{9,11},{10,... | collective-permute-start | bytes 1105928 | tf_op jit(solution)/shard_map/ppermute | solution.py:760
  268.7 22.9 %collective-permute-start.37 = (bf16[128,1280]{1,0:T(8,128)(2,1)S(1)}, bf16[128,1280]{1,0:T(8,128)(2,1)S(1)}, u32[]{:S(2)}, u32[]{:S(2)}) collective-permute-start(bf16[128,1280]{1,0:T(8,128)(2,1)S(1)} %add_convert_fusion.1), channel_id=1, source_target_pairs={{0,6},{1,7},{2,4},{3,5},{4,2},{5,3},{6,0},{7,1},{8,14},{9,15},{10,... | collective-permute-start | bytes 983048 | tf_op jit(solution)/shard_map/ppermute | solution.py:885
  270.1 26.7 %collective-permute-start.38 = (bf16[1,2,144,640]{3,2,1,0:T(8,128)(2,1)}, bf16[1,2,144,640]{3,2,1,0:T(8,128)(2,1)S(1)}, u32[]{:S(2)}, u32[]{:S(2)}) collective-permute-start(bf16[1,2,144,640]{3,2,1,0:T(8,128)(2,1)} %get-tuple-element.139), channel_id=1, source_target_pairs={{0,6},{1,7},{2,4},{3,5},{4,2},{5,3},{6,0},{7,1},{8,14},{9,15},{10,... | collective-permute-start | bytes 1105928 | tf_op jit(solution)/shard_map/ppermute | solution.py:760
  (51 other events, 329.1 us)

commit v4 on v2

--- a/solution.py
+++ b/solution.py
@@ -814,18 +814,18 @@
     x_piece = stack_pieces(x_z)
     x_plane = send_plane(x_piece, x_piece)
     dy_z = send_along_z(cotangent)
-    x_plane = after(x_plane, *dy_z[:2])
-    x_plane = [*x_plane, *send_diagonal(*x_plane)]
     near_own = join_plane(tp_index, near, near_x, near_y, *near_d)
     near_other = swap_cores(near_own)
     x_near = [(near_own, 0, tok_count), (near_other, 0, tok_count)]
     hidden_near, slope_near, act_near = forward_rows(x_near, w_both, 2 * tile)
     spare_rows = -shadow_part % 128 + shadow_part
     down = jnp.pad(w_down[0], ((0, spare_rows), (0, 0)))
+    *x_plane, down = after([*x_plane, down], *dy_z[:2], hidden_near)
+    x_plane = [*x_plane, *send_diagonal(*x_plane)]
     (shadow_blocks,) = after([shadow_blocks], x_z[0])
     shadow_kept, shadow_taken = exchange_cores(shadow_blocks)
-    fenced = after([*x_plane[2:], down, *shadow_taken, *dy_z], hidden_near)
-    x_plane[2:], down, shadow_taken, dy_z = fenced[:2], fenced[2], fenced[3:4], fenced[4:]
+    fenced = after([*x_plane[2:], *shadow_taken, *dy_z])
+    x_plane[2:], shadow_taken, dy_z = fenced[:2], fenced[2:3], fenced[3:]
 
     dy_piece = stack_pieces(dy_z)
     dy_plane = send_plane(dy_piece)

time: 301 us -> 300 us (level)
  starting transfers between devices: 39.6 us -> 35.5 us
    ppermute x13, starting transfers between devices: 19 us -> 15.7 us  [send_plane(): lax.ppermute(p, 'tp', swap_pairs(lax.axis_size('tp'), bit))]
    unnamed x70 -> x74, local copies, waits for them, and re-layouts: 10.6 us -> 9.92 us
  transfers between devices with their start and end apart: 39 -> 39, of which waited for: 17 -> 16; matrix products, arithmetic and copies ran while one was open for 12% -> 12% of each run, Pallas kernels for 35% -> 35%
where the time goes in v4:
time: 300 us; the launch traced here: 297 us
  Pallas kernels  127 us (42%)
  waiting for transfers between devices  87.2 us (29%)
  starting transfers between devices  35.5 us (12%)
  other arithmetic  23.8 us (8%)
  local copies, waits for them, and re-layouts  22.4 us (7%)
    pallas_call x10, Pallas kernels, kernel_call(): pl.pallas_call(run, out_shape=out_shape, grid_spec=pltpu.PrefetchScalarGr...  94.1 us
    ppermute x6, waiting for transfers between devices, send_piece(): return lax.ppermute(piece, 'ep', swap_pairs(lax.axis_size('ep'), 2 * shift))  28.1 us
    ppermute x6, waiting for transfers between devices, send_along_z(): lax.ppermute(own, 'ep', swap_pairs(ep_count, 2 * s))  23.4 us
    ppermute x3, waiting for transfers between devices, send_rows(): return lax.ppermute(piece, 'ep', swap_pairs(ep_count, 2 * (i + 1)))  19.8 us
    ppermute x13, starting transfers between devices, send_plane(): lax.ppermute(p, 'tp', swap_pairs(lax.axis_size('tp'), bit))  15.7 us
    pallas_call x3, Pallas kernels, join_plane(): pl.pallas_call(body, out_shape=shape_of(rows, count * quarter), grid_spec...  14.1 us
    unnamed x74, local copies, waits for them, and re-layouts  9.92 us
    ppermute x13, waiting for transfers between devices, send_plane(): lax.ppermute(p, 'tp', swap_pairs(lax.axis_size('tp'), bit))  9.43 us
  transfers between devices with their start and end apart: 39, of which 16 were waited for; matrix products, arithmetic and copies ran while one was open for 12% of the time, Pallas kernels for 35%

profile of v4, /device:TPU:16, one launch (start us, length us, event | category | flops | bytes accessed | tf_op | source)
XLA Modules:
  0.0 297.1 jit_solution(7218646569909507069)
XLA Ops:
  9.1 7.1 %pad_maximum_fusion.refs_5_.refs_2_ = bf16[5120,768]{1,0:T(8,128)(2,1)} fusion(bf16[5120,384]{1,0:T(8,128)(2,1)} %bitcast.98, bf16[5120,384]{1,0:T(8,128)(2,1)} %bitcast.99), kind=kLoop, calls=%fused_computation | loop fusion | flops 15728640 | bytes 15728640 | tf_op jit(solution)/shard_map/concatenate | solution.py:810
  30.7 6.3 %collective-permute-done.6.refs_4_ = bf16[128,1280]{1,0:T(8,128)(2,1)S(1)} collective-permute-done((bf16[128,1280]{1,0:T(8,128)(2,1)}, bf16[128,1280]{1,0:T(8,128)(2,1)S(1)}, u32[]{:S(2)}, u32[]{:S(2)}) %collective-permute-start.6) | collective-permute-done | bytes 327712 | tf_op jit(solution)/shard_map/ppermute | solution.py:725
  38.6 4.3 %join_plane.3.refs_0_.refs_1_.refs_5_ = bf16[256,5120]{1,0:T(8,128)(2,1)} custom-call(s32[1]{0:T(128)} %bitcast.column_ref, bf16[256,1280]{1,0:T(8,128)(2,1)} %stack_pieces.3.refs_0_, bf16[256,1280]{1,0:T(8,128)(2,1)} %get-tuple-element.73.refs_1_, bf16[256,1280]{1,0:T(8,128)(2,1)} %get-tuple-element.74.refs_2_, ...), custom_call_target="tpu_custom_call" | custom-call | flops 1 | bytes 1 | tf_op jit(solution)/shard_map/join_plane/pallas_call | solution.py:236
  50.8 6.1 %pad.9.refs_2_ = bf16[512,5120]{1,0:T(8,128)(2,1)} pad(bf16[384,5120]{1,0:T(8,128)(2,1)} %bitcast.96, bf16[]{:T(256)} %constant.71.clone.1), padding=0_128x0_0 | pad | bytes 9175042 | tf_op jit(solution)/shard_map/jit(_pad)/pad | solution.py:822
  56.9 6.9 %forward_rows.3 = (bf16[256,384]{1,0:T(8,128)(2,1)}, bf16[256,384]{1,0:T(8,128)(2,1)}, bf16[256,384]{1,0:T(8,128)(2,1)}) custom-call(s32[1]{0:T(128)} %constant.69.clone.1.column_ref, bf16[256,5120]{1,0:T(8,128)(2,1)} %join_plane.3.refs_0_.refs_1_.refs_5_, bf16[256,5120]{1,0:T(8,128)(2,1)} %copy-done, bf16[5120,768]{1,0:T(8,128)(2,1)} %pad_maximum_fusion.refs_5_.refs_2_), custom_call_target="tpu_custom_call" | custom-call | flops 1 | bytes 1 | tf_op jit(solution)/shard_map/forward_rows/pallas_call | solution.py:196
  63.8 6.2 %collective-permute-done.8.refs_0_ = bf16[384,1280]{1,0:T(8,128)(2,1)} collective-permute-done((bf16[384,1280]{1,0:T(8,128)(2,1)}, bf16[384,1280]{1,0:T(8,128)(2,1)}, u32[]{:S(2)}, u32[]{:S(2)}) %collective-permute-start.8) | collective-permute-done | bytes 983072 | tf_op jit(solution)/shard_map/ppermute | solution.py:734
  74.9 13.9 %collective-permute-done.15.refs_5_ = bf16[128,1280]{1,0:T(8,128)(2,1)S(1)} collective-permute-done((bf16[128,1280]{1,0:T(8,128)(2,1)}, bf16[128,1280]{1,0:T(8,128)(2,1)S(1)}, u32[]{:S(2)}, u32[]{:S(2)}) %collective-permute-start.15) | collective-permute-done | bytes 327712 | tf_op jit(solution)/shard_map/ppermute | solution.py:725
  93.4 5.1 %join_plane.4.refs_0_ = bf16[384,5120]{1,0:T(8,128)(2,1)} custom-call(s32[1]{0:T(128)} %bitcast.column_ref, bf16[384,1280]{1,0:T(8,128)(2,1)} %stack_pieces.4.refs_0_, bf16[384,1280]{1,0:T(8,128)(2,1)} %get-tuple-element.81.refs_1_, bf16[384,1280]{1,0:T(8,128)(2,1)} %get-tuple-element.82.refs_2_, bf16[192,1280]{1,0:T(8,128)(2,1)} %get-tuple-element.83.refs_3_, ...), custom_call_target="tpu_custom_call" | custom-call | flops 1 | bytes 1 | tf_op jit(solution)/shard_map/join_plane/pallas_call | solution.py:236
  105.6 11.5 %forward_rows.4 = (bf16[768,384]{1,0:T(8,128)(2,1)}, bf16[768,384]{1,0:T(8,128)(2,1)}, bf16[768,384]{1,0:T(8,128)(2,1)}) custom-call(s32[1]{0:T(128)} %constant.69.clone.1.column_ref, bf16[384,5120]{1,0:T(8,128)(2,1)} %join_plane.4.refs_0_, bf16[384,5120]{1,0:T(8,128)(2,1)} %collective-permute-done.16.refs_1_.refs_3_, ...), custom_call_target="tpu_custom_call" | custom-call | flops 1 | bytes 1 | tf_op jit(solution)/shard_map/forward_rows/pallas_call | solution.py:196
  119.0 14.0 %collective-permute-done.18.refs_2_.refs_5_ = bf16[1,2,160,640]{3,2,1,0:T(8,128)(2,1)S(1)} collective-permute-done((bf16[1,2,160,640]{3,2,1,0:T(8,128)(2,1)S(1)}, bf16[1,2,160,640]{3,2,1,0:T(8,128)(2,1)S(1)}, u32[]{:S(2)}, u32[]{:S(2)}) %collective-permute-start.18) | collective-permute-done | bytes 409632 | tf_op jit(solution)/shard_map/ppermute | solution.py:760
  133.0 8.9 %collective-permute-done.19.refs_3_.refs_6_ = bf16[1,2,160,640]{3,2,1,0:T(8,128)(2,1)S(1)} collective-permute-done((bf16[1,2,160,640]{3,2,1,0:T(8,128)(2,1)}, bf16[1,2,160,640]{3,2,1,0:T(8,128)(2,1)S(1)}, u32[]{:S(2)}, u32[]{:S(2)}) %collective-permute-start.19) | collective-permute-done | bytes 409632 | tf_op jit(solution)/shard_map/ppermute | solution.py:760
  142.7 5.0 %lay_out_shadow.1 = (bf16[256,5120]{1,0:T(8,128)(2,1)}, bf16[512,5120]{1,0:T(8,128)(2,1)}) custom-call(s32[1]{0:T(128)} %bitcast.14.chip_ref, bf16[1,2,160,640]{3,2,1,0:T(8,128)(2,1)} %get-tuple-element.146.refs_0_.refs_3_, bf16[1,2,160,640]{3,2,1,0:T(8,128)(2,1)} %copy-done.15, ...), custom_call_target="tpu_custom_call", output_to_operand_aliasing={{1}: (5, {})} | custom-call | flops 1 | bytes 1 | tf_op jit(solution)/shard_map/lay_out_shadow/pallas_call | solution.py:306
  147.7 8.0 %forward_rows.5 = (bf16[1024,128]{1,0:T(8,128)(2,1)}, bf16[1024,128]{1,0:T(8,128)(2,1)}, bf16[1024,128]{1,0:T(8,128)(2,1)}) custom-call(s32[1]{0:T(128)} %constant.69.clone.1.column_ref, bf16[384,5120]{1,0:T(8,128)(2,1)} %join_plane.4.refs_0_, bf16[256,5120]{1,0:T(8,128)(2,1)} %join_plane.3.refs_0_.refs_1_.refs_5_, bf16[256,5120]{1,0:T(8,128)(2,1)} %copy-done, ...), custom_call_target="tpu_custom_call" | custom-call | flops 1 | bytes 1 | tf_op jit(solution)/shard_map/forward_rows/pallas_call | solution.py:196
  159.0 6.9 %output_other.1 = (bf16[256,5120]{1,0:T(8,128)(2,1)}, bf16[256,5120]{1,0:T(8,128)(2,1)}) custom-call(s32[1]{0:T(128)} %bitcast.column_ref, bf16[1024,512]{1,0:T(8,128)(2,1)} %get-tuple-element.93.refs_0_.refs_10_.refs_4_, bf16[512,5120]{1,0:T(8,128)(2,1)} %get-tuple-element.94.refs_1_.refs_3_), custom_call_target="tpu_custom_call" | custom-call | flops 1 | bytes 1 | tf_op jit(solution)/shard_map/output_other/pallas_call | solution.py:196
  165.9 4.7 %join_plane.5.refs_0_.refs_4_ = bf16[384,5120]{1,0:T(8,128)(2,1)} custom-call(s32[1]{0:T(128)} %bitcast.column_ref, bf16[384,1280]{1,0:T(8,128)(2,1)} %stack_pieces.5.refs_5_.refs_0_, bf16[384,1280]{1,0:T(8,128)(2,1)} %get-tuple-element.97.refs_1_, bf16[384,1280]{1,0:T(8,128)(2,1)} %get-tuple-element.98.refs_2_, bf16[384,1280]{1,0:T(8,128)(2,1)} %get-tuple-element.99.refs_3_), custom_call_target="tpu_custom_call" | custom-call | flops 1 | bytes 1 | tf_op jit(solution)/shard_map/join_plane/pallas_call | solution.py:236
  171.2 9.9 %backward_rows.2 = (bf16[640,768]{1,0:T(8,128)(2,1)}, bf16[640,256]{1,0:T(8,128)(2,1)}) custom-call(s32[1]{0:T(128)} %constant.69.clone.1.column_ref, bf16[384,5120]{1,0:T(8,128)(2,1)} %join_plane.5.refs_0_.refs_4_, bf16[256,5120]{1,0:T(8,128)(2,1)} %join_plane.3.refs_0_.refs_1_.refs_5_, bf16[256,5120]{1,0:T(8,128)(2,1)} %copy-done, ...), custom_call_target="tpu_custom_call" | custom-call | flops 1 | bytes 1 | tf_op jit(solution)/shard_map/backward_rows/pallas_call | solution.py:196
  181.1 4.1 %collective-permute-done.21.refs_3_ = bf16[256,5120]{1,0:T(8,128)(2,1)} collective-permute-done((bf16[256,5120]{1,0:T(8,128)(2,1)}, bf16[256,5120]{1,0:T(8,128)(2,1)}, u32[]{:S(2)}, u32[]{:S(2)}) %collective-permute-start.21) | collective-permute-done | bytes 2621472 | tf_op jit(solution)/shard_map/ppermute | solution.py:729
  185.3 10.1 %output_own.1 = (f32[256,1280]{1,0:T(8,128)}, bf16[256,1280]{1,0:T(8,128)(2,1)}, bf16[256,1280]{1,0:T(8,128)(2,1)}, bf16[256,1280]{1,0:T(8,128)(2,1)}, f32[256,1...) custom-call(s32[1]{0:T(128)} %bitcast.column_ref, ...), custom_call_target="tpu_custom_call" | custom-call | flops 1 | bytes 1 | tf_op jit(solution)/shard_map/output_own/pallas_call | solution.py:196
  200.8 7.7 %backward_rows.3 = (bf16[384,768]{1,0:T(8,128)(2,1)}, bf16[384,256]{1,0:T(8,128)(2,1)}) custom-call(s32[1]{0:T(128)} %constant.69.clone.1.column_ref, bf16[384,5120]{1,0:T(8,128)(2,1)} %copy-done.2, bf16[512,5120]{1,0:T(8,128)(2,1)} %get-tuple-element.94.refs_1_.refs_3_, bf16[768,384]{1,0:T(8,128)(2,1)} %get-tuple-element.100.refs_4_.refs_2_, ...), custom_call_target="tpu_custom_call" | custom-call | flops 1 | bytes 1 | tf_op jit(solution)/shard_map/backward_rows/pallas_call | solution.py:196
  208.5 11.1 %shadow_grads.1.refs_3_ = bf16[8,144,640]{2,1,0:T(8,128)(2,1)} custom-call(s32[1]{0:T(128)} %constant.69.clone.1.column_ref, bf16[384,5120]{1,0:T(8,128)(2,1)} %join_plane.4.refs_0_, bf16[256,5120]{1,0:T(8,128)(2,1)} %join_plane.3.refs_0_.refs_1_.refs_5_, bf16[256,5120]{1,0:T(8,128)(2,1)} %copy-done, ...), custom_call_target="tpu_custom_call" | custom-call | flops 1 | bytes 1 | tf_op jit(solution)/shard_map/shadow_grads/pallas_call | solution.py:196
  236.5 9.1 %down_grad.1.refs_5_ = bf16[384,5120]{1,0:T(8,128)(2,1)} custom-call(s32[1]{0:T(128)} %constant.69.clone.1.column_ref, bf16[384,5120]{1,0:T(8,128)(2,1)} %join_plane.5.refs_0_.refs_4_, bf16[256,5120]{1,0:T(8,128)(2,1)} %join_plane.3.refs_0_.refs_1_.refs_5_, bf16[256,5120]{1,0:T(8,128)(2,1)} %copy-done, bf16[384,5120]{1,0:T(8,128)(2,1)} %copy-done.2, ...), custom_call_target="tpu_custom_call" | custom-call | flops 1 | bytes 1 | tf_op jit(solution)/shard_map/down_grad/pallas_call | solution.py:196
  249.9 12.9 %input_grads.1 = (bf16[5120,384]{1,0:T(8,128)(2,1)}, bf16[5120,384]{1,0:T(8,128)(2,1)}) custom-call(s32[1]{0:T(128)} %constant.69.clone.1.column_ref, bf16[384,5120]{1,0:T(8,128)(2,1)} %join_plane.4.refs_0_, bf16[256,5120]{1,0:T(8,128)(2,1)} %join_plane.3.refs_0_.refs_1_.refs_5_, bf16[256,5120]{1,0:T(8,128)(2,1)} %copy-done, ...), custom_call_target="tpu_custom_call" | custom-call | flops 1 | bytes 1 | tf_op jit(solution)/shard_map/input_grads/pallas_call | solution.py:196
  268.0 19.2 %collective-permute-done.37 = bf16[128,1280]{1,0:T(8,128)(2,1)S(1)} collective-permute-done((bf16[128,1280]{1,0:T(8,128)(2,1)S(1)}, bf16[128,1280]{1,0:T(8,128)(2,1)S(1)}, u32[]{:S(2)}, u32[]{:S(2)}) %collective-permute-start.37) | collective-permute-done | bytes 327712 | tf_op jit(solution)/shard_map/ppermute | solution.py:884
  289.5 3.4 %collective-permute-done.38.refs_3_ = bf16[1,2,144,640]{3,2,1,0:T(8,128)(2,1)S(1)} collective-permute-done((bf16[1,2,144,640]{3,2,1,0:T(8,128)(2,1)}, bf16[1,2,144,640]{3,2,1,0:T(8,128)(2,1)S(1)}, u32[]{:S(2)}, u32[]{:S(2)}) %collective-permute-start.38) | collective-permute-done | bytes 368672 | tf_op jit(solution)/shard_map/ppermute | solution.py:760
  (182 shorter events, 93.8 us)
Async XLA Ops:
  2.6 16.8 %collective-permute-start = (bf16[256,1280]{1,0:T(8,128)(2,1)}, bf16[256,1280]{1,0:T(8,128)(2,1)S(1)}, u32[]{:S(2)}, u32[]{:S(2)}) collective-permute-start(bf16[256,1280]{1,0:T(8,128)(2,1)} %stack_pieces.3.refs_0_), channel_id=1, source_target_pairs={{0,8},{8,0},{16,24},{24,16},{1,9},{9,1},{17,25},{25,17},{2,10},{10... | collective-permute-start | bytes 1966088 | tf_op jit(solution)/shard_map/ppermute | solution.py:734
  4.1 16.4 %collective-permute-start.1 = (bf16[256,1280]{1,0:T(8,128)(2,1)}, bf16[256,1280]{1,0:T(8,128)(2,1)S(1)}, u32[]{:S(2)}, u32[]{:S(2)}) collective-permute-start(bf16[256,1280]{1,0:T(8,128)(2,1)} %stack_pieces.3.refs_0_), channel_id=1, source_target_pairs={{0,16},{8,24},{16,0},{24,8},{1,17},{9,25},{17,1},{25,9},{2,18},{10... | collective-permute-start | bytes 1966088 | tf_op jit(solution)/shard_map/ppermute | solution.py:734
  7.2 23.5 %collective-permute-start.5 = (bf16[128,1280]{1,0:T(8,128)(2,1)}, bf16[128,1280]{1,0:T(8,128)(2,1)S(1)}, u32[]{:S(2)}, u32[]{:S(2)}) collective-permute-start(bf16[128,1280]{1,0:T(8,128)(2,1)} %refs_0_.1), channel_id=1, source_target_pairs={{0,4},{1,5},{2,6},{3,7},{4,0},{5,1},{6,2},{7,3},{8,12},{9,13},{10,... | collective-permute-start | bytes 983048 | tf_op jit(solution)/shard_map/ppermute | solution.py:725
  7.5 29.5 %collective-permute-start.6 = (bf16[128,1280]{1,0:T(8,128)(2,1)}, bf16[128,1280]{1,0:T(8,128)(2,1)S(1)}, u32[]{:S(2)}, u32[]{:S(2)}) collective-permute-start(bf16[128,1280]{1,0:T(8,128)(2,1)} %refs_0_.1), channel_id=1, source_target_pairs={{0,6},{1,7},{2,4},{3,5},{4,2},{5,3},{6,0},{7,1},{8,14},{9,15},{10,... | collective-permute-start | bytes 983048 | tf_op jit(solution)/shard_map/ppermute | solution.py:725
  45.5 24.5 %collective-permute-start.8 = (bf16[384,1280]{1,0:T(8,128)(2,1)}, bf16[384,1280]{1,0:T(8,128)(2,1)}, u32[]{:S(2)}, u32[]{:S(2)}) collective-permute-start(bf16[384,1280]{1,0:T(8,128)(2,1)} %stack_pieces.4.refs_0_), channel_id=1, source_target_pairs={{0,8},{8,0},{16,24},{24,16},{1,9},{9,1},{17,25},{25,17},{2,10},{10... | collective-permute-start | bytes 2949128 | tf_op jit(solution)/shard_map/ppermute | solution.py:734
  46.0 24.2 %collective-permute-start.9 = (bf16[384,1280]{1,0:T(8,128)(2,1)}, bf16[384,1280]{1,0:T(8,128)(2,1)}, u32[]{:S(2)}, u32[]{:S(2)}) collective-permute-start(bf16[384,1280]{1,0:T(8,128)(2,1)} %stack_pieces.4.refs_0_), channel_id=1, source_target_pairs={{0,16},{8,24},{16,0},{24,8},{1,17},{9,25},{17,1},{25,9},{2,18},{10... | collective-permute-start | bytes 2949128 | tf_op jit(solution)/shard_map/ppermute | solution.py:734
  46.5 17.4 %collective-permute-start.10 = (bf16[128,1280]{1,0:T(8,128)(2,1)}, bf16[128,1280]{1,0:T(8,128)(2,1)}, u32[]{:S(2)}, u32[]{:S(2)}) collective-permute-start(bf16[128,1280]{1,0:T(8,128)(2,1)} %refs_1_.1), channel_id=1, source_target_pairs={{0,2},{1,3},{2,0},{3,1},{4,6},{5,7},{6,4},{7,5},{8,10},{9,11},{10,... | collective-permute-start | bytes 983048 | tf_op jit(solution)/shard_map/ppermute | solution.py:725
  46.5 17.4 %collective-permute-start.11 = (bf16[128,1280]{1,0:T(8,128)(2,1)}, bf16[128,1280]{1,0:T(8,128)(2,1)}, u32[]{:S(2)}, u32[]{:S(2)}) collective-permute-start(bf16[128,1280]{1,0:T(8,128)(2,1)} %refs_1_.1), channel_id=1, source_target_pairs={{0,4},{1,5},{2,6},{3,7},{4,0},{5,1},{6,2},{7,3},{8,12},{9,13},{10,... | collective-permute-start | bytes 983048 | tf_op jit(solution)/shard_map/ppermute | solution.py:725
  50.8 38.0 %collective-permute-start.14 = (bf16[4,160,640]{2,1,0:T(8,128)(2,1)}, bf16[4,160,640]{2,1,0:T(8,128)(2,1)S(1)}, u32[]{:S(2)}, u32[]{:S(2)}) collective-permute-start(bf16[4,160,640]{2,1,0:T(8,128)(2,1)} %select_bitcast_fusion), channel_id=1, source_target_pairs={{0,1},{1,0},{2,3},{3,2},{4,5},{5,4},{6,7},{7,6},{8,9},{9,8},{10,11... | collective-permute-start | bytes 2457608 | tf_op jit(solution)/shard_map/ppermute | solution.py:729
  71.3 17.5 %collective-permute-start.12 = (bf16[192,1280]{1,0:T(8,128)(2,1)S(1)}, bf16[192,1280]{1,0:T(8,128)(2,1)S(1)}, u32[]{:S(2)}, u32[]{:S(2)}) collective-permute-start(bf16[192,1280]{1,0:T(8,128)(2,1)S(1)} %slice.86), channel_id=1, source_target_pairs={{0,16},{8,24},{16,0},{24,8},{1,17},{9,25},{17,1},{25,9},{2,18},{10... | collective-permute-start | bytes 1474568 | tf_op jit(solution)/shard_map/ppermute | solution.py:740
  98.5 67.4 %collective-permute-start.22 = (bf16[384,1280]{1,0:T(8,128)(2,1)S(1)}, bf16[384,1280]{1,0:T(8,128)(2,1)}, u32[]{:S(2)}, u32[]{:S(2)}) collective-permute-start(bf16[384,1280]{1,0:T(8,128)(2,1)S(1)} %copy-done.4), channel_id=1, source_target_pairs={{0,8},{8,0},{16,24},{24,16},{1,9},{9,1},{17,25},{25,17},{2,10},{10... | collective-permute-start | bytes 2949128 | tf_op jit(solution)/shard_map/ppermute | solution.py:734
  99.2 66.7 %collective-permute-start.23 = (bf16[384,1280]{1,0:T(8,128)(2,1)S(1)}, bf16[384,1280]{1,0:T(8,128)(2,1)}, u32[]{:S(2)}, u32[]{:S(2)}) collective-permute-start(bf16[384,1280]{1,0:T(8,128)(2,1)S(1)} %copy-done.4), channel_id=1, source_target_pairs={{0,16},{8,24},{16,0},{24,8},{1,17},{9,25},{17,1},{25,9},{2,18},{10... | collective-permute-start | bytes 2949128 | tf_op jit(solution)/shard_map/ppermute | solution.py:734
  100.7 65.2 %collective-permute-start.24 = (bf16[384,1280]{1,0:T(8,128)(2,1)S(1)}, bf16[384,1280]{1,0:T(8,128)(2,1)}, u32[]{:S(2)}, u32[]{:S(2)}) collective-permute-start(bf16[384,1280]{1,0:T(8,128)(2,1)S(1)} %copy-done.4), channel_id=1, source_target_pairs={{0,24},{8,16},{16,8},{24,0},{1,25},{9,17},{17,9},{25,1},{2,26},{10... | collective-permute-start | bytes 2949128 | tf_op jit(solution)/shard_map/ppermute | solution.py:734
  105.6 27.4 %collective-permute-start.18 = (bf16[1,2,160,640]{3,2,1,0:T(8,128)(2,1)S(1)}, bf16[1,2,160,640]{3,2,1,0:T(8,128)(2,1)S(1)}, u32[]{:S(2)}, u32[]{:S(2)}) collective-permute-start(bf16[1,2,160,640]{3,2,1,0:T(8,128)(2,1)S(1)} %get-tuple-element.148), channel_id=1, source_target_pairs={{0,4},{1,5},{2,6},{3,7},{4,0},{5,1},{6,2},{7,3},{8,12},{9,13},{10,... | collective-permute-start | bytes 1228808 | tf_op jit(solution)/shard_map/ppermute | solution.py:760
  118.9 23.0 %collective-permute-start.19 = (bf16[1,2,160,640]{3,2,1,0:T(8,128)(2,1)}, bf16[1,2,160,640]{3,2,1,0:T(8,128)(2,1)S(1)}, u32[]{:S(2)}, u32[]{:S(2)}) collective-permute-start(bf16[1,2,160,640]{3,2,1,0:T(8,128)(2,1)} %after.15), channel_id=1, source_target_pairs={{0,6},{1,7},{2,4},{3,5},{4,2},{5,3},{6,0},{7,1},{8,14},{9,15},{10,... | collective-permute-start | bytes 1228808 | tf_op jit(solution)/shard_map/ppermute | solution.py:760
  170.6 28.2 %collective-permute-start.31 = (bf16[384,5120]{1,0:T(8,128)(2,1)}, bf16[384,5120]{1,0:T(8,128)(2,1)S(1)}, u32[]{:S(2)}, u32[]{:S(2)}) collective-permute-start(bf16[384,5120]{1,0:T(8,128)(2,1)} %join_plane.5.refs_0_.refs_4_), channel_id=1, source_target_pairs={{0,1},{1,0},{2,3},{3,2},{4,5},{5,4},{6,7},{7,6},{8,9},{9,8},{10,11... | collective-permute-start | bytes 11796488 | tf_op jit(solution)/shard_map/ppermute | solution.py:729
  195.4 27.1 %collective-permute-start.28 = (bf16[256,1280]{1,0:T(8,128)(2,1)}, bf16[256,1280]{1,0:T(8,128)(2,1)}, u32[]{:S(2)}, u32[]{:S(2)}) collective-permute-start(bf16[256,1280]{1,0:T(8,128)(2,1)} %get-tuple-element.114.refs_8_), channel_id=1, source_target_pairs={{0,8},{8,0},{16,24},{24,16},{1,9},{9,1},{17,25},{25,17},{2,10},{10... | collective-permute-start | bytes 1966088 | tf_op jit(solution)/shard_map/ppermute | solution.py:734
  195.9 30.1 %collective-permute-start.29 = (bf16[256,1280]{1,0:T(8,128)(2,1)}, bf16[256,1280]{1,0:T(8,128)(2,1)}, u32[]{:S(2)}, u32[]{:S(2)}) collective-permute-start(bf16[256,1280]{1,0:T(8,128)(2,1)} %get-tuple-element.115), channel_id=1, source_target_pairs={{0,16},{8,24},{16,0},{24,8},{1,17},{9,25},{17,1},{25,9},{2,18},{10... | collective-permute-start | bytes 1966088 | tf_op jit(solution)/shard_map/ppermute | solution.py:734
  197.5 31.2 %collective-permute-start.30 = (bf16[256,1280]{1,0:T(8,128)(2,1)}, bf16[256,1280]{1,0:T(8,128)(2,1)}, u32[]{:S(2)}, u32[]{:S(2)}) collective-permute-start(bf16[256,1280]{1,0:T(8,128)(2,1)} %get-tuple-element.116), channel_id=1, source_target_pairs={{0,24},{8,16},{16,8},{24,0},{1,25},{9,17},{17,9},{25,1},{2,26},{10... | collective-permute-start | bytes 1966088 | tf_op jit(solution)/shard_map/ppermute | solution.py:734
  221.9 40.9 %collective-permute-start.25 = (bf16[256,1280]{1,0:T(8,128)(2,1)}, bf16[256,1280]{1,0:T(8,128)(2,1)S(1)}, u32[]{:S(2)}, u32[]{:S(2)}) collective-permute-start(bf16[256,1280]{1,0:T(8,128)(2,1)} %get-tuple-element.110.refs_9_), channel_id=1, source_target_pairs={{0,8},{8,0},{16,24},{24,16},{1,9},{9,1},{17,25},{25,17},{2,10},{10... | collective-permute-start | bytes 1966088 | tf_op jit(solution)/shard_map/ppermute | solution.py:734
  222.5 40.3 %collective-permute-start.26 = (bf16[256,1280]{1,0:T(8,128)(2,1)}, bf16[256,1280]{1,0:T(8,128)(2,1)S(1)}, u32[]{:S(2)}, u32[]{:S(2)}) collective-permute-start(bf16[256,1280]{1,0:T(8,128)(2,1)} %get-tuple-element.111), channel_id=1, source_target_pairs={{0,16},{8,24},{16,0},{24,8},{1,17},{9,25},{17,1},{25,9},{2,18},{10... | collective-permute-start | bytes 1966088 | tf_op jit(solution)/shard_map/ppermute | solution.py:734
  226.0 36.8 %collective-permute-start.27 = (bf16[256,1280]{1,0:T(8,128)(2,1)}, bf16[256,1280]{1,0:T(8,128)(2,1)S(1)}, u32[]{:S(2)}, u32[]{:S(2)}) collective-permute-start(bf16[256,1280]{1,0:T(8,128)(2,1)} %get-tuple-element.112), channel_id=1, source_target_pairs={{0,24},{8,16},{16,8},{24,0},{1,25},{9,17},{17,9},{25,1},{2,26},{10... | collective-permute-start | bytes 1966088 | tf_op jit(solution)/shard_map/ppermute | solution.py:734
  265.9 21.2 %collective-permute-start.37 = (bf16[128,1280]{1,0:T(8,128)(2,1)S(1)}, bf16[128,1280]{1,0:T(8,128)(2,1)S(1)}, u32[]{:S(2)}, u32[]{:S(2)}) collective-permute-start(bf16[128,1280]{1,0:T(8,128)(2,1)S(1)} %add_convert_fusion.1), channel_id=1, source_target_pairs={{0,6},{1,7},{2,4},{3,5},{4,2},{5,3},{6,0},{7,1},{8,14},{9,15},{10,... | collective-permute-start | bytes 983048 | tf_op jit(solution)/shard_map/ppermute | solution.py:884
  266.6 26.4 %collective-permute-start.38 = (bf16[1,2,144,640]{3,2,1,0:T(8,128)(2,1)}, bf16[1,2,144,640]{3,2,1,0:T(8,128)(2,1)S(1)}, u32[]{:S(2)}, u32[]{:S(2)}) collective-permute-start(bf16[1,2,144,640]{3,2,1,0:T(8,128)(2,1)} %get-tuple-element.135), channel_id=1, source_target_pairs={{0,6},{1,7},{2,4},{3,5},{4,2},{5,3},{6,0},{7,1},{8,14},{9,15},{10,... | collective-permute-start | bytes 1105928 | tf_op jit(solution)/shard_map/ppermute | solution.py:760
  (52 other events, 387.0 us)

commit v5 on v4

--- a/solution.py
+++ b/solution.py
@@ -820,7 +820,7 @@
     hidden_near, slope_near, act_near = forward_rows(x_near, w_both, 2 * tile)
     spare_rows = -shadow_part % 128 + shadow_part
     down = jnp.pad(w_down[0], ((0, spare_rows), (0, 0)))
-    *x_plane, down = after([*x_plane, down], *dy_z[:2], hidden_near)
+    *x_plane, down = after([*x_plane, down], *dy_z, hidden_near)
     x_plane = [*x_plane, *send_diagonal(*x_plane)]
     (shadow_blocks,) = after([shadow_blocks], x_z[0])
     shadow_kept, shadow_taken = exchange_cores(shadow_blocks)

time: 300 us -> 307 us (1.023)
  waiting for transfers between devices: 87.2 us -> 92.2 us
  starting transfers between devices: 35.5 us -> 39.6 us
    ppermute x2, waiting for transfers between devices: 0.01 us -> 7.83 us  [send_diagonal(): lax.ppermute(from_x[:half], 'tp', across)]
    ppermute x6, starting transfers between devices: 4.45 us -> 9.91 us  [send_piece(): return lax.ppermute(piece, 'ep', swap_pairs(lax.axis_size('ep'), 2 * shift))]
    ppermute x13, waiting for transfers between devices: 9.43 us -> 5.78 us  [send_plane(): lax.ppermute(p, 'tp', swap_pairs(lax.axis_size('tp'), bit))]
    unnamed x74 -> x76, local copies, waits for them, and re-layouts: 9.92 us -> 9.23 us
  transfers between devices with their start and end apart: 39 -> 39, of which waited for: 16 -> 16; matrix products, arithmetic and copies ran while one was open for 12% -> 11% of each run, Pallas kernels for 35% -> 34%
where the time goes in v5:
time: 307 us; the launch traced here: 305 us
  Pallas kernels  127 us (41%)
  waiting for transfers between devices  92.2 us (30%)
  starting transfers between devices  39.6 us (13%)
  other arithmetic  23.8 us (8%)
  local copies, waits for them, and re-layouts  21.6 us (7%)
    pallas_call x10, Pallas kernels, kernel_call(): pl.pallas_call(run, out_shape=out_shape, grid_spec=pltpu.PrefetchScalarGr...  94.1 us
    ppermute x6, waiting for transfers between devices, send_piece(): return lax.ppermute(piece, 'ep', swap_pairs(lax.axis_size('ep'), 2 * shift))  27.7 us
    ppermute x6, waiting for transfers between devices, send_along_z(): lax.ppermute(own, 'ep', swap_pairs(ep_count, 2 * s))  22.6 us
    ppermute x3, waiting for transfers between devices, send_rows(): return lax.ppermute(piece, 'ep', swap_pairs(ep_count, 2 * (i + 1)))  21.7 us
    pallas_call x3, Pallas kernels, join_plane(): pl.pallas_call(body, out_shape=shape_of(rows, count * quarter), grid_spec...  14.1 us
    ppermute x13, starting transfers between devices, send_plane(): lax.ppermute(p, 'tp', swap_pairs(lax.axis_size('tp'), bit))  12.9 us
    ppermute x6, starting transfers between devices, send_piece(): return lax.ppermute(piece, 'ep', swap_pairs(lax.axis_size('ep'), 2 * shift))  9.91 us
    unnamed x76, local copies, waits for them, and re-layouts  9.23 us
  transfers between devices with their start and end apart: 39, of which 16 were waited for; matrix products, arithmetic and copies ran while one was open for 11% of the time, Pallas kernels for 34%

profile of v5, /device:TPU:16, one launch (start us, length us, event | category | flops | bytes accessed | tf_op | source)
XLA Modules:
  0.0 305.5 jit_solution(1262904596347598168)
XLA Ops:
  9.1 7.1 %pad_maximum_fusion.refs_5_.refs_2_ = bf16[5120,768]{1,0:T(8,128)(2,1)} fusion(bf16[5120,384]{1,0:T(8,128)(2,1)} %bitcast.98, bf16[5120,384]{1,0:T(8,128)(2,1)} %bitcast.99), kind=kLoop, calls=%fused_computation | loop fusion | flops 15728640 | bytes 15728640 | tf_op jit(solution)/shard_map/concatenate | solution.py:810
  30.7 6.3 %collective-permute-done.6.refs_4_ = bf16[128,1280]{1,0:T(8,128)(2,1)S(1)} collective-permute-done((bf16[128,1280]{1,0:T(8,128)(2,1)}, bf16[128,1280]{1,0:T(8,128)(2,1)S(1)}, u32[]{:S(2)}, u32[]{:S(2)}) %collective-permute-start.6) | collective-permute-done | bytes 327712 | tf_op jit(solution)/shard_map/ppermute | solution.py:725
  38.6 4.3 %join_plane.3.refs_0_.refs_1_.refs_5_ = bf16[256,5120]{1,0:T(8,128)(2,1)} custom-call(s32[1]{0:T(128)} %bitcast.column_ref, bf16[256,1280]{1,0:T(8,128)(2,1)} %stack_pieces.3.refs_0_, bf16[256,1280]{1,0:T(8,128)(2,1)} %get-tuple-element.73.refs_1_, bf16[256,1280]{1,0:T(8,128)(2,1)} %get-tuple-element.74.refs_2_, ...), custom_call_target="tpu_custom_call" | custom-call | flops 1 | bytes 1 | tf_op jit(solution)/shard_map/join_plane/pallas_call | solution.py:236
  48.4 11.5 %collective-permute-done.10.refs_3_ = bf16[128,1280]{1,0:T(8,128)(2,1)S(1)} collective-permute-done((bf16[128,1280]{1,0:T(8,128)(2,1)}, bf16[128,1280]{1,0:T(8,128)(2,1)S(1)}, u32[]{:S(2)}, u32[]{:S(2)}) %collective-permute-start.10) | collective-permute-done | bytes 327712 | tf_op jit(solution)/shard_map/ppermute | solution.py:725
  63.9 6.0 %pad.9.refs_2_ = bf16[512,5120]{1,0:T(8,128)(2,1)} pad(bf16[384,5120]{1,0:T(8,128)(2,1)} %bitcast.96, bf16[]{:T(256)} %constant.71.clone.1), padding=0_128x0_0 | pad | bytes 9175042 | tf_op jit(solution)/shard_map/jit(_pad)/pad | solution.py:822
  70.0 6.9 %forward_rows.3 = (bf16[256,384]{1,0:T(8,128)(2,1)}, bf16[256,384]{1,0:T(8,128)(2,1)}, bf16[256,384]{1,0:T(8,128)(2,1)}) custom-call(s32[1]{0:T(128)} %constant.69.clone.1.column_ref, bf16[256,5120]{1,0:T(8,128)(2,1)} %join_plane.3.refs_0_.refs_1_.refs_5_, bf16[256,5120]{1,0:T(8,128)(2,1)} %copy-done, bf16[5120,768]{1,0:T(8,128)(2,1)} %pad_maximum_fusion.refs_5_.refs_2_), custom_call_target="tpu_custom_call" | custom-call | flops 1 | bytes 1 | tf_op jit(solution)/shard_map/forward_rows/pallas_call | solution.py:196
  84.6 7.8 %collective-permute-done.13.refs_0_ = bf16[192,1280]{1,0:T(8,128)(2,1)S(1)} collective-permute-done((bf16[192,1280]{1,0:T(8,128)(2,1)S(1)}, bf16[192,1280]{1,0:T(8,128)(2,1)S(1)}, u32[]{:S(2)}, u32[]{:S(2)}) %collective-permute-start.13) | collective-permute-done | bytes 491552 | tf_op jit(solution)/shard_map/ppermute | solution.py:740
  98.4 5.1 %join_plane.4.refs_0_ = bf16[384,5120]{1,0:T(8,128)(2,1)} custom-call(s32[1]{0:T(128)} %bitcast.column_ref, bf16[384,1280]{1,0:T(8,128)(2,1)} %stack_pieces.4.refs_0_, bf16[384,1280]{1,0:T(8,128)(2,1)} %get-tuple-element.81.refs_1_, bf16[384,1280]{1,0:T(8,128)(2,1)} %get-tuple-element.82.refs_2_, bf16[192,1280]{1,0:T(8,128)(2,1)} %get-tuple-element.83.refs_3_, ...), custom_call_target="tpu_custom_call" | custom-call | flops 1 | bytes 1 | tf_op jit(solution)/shard_map/join_plane/pallas_call | solution.py:236
  112.8 11.5 %forward_rows.4 = (bf16[768,384]{1,0:T(8,128)(2,1)}, bf16[768,384]{1,0:T(8,128)(2,1)}, bf16[768,384]{1,0:T(8,128)(2,1)}) custom-call(s32[1]{0:T(128)} %constant.69.clone.1.column_ref, bf16[384,5120]{1,0:T(8,128)(2,1)} %join_plane.4.refs_0_, bf16[384,5120]{1,0:T(8,128)(2,1)} %collective-permute-done.16.refs_1_.refs_3_, ...), custom_call_target="tpu_custom_call" | custom-call | flops 1 | bytes 1 | tf_op jit(solution)/shard_map/forward_rows/pallas_call | solution.py:196
  126.0 14.3 %collective-permute-done.18.refs_2_.refs_5_ = bf16[1,2,160,640]{3,2,1,0:T(8,128)(2,1)S(1)} collective-permute-done((bf16[1,2,160,640]{3,2,1,0:T(8,128)(2,1)S(1)}, bf16[1,2,160,640]{3,2,1,0:T(8,128)(2,1)S(1)}, u32[]{:S(2)}, u32[]{:S(2)}) %collective-permute-start.18) | collective-permute-done | bytes 409632 | tf_op jit(solution)/shard_map/ppermute | solution.py:760
  140.3 10.0 %collective-permute-done.19.refs_3_.refs_6_ = bf16[1,2,160,640]{3,2,1,0:T(8,128)(2,1)S(1)} collective-permute-done((bf16[1,2,160,640]{3,2,1,0:T(8,128)(2,1)}, bf16[1,2,160,640]{3,2,1,0:T(8,128)(2,1)S(1)}, u32[]{:S(2)}, u32[]{:S(2)}) %collective-permute-start.19) | collective-permute-done | bytes 409632 | tf_op jit(solution)/shard_map/ppermute | solution.py:760
  151.0 4.9 %lay_out_shadow.1 = (bf16[256,5120]{1,0:T(8,128)(2,1)}, bf16[512,5120]{1,0:T(8,128)(2,1)}) custom-call(s32[1]{0:T(128)} %bitcast.14.chip_ref, bf16[1,2,160,640]{3,2,1,0:T(8,128)(2,1)} %get-tuple-element.146.refs_0_.refs_3_, bf16[1,2,160,640]{3,2,1,0:T(8,128)(2,1)} %copy-done.17, ...), custom_call_target="tpu_custom_call", output_to_operand_aliasing={{1}: (5, {})} | custom-call | flops 1 | bytes 1 | tf_op jit(solution)/shard_map/lay_out_shadow/pallas_call | solution.py:306
  155.9 8.0 %forward_rows.5 = (bf16[1024,128]{1,0:T(8,128)(2,1)}, bf16[1024,128]{1,0:T(8,128)(2,1)}, bf16[1024,128]{1,0:T(8,128)(2,1)}) custom-call(s32[1]{0:T(128)} %constant.69.clone.1.column_ref, bf16[384,5120]{1,0:T(8,128)(2,1)} %join_plane.4.refs_0_, bf16[256,5120]{1,0:T(8,128)(2,1)} %join_plane.3.refs_0_.refs_1_.refs_5_, bf16[256,5120]{1,0:T(8,128)(2,1)} %copy-done, ...), custom_call_target="tpu_custom_call" | custom-call | flops 1 | bytes 1 | tf_op jit(solution)/shard_map/forward_rows/pallas_call | solution.py:196
  167.3 6.9 %output_other.1 = (bf16[256,5120]{1,0:T(8,128)(2,1)}, bf16[256,5120]{1,0:T(8,128)(2,1)}) custom-call(s32[1]{0:T(128)} %bitcast.column_ref, bf16[1024,512]{1,0:T(8,128)(2,1)} %get-tuple-element.93.refs_0_.refs_10_.refs_4_, bf16[512,5120]{1,0:T(8,128)(2,1)} %get-tuple-element.94.refs_1_.refs_3_), custom_call_target="tpu_custom_call" | custom-call | flops 1 | bytes 1 | tf_op jit(solution)/shard_map/output_other/pallas_call | solution.py:196
  174.2 4.7 %join_plane.5.refs_0_.refs_4_ = bf16[384,5120]{1,0:T(8,128)(2,1)} custom-call(s32[1]{0:T(128)} %bitcast.column_ref, bf16[384,1280]{1,0:T(8,128)(2,1)} %stack_pieces.5.refs_5_.refs_0_, bf16[384,1280]{1,0:T(8,128)(2,1)} %get-tuple-element.97.refs_1_, bf16[384,1280]{1,0:T(8,128)(2,1)} %get-tuple-element.98.refs_2_, bf16[384,1280]{1,0:T(8,128)(2,1)} %get-tuple-element.99.refs_3_), custom_call_target="tpu_custom_call" | custom-call | flops 1 | bytes 1 | tf_op jit(solution)/shard_map/join_plane/pallas_call | solution.py:236
  179.4 9.9 %backward_rows.2 = (bf16[640,768]{1,0:T(8,128)(2,1)}, bf16[640,256]{1,0:T(8,128)(2,1)}) custom-call(s32[1]{0:T(128)} %constant.69.clone.1.column_ref, bf16[384,5120]{1,0:T(8,128)(2,1)} %join_plane.5.refs_0_.refs_4_, bf16[256,5120]{1,0:T(8,128)(2,1)} %join_plane.3.refs_0_.refs_1_.refs_5_, bf16[256,5120]{1,0:T(8,128)(2,1)} %copy-done, ...), custom_call_target="tpu_custom_call" | custom-call | flops 1 | bytes 1 | tf_op jit(solution)/shard_map/backward_rows/pallas_call | solution.py:196
  189.4 4.1 %collective-permute-done.21.refs_3_ = bf16[256,5120]{1,0:T(8,128)(2,1)} collective-permute-done((bf16[256,5120]{1,0:T(8,128)(2,1)}, bf16[256,5120]{1,0:T(8,128)(2,1)}, u32[]{:S(2)}, u32[]{:S(2)}) %collective-permute-start.21) | collective-permute-done | bytes 2621472 | tf_op jit(solution)/shard_map/ppermute | solution.py:729
  193.5 10.1 %output_own.1 = (f32[256,1280]{1,0:T(8,128)}, bf16[256,1280]{1,0:T(8,128)(2,1)}, bf16[256,1280]{1,0:T(8,128)(2,1)}, bf16[256,1280]{1,0:T(8,128)(2,1)}, f32[256,1...) custom-call(s32[1]{0:T(128)} %bitcast.column_ref, ...), custom_call_target="tpu_custom_call" | custom-call | flops 1 | bytes 1 | tf_op jit(solution)/shard_map/output_own/pallas_call | solution.py:196
  209.0 7.7 %backward_rows.3 = (bf16[384,768]{1,0:T(8,128)(2,1)}, bf16[384,256]{1,0:T(8,128)(2,1)}) custom-call(s32[1]{0:T(128)} %constant.69.clone.1.column_ref, bf16[384,5120]{1,0:T(8,128)(2,1)} %copy-done.2, bf16[512,5120]{1,0:T(8,128)(2,1)} %get-tuple-element.94.refs_1_.refs_3_, bf16[768,384]{1,0:T(8,128)(2,1)} %get-tuple-element.100.refs_4_.refs_2_, ...), custom_call_target="tpu_custom_call" | custom-call | flops 1 | bytes 1 | tf_op jit(solution)/shard_map/backward_rows/pallas_call | solution.py:196
  216.7 11.1 %shadow_grads.1.refs_3_ = bf16[8,144,640]{2,1,0:T(8,128)(2,1)} custom-call(s32[1]{0:T(128)} %constant.69.clone.1.column_ref, bf16[384,5120]{1,0:T(8,128)(2,1)} %join_plane.4.refs_0_, bf16[256,5120]{1,0:T(8,128)(2,1)} %join_plane.3.refs_0_.refs_1_.refs_5_, bf16[256,5120]{1,0:T(8,128)(2,1)} %copy-done, ...), custom_call_target="tpu_custom_call" | custom-call | flops 1 | bytes 1 | tf_op jit(solution)/shard_map/shadow_grads/pallas_call | solution.py:196
  232.1 4.7 %collective-permute-done.29.refs_1_ = bf16[256,1280]{1,0:T(8,128)(2,1)} collective-permute-done((bf16[256,1280]{1,0:T(8,128)(2,1)}, bf16[256,1280]{1,0:T(8,128)(2,1)}, u32[]{:S(2)}, u32[]{:S(2)}) %collective-permute-start.29) | collective-permute-done | bytes 655392 | tf_op jit(solution)/shard_map/ppermute | solution.py:734
  243.2 9.1 %down_grad.1.refs_5_ = bf16[384,5120]{1,0:T(8,128)(2,1)} custom-call(s32[1]{0:T(128)} %constant.69.clone.1.column_ref, bf16[384,5120]{1,0:T(8,128)(2,1)} %join_plane.5.refs_0_.refs_4_, bf16[256,5120]{1,0:T(8,128)(2,1)} %join_plane.3.refs_0_.refs_1_.refs_5_, bf16[256,5120]{1,0:T(8,128)(2,1)} %copy-done, bf16[384,5120]{1,0:T(8,128)(2,1)} %copy-done.2, ...), custom_call_target="tpu_custom_call" | custom-call | flops 1 | bytes 1 | tf_op jit(solution)/shard_map/down_grad/pallas_call | solution.py:196
  256.8 12.9 %input_grads.1 = (bf16[5120,384]{1,0:T(8,128)(2,1)}, bf16[5120,384]{1,0:T(8,128)(2,1)}) custom-call(s32[1]{0:T(128)} %constant.69.clone.1.column_ref, bf16[384,5120]{1,0:T(8,128)(2,1)} %join_plane.4.refs_0_, bf16[256,5120]{1,0:T(8,128)(2,1)} %join_plane.3.refs_0_.refs_1_.refs_5_, bf16[256,5120]{1,0:T(8,128)(2,1)} %copy-done, ...), custom_call_target="tpu_custom_call" | custom-call | flops 1 | bytes 1 | tf_op jit(solution)/shard_map/input_grads/pallas_call | solution.py:196
  274.9 20.9 %collective-permute-done.37 = bf16[128,1280]{1,0:T(8,128)(2,1)S(1)} collective-permute-done((bf16[128,1280]{1,0:T(8,128)(2,1)S(1)}, bf16[128,1280]{1,0:T(8,128)(2,1)S(1)}, u32[]{:S(2)}, u32[]{:S(2)}) %collective-permute-start.37) | collective-permute-done | bytes 327712 | tf_op jit(solution)/shard_map/ppermute | solution.py:884
  (184 shorter events, 98.6 us)
Async XLA Ops:
  2.6 16.8 %collective-permute-start = (bf16[256,1280]{1,0:T(8,128)(2,1)}, bf16[256,1280]{1,0:T(8,128)(2,1)S(1)}, u32[]{:S(2)}, u32[]{:S(2)}) collective-permute-start(bf16[256,1280]{1,0:T(8,128)(2,1)} %stack_pieces.3.refs_0_), channel_id=1, source_target_pairs={{0,8},{8,0},{16,24},{24,16},{1,9},{9,1},{17,25},{25,17},{2,10},{10... | collective-permute-start | bytes 1966088 | tf_op jit(solution)/shard_map/ppermute | solution.py:734
  4.1 16.4 %collective-permute-start.1 = (bf16[256,1280]{1,0:T(8,128)(2,1)}, bf16[256,1280]{1,0:T(8,128)(2,1)S(1)}, u32[]{:S(2)}, u32[]{:S(2)}) collective-permute-start(bf16[256,1280]{1,0:T(8,128)(2,1)} %stack_pieces.3.refs_0_), channel_id=1, source_target_pairs={{0,16},{8,24},{16,0},{24,8},{1,17},{9,25},{17,1},{25,9},{2,18},{10... | collective-permute-start | bytes 1966088 | tf_op jit(solution)/shard_map/ppermute | solution.py:734
  7.2 23.5 %collective-permute-start.5 = (bf16[128,1280]{1,0:T(8,128)(2,1)}, bf16[128,1280]{1,0:T(8,128)(2,1)S(1)}, u32[]{:S(2)}, u32[]{:S(2)}) collective-permute-start(bf16[128,1280]{1,0:T(8,128)(2,1)} %refs_0_.1), channel_id=1, source_target_pairs={{0,4},{1,5},{2,6},{3,7},{4,0},{5,1},{6,2},{7,3},{8,12},{9,13},{10,... | collective-permute-start | bytes 983048 | tf_op jit(solution)/shard_map/ppermute | solution.py:725
  7.5 29.5 %collective-permute-start.6 = (bf16[128,1280]{1,0:T(8,128)(2,1)}, bf16[128,1280]{1,0:T(8,128)(2,1)S(1)}, u32[]{:S(2)}, u32[]{:S(2)}) collective-permute-start(bf16[128,1280]{1,0:T(8,128)(2,1)} %refs_0_.1), channel_id=1, source_target_pairs={{0,6},{1,7},{2,4},{3,5},{4,2},{5,3},{6,0},{7,1},{8,14},{9,15},{10,... | collective-permute-start | bytes 983048 | tf_op jit(solution)/shard_map/ppermute | solution.py:725
  42.8 21.0 %collective-permute-start.7 = (bf16[256,5120]{1,0:T(8,128)(2,1)}, bf16[256,5120]{1,0:T(8,128)(2,1)S(1)}, u32[]{:S(2)}, u32[]{:S(2)}) collective-permute-start(bf16[256,5120]{1,0:T(8,128)(2,1)} %join_plane.3.refs_0_.refs_1_.refs_5_), channel_id=1, source_target_pairs={{0,1},{1,0},{2,3},{3,2},{4,5},{5,4},{6,7},{7,6},{8,9},{9,8},{10,11... | collective-permute-start | bytes 7864328 | tf_op jit(solution)/shard_map/ppermute | solution.py:729
  45.5 33.0 %collective-permute-start.8 = (bf16[384,1280]{1,0:T(8,128)(2,1)}, bf16[384,1280]{1,0:T(8,128)(2,1)}, u32[]{:S(2)}, u32[]{:S(2)}) collective-permute-start(bf16[384,1280]{1,0:T(8,128)(2,1)} %stack_pieces.4.refs_0_), channel_id=1, source_target_pairs={{0,8},{8,0},{16,24},{24,16},{1,9},{9,1},{17,25},{25,17},{2,10},{10... | collective-permute-start | bytes 2949128 | tf_op jit(solution)/shard_map/ppermute | solution.py:734
  46.0 32.5 %collective-permute-start.9 = (bf16[384,1280]{1,0:T(8,128)(2,1)}, bf16[384,1280]{1,0:T(8,128)(2,1)}, u32[]{:S(2)}, u32[]{:S(2)}) collective-permute-start(bf16[384,1280]{1,0:T(8,128)(2,1)} %stack_pieces.4.refs_0_), channel_id=1, source_target_pairs={{0,16},{8,24},{16,0},{24,8},{1,17},{9,25},{17,1},{25,9},{2,18},{10... | collective-permute-start | bytes 2949128 | tf_op jit(solution)/shard_map/ppermute | solution.py:734
  46.5 30.4 %collective-permute-start.11 = (bf16[128,1280]{1,0:T(8,128)(2,1)}, bf16[128,1280]{1,0:T(8,128)(2,1)}, u32[]{:S(2)}, u32[]{:S(2)}) collective-permute-start(bf16[128,1280]{1,0:T(8,128)(2,1)} %refs_1_.1), channel_id=1, source_target_pairs={{0,4},{1,5},{2,6},{3,7},{4,0},{5,1},{6,2},{7,3},{8,12},{9,13},{10,... | collective-permute-start | bytes 983048 | tf_op jit(solution)/shard_map/ppermute | solution.py:725
  59.9 18.6 %collective-permute-start.12 = (bf16[128,1280]{1,0:T(8,128)(2,1)}, bf16[128,1280]{1,0:T(8,128)(2,1)S(1)}, u32[]{:S(2)}, u32[]{:S(2)}) collective-permute-start(bf16[128,1280]{1,0:T(8,128)(2,1)} %refs_1_.1), channel_id=1, source_target_pairs={{0,6},{1,7},{2,4},{3,5},{4,2},{5,3},{6,0},{7,1},{8,14},{9,15},{10,... | collective-permute-start | bytes 983048 | tf_op jit(solution)/shard_map/ppermute | solution.py:725
  63.9 20.8 %collective-permute-start.15 = (bf16[4,160,640]{2,1,0:T(8,128)(2,1)}, bf16[4,160,640]{2,1,0:T(8,128)(2,1)S(1)}, u32[]{:S(2)}, u32[]{:S(2)}) collective-permute-start(bf16[4,160,640]{2,1,0:T(8,128)(2,1)} %select_bitcast_fusion), channel_id=1, source_target_pairs={{0,1},{1,0},{2,3},{3,2},{4,5},{5,4},{6,7},{7,6},{8,9},{9,8},{10,11... | collective-permute-start | bytes 2457608 | tf_op jit(solution)/shard_map/ppermute | solution.py:729
  103.5 70.7 %collective-permute-start.22 = (bf16[384,1280]{1,0:T(8,128)(2,1)S(1)}, bf16[384,1280]{1,0:T(8,128)(2,1)}, u32[]{:S(2)}, u32[]{:S(2)}) collective-permute-start(bf16[384,1280]{1,0:T(8,128)(2,1)S(1)} %copy-done.4), channel_id=1, source_target_pairs={{0,8},{8,0},{16,24},{24,16},{1,9},{9,1},{17,25},{25,17},{2,10},{10... | collective-permute-start | bytes 2949128 | tf_op jit(solution)/shard_map/ppermute | solution.py:734
  105.0 69.1 %collective-permute-start.23 = (bf16[384,1280]{1,0:T(8,128)(2,1)S(1)}, bf16[384,1280]{1,0:T(8,128)(2,1)}, u32[]{:S(2)}, u32[]{:S(2)}) collective-permute-start(bf16[384,1280]{1,0:T(8,128)(2,1)S(1)} %copy-done.4), channel_id=1, source_target_pairs={{0,16},{8,24},{16,0},{24,8},{1,17},{9,25},{17,1},{25,9},{2,18},{10... | collective-permute-start | bytes 2949128 | tf_op jit(solution)/shard_map/ppermute | solution.py:734
  105.5 68.7 %collective-permute-start.24 = (bf16[384,1280]{1,0:T(8,128)(2,1)S(1)}, bf16[384,1280]{1,0:T(8,128)(2,1)}, u32[]{:S(2)}, u32[]{:S(2)}) collective-permute-start(bf16[384,1280]{1,0:T(8,128)(2,1)S(1)} %copy-done.4), channel_id=1, source_target_pairs={{0,24},{8,16},{16,8},{24,0},{1,25},{9,17},{17,9},{25,1},{2,26},{10... | collective-permute-start | bytes 2949128 | tf_op jit(solution)/shard_map/ppermute | solution.py:734
  110.7 29.6 %collective-permute-start.18 = (bf16[1,2,160,640]{3,2,1,0:T(8,128)(2,1)S(1)}, bf16[1,2,160,640]{3,2,1,0:T(8,128)(2,1)S(1)}, u32[]{:S(2)}, u32[]{:S(2)}) collective-permute-start(bf16[1,2,160,640]{3,2,1,0:T(8,128)(2,1)S(1)} %get-tuple-element.148), channel_id=1, source_target_pairs={{0,4},{1,5},{2,6},{3,7},{4,0},{5,1},{6,2},{7,3},{8,12},{9,13},{10,... | collective-permute-start | bytes 1228808 | tf_op jit(solution)/shard_map/ppermute | solution.py:760
  124.3 25.9 %collective-permute-start.19 = (bf16[1,2,160,640]{3,2,1,0:T(8,128)(2,1)}, bf16[1,2,160,640]{3,2,1,0:T(8,128)(2,1)S(1)}, u32[]{:S(2)}, u32[]{:S(2)}) collective-permute-start(bf16[1,2,160,640]{3,2,1,0:T(8,128)(2,1)} %after.15), channel_id=1, source_target_pairs={{0,6},{1,7},{2,4},{3,5},{4,2},{5,3},{6,0},{7,1},{8,14},{9,15},{10,... | collective-permute-start | bytes 1228808 | tf_op jit(solution)/shard_map/ppermute | solution.py:760
  178.9 28.2 %collective-permute-start.31 = (bf16[384,5120]{1,0:T(8,128)(2,1)}, bf16[384,5120]{1,0:T(8,128)(2,1)S(1)}, u32[]{:S(2)}, u32[]{:S(2)}) collective-permute-start(bf16[384,5120]{1,0:T(8,128)(2,1)} %join_plane.5.refs_0_.refs_4_), channel_id=1, source_target_pairs={{0,1},{1,0},{2,3},{3,2},{4,5},{5,4},{6,7},{7,6},{8,9},{9,8},{10,11... | collective-permute-start | bytes 11796488 | tf_op jit(solution)/shard_map/ppermute | solution.py:729
  203.6 28.1 %collective-permute-start.28 = (bf16[256,1280]{1,0:T(8,128)(2,1)}, bf16[256,1280]{1,0:T(8,128)(2,1)}, u32[]{:S(2)}, u32[]{:S(2)}) collective-permute-start(bf16[256,1280]{1,0:T(8,128)(2,1)} %get-tuple-element.114.refs_8_), channel_id=1, source_target_pairs={{0,8},{8,0},{16,24},{24,16},{1,9},{9,1},{17,25},{25,17},{2,10},{10... | collective-permute-start | bytes 1966088 | tf_op jit(solution)/shard_map/ppermute | solution.py:734
  205.1 31.6 %collective-permute-start.29 = (bf16[256,1280]{1,0:T(8,128)(2,1)}, bf16[256,1280]{1,0:T(8,128)(2,1)}, u32[]{:S(2)}, u32[]{:S(2)}) collective-permute-start(bf16[256,1280]{1,0:T(8,128)(2,1)} %get-tuple-element.115), channel_id=1, source_target_pairs={{0,16},{8,24},{16,0},{24,8},{1,17},{9,25},{17,1},{25,9},{2,18},{10... | collective-permute-start | bytes 1966088 | tf_op jit(solution)/shard_map/ppermute | solution.py:734
  205.5 31.3 %collective-permute-start.30 = (bf16[256,1280]{1,0:T(8,128)(2,1)}, bf16[256,1280]{1,0:T(8,128)(2,1)}, u32[]{:S(2)}, u32[]{:S(2)}) collective-permute-start(bf16[256,1280]{1,0:T(8,128)(2,1)} %get-tuple-element.116), channel_id=1, source_target_pairs={{0,24},{8,16},{16,8},{24,0},{1,25},{9,17},{17,9},{25,1},{2,26},{10... | collective-permute-start | bytes 1966088 | tf_op jit(solution)/shard_map/ppermute | solution.py:734
  230.2 39.5 %collective-permute-start.25 = (bf16[256,1280]{1,0:T(8,128)(2,1)}, bf16[256,1280]{1,0:T(8,128)(2,1)S(1)}, u32[]{:S(2)}, u32[]{:S(2)}) collective-permute-start(bf16[256,1280]{1,0:T(8,128)(2,1)} %get-tuple-element.110.refs_9_), channel_id=1, source_target_pairs={{0,8},{8,0},{16,24},{24,16},{1,9},{9,1},{17,25},{25,17},{2,10},{10... | collective-permute-start | bytes 1966088 | tf_op jit(solution)/shard_map/ppermute | solution.py:734
  231.7 38.0 %collective-permute-start.26 = (bf16[256,1280]{1,0:T(8,128)(2,1)}, bf16[256,1280]{1,0:T(8,128)(2,1)S(1)}, u32[]{:S(2)}, u32[]{:S(2)}) collective-permute-start(bf16[256,1280]{1,0:T(8,128)(2,1)} %get-tuple-element.111), channel_id=1, source_target_pairs={{0,16},{8,24},{16,0},{24,8},{1,17},{9,25},{17,1},{25,9},{2,18},{10... | collective-permute-start | bytes 1966088 | tf_op jit(solution)/shard_map/ppermute | solution.py:734
  236.8 32.9 %collective-permute-start.27 = (bf16[256,1280]{1,0:T(8,128)(2,1)}, bf16[256,1280]{1,0:T(8,128)(2,1)S(1)}, u32[]{:S(2)}, u32[]{:S(2)}) collective-permute-start(bf16[256,1280]{1,0:T(8,128)(2,1)} %get-tuple-element.112), channel_id=1, source_target_pairs={{0,24},{8,16},{16,8},{24,0},{1,25},{9,17},{17,9},{25,1},{2,26},{10... | collective-permute-start | bytes 1966088 | tf_op jit(solution)/shard_map/ppermute | solution.py:734
  272.8 23.0 %collective-permute-start.37 = (bf16[128,1280]{1,0:T(8,128)(2,1)S(1)}, bf16[128,1280]{1,0:T(8,128)(2,1)S(1)}, u32[]{:S(2)}, u32[]{:S(2)}) collective-permute-start(bf16[128,1280]{1,0:T(8,128)(2,1)S(1)} %add_convert_fusion.1), channel_id=1, source_target_pairs={{0,6},{1,7},{2,4},{3,5},{4,2},{5,3},{6,0},{7,1},{8,14},{9,15},{10,... | collective-permute-start | bytes 983048 | tf_op jit(solution)/shard_map/ppermute | solution.py:884
  274.1 27.2 %collective-permute-start.38 = (bf16[1,2,144,640]{3,2,1,0:T(8,128)(2,1)}, bf16[1,2,144,640]{3,2,1,0:T(8,128)(2,1)S(1)}, u32[]{:S(2)}, u32[]{:S(2)}) collective-permute-start(bf16[1,2,144,640]{3,2,1,0:T(8,128)(2,1)} %get-tuple-element.135), channel_id=1, source_target_pairs={{0,6},{1,7},{2,4},{3,5},{4,2},{5,3},{6,0},{7,1},{8,14},{9,15},{10,... | collective-permute-start | bytes 1105928 | tf_op jit(solution)/shard_map/ppermute | solution.py:760
  (53 other events, 398.9 us)

commit v6 on v3

--- a/solution.py
+++ b/solution.py
@@ -820,26 +820,25 @@
     hidden_near, slope_near, act_near = forward_rows(x_near, w_both, 2 * tile)
     spare_rows = -shadow_part % 128 + shadow_part
     down = jnp.pad(w_down[0], ((0, spare_rows), (0, 0)))
-    *x_plane, down = after([*x_plane, down], *dy_z[:2], hidden_near)
-    x_plane = [*x_plane, *send_diagonal(*x_plane)]
     (shadow_blocks,) = after([shadow_blocks], x_z[0])
     shadow_kept, shadow_taken = exchange_cores(shadow_blocks)
     shadow_pieces = chip_pieces(shadow_kept, shadow_taken)
-    shadow_pieces[1] = send_piece(shadow_pieces[1], 1)
+    shadow_pieces[-1] = send_piece(shadow_pieces[-1], steps - 1)
+    fenced = after([*x_plane, down, *shadow_pieces[1:]], *dy_z[:2], hidden_near)
+    x_plane, down, shadow_pieces[1:] = fenced[:2], fenced[2], fenced[3:]
+    x_plane = [*x_plane, *send_diagonal(*x_plane)]
     fenced = after([*x_plane[2:], *shadow_pieces[1:], *dy_z])
     x_plane[2:], shadow_pieces[1:], dy_z = fenced[:2], fenced[2 : 1 + steps], fenced[1 + steps :]
 
     dy_piece = stack_pieces(dy_z)
     dy_plane = send_plane(dy_piece)
-    for shift in range(2, steps - 1):
+    for shift in range(1, steps - 1):
         shadow_pieces[shift] = send_piece(shadow_pieces[shift], shift)
     x_own = join_plane(tp_index, x_piece, *x_plane, earlier=[dy_piece])
     x_other = swap_cores(x_own)
     x_far = [(x_own, 0, later), (x_other, 0, later)]
     x_groups = [x_far[0], x_near[0], x_near[1], x_far[1]]
     hidden_far, slope_far, act_far = forward_rows(x_far, w_both, 2 * tile)
-    shadow_pieces[-1:] = after(shadow_pieces[-1:], hidden_far)
-    shadow_pieces[-1] = send_piece(shadow_pieces[-1], steps - 1)
     chip = ep_index // 2
     shadow_in, down = lay_out_shadow(shadow_pieces, down, shadow_part, chip, earlier=[hidden_far])
     hidden_s, slope_s, act_s = forward_rows(x_groups, shadow_in, 2 * tile, transposed=True)

time: 302 us -> 298 us (0.987)
  waiting for transfers between devices: 78.6 us -> 86.3 us
  starting transfers between devices: 44.4 us -> 37.4 us
  local copies, waits for them, and re-layouts: 24.4 us -> 19.8 us
    ppermute x6, waiting for transfers between devices: 18.4 us -> 40.2 us  [send_along_z(): lax.ppermute(own, 'ep', swap_pairs(ep_count, 2 * s))]
    ppermute x6, waiting for transfers between devices: 27.7 us -> 9.26 us  [send_piece(): return lax.ppermute(piece, 'ep', swap_pairs(lax.axis_size('ep'), 2 * shift))]
    ppermute x6, starting transfers between devices: 11.4 us -> 5.32 us  [send_piece(): return lax.ppermute(piece, 'ep', swap_pairs(lax.axis_size('ep'), 2 * shift))]
    ppermute x13, starting transfers between devices: 17.8 us -> 12.6 us  [send_plane(): lax.ppermute(p, 'tp', swap_pairs(lax.axis_size('tp'), bit))]
    ppermute x7, waiting for transfers between devices: 4.16 us -> 7.71 us  [swap_cores(): return lax.ppermute(block, 'ep', swap_pairs(lax.axis_size('ep'), 1))]
    ppermute x6, starting transfers between devices: 5.89 us -> 9.14 us  [send_along_z(): lax.ppermute(own, 'ep', swap_pairs(ep_count, 2 * s))]
    unnamed x72 -> x70, local copies, waits for them, and re-layouts: 12.7 us -> 10.4 us
  transfers between devices with their start and end apart: 39 -> 39, of which waited for: 14 -> 16; matrix products, arithmetic and copies ran while one was open for 12% -> 11% of each run, Pallas kernels for 35% -> 35%
where the time goes in v6:
time: 298 us; the launch traced here: 297 us
  Pallas kernels  127 us (43%)
  waiting for transfers between devices  86.3 us (29%)
  starting transfers between devices  37.4 us (13%)
  other arithmetic  25.6 us (9%)
  local copies, waits for them, and re-layouts  19.8 us (7%)
    pallas_call x10, Pallas kernels, kernel_call(): pl.pallas_call(run, out_shape=out_shape, grid_spec=pltpu.PrefetchScalarGr...  94.1 us
    ppermute x6, waiting for transfers between devices, send_along_z(): lax.ppermute(own, 'ep', swap_pairs(ep_count, 2 * s))  40.2 us
    ppermute x3, waiting for transfers between devices, send_rows(): return lax.ppermute(piece, 'ep', swap_pairs(ep_count, 2 * (i + 1)))  23.8 us
    pallas_call x3, Pallas kernels, join_plane(): pl.pallas_call(body, out_shape=shape_of(rows, count * quarter), grid_spec...  13.7 us
    ppermute x13, starting transfers between devices, send_plane(): lax.ppermute(p, 'tp', swap_pairs(lax.axis_size('tp'), bit))  12.6 us
    unnamed x70, local copies, waits for them, and re-layouts  10.4 us
    ppermute x6, waiting for transfers between devices, send_piece(): return lax.ppermute(piece, 'ep', swap_pairs(lax.axis_size('ep'), 2 * shift))  9.26 us
    ppermute x6, starting transfers between devices, send_along_z(): lax.ppermute(own, 'ep', swap_pairs(ep_count, 2 * s))  9.14 us
  transfers between devices with their start and end apart: 39, of which 16 were waited for; matrix products, arithmetic and copies ran while one was open for 11% of the time, Pallas kernels for 35%

profile of v6, /device:TPU:16, one launch (start us, length us, event | category | flops | bytes accessed | tf_op | source)
XLA Modules:
  0.0 296.9 jit_solution(8850559657139970863)
XLA Ops:
  9.1 7.2 %pad_maximum_fusion.refs_5_.refs_2_ = bf16[5120,768]{1,0:T(8,128)(2,1)} fusion(bf16[5120,384]{1,0:T(8,128)(2,1)} %bitcast.98, bf16[5120,384]{1,0:T(8,128)(2,1)} %bitcast.99), kind=kLoop, calls=%fused_computation | loop fusion | flops 15728640 | bytes 15728640 | tf_op jit(solution)/shard_map/concatenate | solution.py:810
  30.7 6.3 %collective-permute-done.6.refs_4_ = bf16[128,1280]{1,0:T(8,128)(2,1)S(1)} collective-permute-done((bf16[128,1280]{1,0:T(8,128)(2,1)}, bf16[128,1280]{1,0:T(8,128)(2,1)S(1)}, u32[]{:S(2)}, u32[]{:S(2)}) %collective-permute-start.6) | collective-permute-done | bytes 327712 | tf_op jit(solution)/shard_map/ppermute | solution.py:725
  38.6 4.3 %join_plane.3.refs_0_.refs_1_.refs_5_ = bf16[256,5120]{1,0:T(8,128)(2,1)} custom-call(s32[1]{0:T(128)} %bitcast.column_ref, bf16[256,1280]{1,0:T(8,128)(2,1)} %stack_pieces.3.refs_0_, bf16[256,1280]{1,0:T(8,128)(2,1)} %get-tuple-element.78.refs_1_, bf16[256,1280]{1,0:T(8,128)(2,1)} %get-tuple-element.79.refs_2_, ...), custom_call_target="tpu_custom_call" | custom-call | flops 1 | bytes 1 | tf_op jit(solution)/shard_map/join_plane/pallas_call | solution.py:236
  58.8 6.9 %forward_rows.3 = (bf16[256,384]{1,0:T(8,128)(2,1)}, bf16[256,384]{1,0:T(8,128)(2,1)}, bf16[256,384]{1,0:T(8,128)(2,1)}) custom-call(s32[1]{0:T(128)} %constant.69.clone.1.column_ref, bf16[256,5120]{1,0:T(8,128)(2,1)} %join_plane.3.refs_0_.refs_1_.refs_5_, bf16[256,5120]{1,0:T(8,128)(2,1)} %copy-done, bf16[5120,768]{1,0:T(8,128)(2,1)} %pad_maximum_fusion.refs_5_.refs_2_), custom_call_target="tpu_custom_call" | custom-call | flops 1 | bytes 1 | tf_op jit(solution)/shard_map/forward_rows/pallas_call | solution.py:196
  68.6 13.3 %collective-permute-done.13.refs_7_.refs_6_ = bf16[128,1280]{1,0:T(8,128)(2,1)S(1)} collective-permute-done((bf16[128,1280]{1,0:T(8,128)(2,1)}, bf16[128,1280]{1,0:T(8,128)(2,1)S(1)}, u32[]{:S(2)}, u32[]{:S(2)}) %collective-permute-start.13) | collective-permute-done | bytes 327712 | tf_op jit(solution)/shard_map/ppermute | solution.py:725
  90.0 14.6 %collective-permute-done.16.refs_7_ = bf16[128,1280]{1,0:T(8,128)(2,1)S(1)} collective-permute-done((bf16[128,1280]{1,0:T(8,128)(2,1)}, bf16[128,1280]{1,0:T(8,128)(2,1)S(1)}, u32[]{:S(2)}, u32[]{:S(2)}) %collective-permute-start.16) | collective-permute-done | bytes 327712 | tf_op jit(solution)/shard_map/ppermute | solution.py:725
  108.3 4.7 %join_plane.4.refs_0_ = bf16[384,5120]{1,0:T(8,128)(2,1)} custom-call(s32[1]{0:T(128)} %bitcast.column_ref, bf16[384,1280]{1,0:T(8,128)(2,1)} %stack_pieces.4.refs_0_, bf16[384,1280]{1,0:T(8,128)(2,1)} %get-tuple-element.86.refs_1_, bf16[384,1280]{1,0:T(8,128)(2,1)} %get-tuple-element.87.refs_2_, bf16[192,1280]{1,0:T(8,128)(2,1)} %get-tuple-element.91.refs_3_, ...), custom_call_target="tpu_custom_call" | custom-call | flops 1 | bytes 1 | tf_op jit(solution)/shard_map/join_plane/pallas_call | solution.py:236
  116.5 3.5 %collective-permute-done.17.refs_1_.refs_3_ = bf16[384,5120]{1,0:T(8,128)(2,1)S(1)} collective-permute-done((bf16[384,5120]{1,0:T(8,128)(2,1)}, bf16[384,5120]{1,0:T(8,128)(2,1)S(1)}, u32[]{:S(2)}, u32[]{:S(2)}) %collective-permute-start.17) | collective-permute-done | bytes 3932192 | tf_op jit(solution)/shard_map/ppermute | solution.py:729
  121.9 11.5 %forward_rows.4 = (bf16[768,384]{1,0:T(8,128)(2,1)}, bf16[768,384]{1,0:T(8,128)(2,1)}, bf16[768,384]{1,0:T(8,128)(2,1)}) custom-call(s32[1]{0:T(128)} %constant.69.clone.1.column_ref, bf16[384,5120]{1,0:T(8,128)(2,1)} %join_plane.4.refs_0_, bf16[384,5120]{1,0:T(8,128)(2,1)} %copy-done.1, bf16[5120,768]{1,0:T(8,128)(2,1)} %pad_maximum_fusion.refs_5_.refs_2_), custom_call_target="tpu_custom_call" | custom-call | flops 1 | bytes 1 | tf_op jit(solution)/shard_map/forward_rows/pallas_call | solution.py:196
  133.4 5.1 %collective-permute-done.19.refs_2_.refs_5_ = bf16[1,2,160,640]{3,2,1,0:T(8,128)(2,1)} collective-permute-done((bf16[1,2,160,640]{3,2,1,0:T(8,128)(2,1)}, bf16[1,2,160,640]{3,2,1,0:T(8,128)(2,1)}, u32[]{:S(2)}, u32[]{:S(2)}) %collective-permute-start.19) | collective-permute-done | bytes 409632 | tf_op jit(solution)/shard_map/ppermute | solution.py:760
  138.5 5.0 %lay_out_shadow.1 = (bf16[256,5120]{1,0:T(8,128)(2,1)}, bf16[512,5120]{1,0:T(8,128)(2,1)}) custom-call(s32[1]{0:T(128)} %bitcast.18.chip_ref, bf16[1,2,160,640]{3,2,1,0:T(8,128)(2,1)} %get-tuple-element.155.refs_0_.refs_3_, bf16[1,2,160,640]{3,2,1,0:T(8,128)(2,1)} %collective-permute-done.18.refs_1_.refs_4_, ...), custom_call_target="tpu_custom_call", output_to_operand_aliasing={{1}: (5, {})} | custom-call | flops 1 | bytes 1 | tf_op jit(solution)/shard_map/lay_out_shadow/pallas_call | solution.py:306
  143.4 8.0 %forward_rows.5 = (bf16[1024,128]{1,0:T(8,128)(2,1)}, bf16[1024,128]{1,0:T(8,128)(2,1)}, bf16[1024,128]{1,0:T(8,128)(2,1)}) custom-call(s32[1]{0:T(128)} %constant.69.clone.1.column_ref, bf16[384,5120]{1,0:T(8,128)(2,1)} %join_plane.4.refs_0_, bf16[256,5120]{1,0:T(8,128)(2,1)} %join_plane.3.refs_0_.refs_1_.refs_5_, bf16[256,5120]{1,0:T(8,128)(2,1)} %copy-done, ...), custom_call_target="tpu_custom_call" | custom-call | flops 1 | bytes 1 | tf_op jit(solution)/shard_map/forward_rows/pallas_call | solution.py:196
  154.8 6.9 %output_other.1 = (bf16[256,5120]{1,0:T(8,128)(2,1)}, bf16[256,5120]{1,0:T(8,128)(2,1)}) custom-call(s32[1]{0:T(128)} %bitcast.column_ref, bf16[1024,512]{1,0:T(8,128)(2,1)} %get-tuple-element.103.refs_0_.refs_10_.refs_4_, bf16[512,5120]{1,0:T(8,128)(2,1)} %get-tuple-element.104.refs_1_.refs_3_), custom_call_target="tpu_custom_call" | custom-call | flops 1 | bytes 1 | tf_op jit(solution)/shard_map/output_other/pallas_call | solution.py:196
  161.8 4.7 %join_plane.5.refs_0_.refs_4_ = bf16[384,5120]{1,0:T(8,128)(2,1)} custom-call(s32[1]{0:T(128)} %bitcast.column_ref, bf16[384,1280]{1,0:T(8,128)(2,1)} %stack_pieces.5.refs_5_.refs_0_, bf16[384,1280]{1,0:T(8,128)(2,1)} %get-tuple-element.107.refs_1_, bf16[384,1280]{1,0:T(8,128)(2,1)} %get-tuple-element.108.refs_2_, bf16[384,1280]{1,0:T(8,128)(2,1)} %get-tuple-element.109.refs_3_), custom_call_target="tpu_custom_call" | custom-call | flops 1 | bytes 1 | tf_op jit(solution)/shard_map/join_plane/pallas_call | solution.py:236
  167.0 9.9 %backward_rows.2 = (bf16[640,768]{1,0:T(8,128)(2,1)}, bf16[640,256]{1,0:T(8,128)(2,1)}) custom-call(s32[1]{0:T(128)} %constant.69.clone.1.column_ref, bf16[384,5120]{1,0:T(8,128)(2,1)} %join_plane.5.refs_0_.refs_4_, bf16[256,5120]{1,0:T(8,128)(2,1)} %join_plane.3.refs_0_.refs_1_.refs_5_, bf16[256,5120]{1,0:T(8,128)(2,1)} %copy-done, ...), custom_call_target="tpu_custom_call" | custom-call | flops 1 | bytes 1 | tf_op jit(solution)/shard_map/backward_rows/pallas_call | solution.py:196
  177.0 4.1 %collective-permute-done.21.refs_3_ = bf16[256,5120]{1,0:T(8,128)(2,1)} collective-permute-done((bf16[256,5120]{1,0:T(8,128)(2,1)}, bf16[256,5120]{1,0:T(8,128)(2,1)}, u32[]{:S(2)}, u32[]{:S(2)}) %collective-permute-start.21) | collective-permute-done | bytes 2621472 | tf_op jit(solution)/shard_map/ppermute | solution.py:729
  181.1 10.1 %output_own.1 = (f32[256,1280]{1,0:T(8,128)}, bf16[256,1280]{1,0:T(8,128)(2,1)}, bf16[256,1280]{1,0:T(8,128)(2,1)}, bf16[256,1280]{1,0:T(8,128)(2,1)}, f32[256,1...) custom-call(s32[1]{0:T(128)} %bitcast.column_ref, ...), custom_call_target="tpu_custom_call" | custom-call | flops 1 | bytes 1 | tf_op jit(solution)/shard_map/output_own/pallas_call | solution.py:196
  196.6 7.7 %backward_rows.3 = (bf16[384,768]{1,0:T(8,128)(2,1)}, bf16[384,256]{1,0:T(8,128)(2,1)}) custom-call(s32[1]{0:T(128)} %constant.69.clone.1.column_ref, bf16[384,5120]{1,0:T(8,128)(2,1)} %copy-done.2, bf16[512,5120]{1,0:T(8,128)(2,1)} %get-tuple-element.104.refs_1_.refs_3_, bf16[768,384]{1,0:T(8,128)(2,1)} %get-tuple-element.110.refs_4_.refs_2_, ...), custom_call_target="tpu_custom_call" | custom-call | flops 1 | bytes 1 | tf_op jit(solution)/shard_map/backward_rows/pallas_call | solution.py:196
  204.3 11.1 %shadow_grads.1.refs_3_ = bf16[8,144,640]{2,1,0:T(8,128)(2,1)} custom-call(s32[1]{0:T(128)} %constant.69.clone.1.column_ref, bf16[384,5120]{1,0:T(8,128)(2,1)} %join_plane.4.refs_0_, bf16[256,5120]{1,0:T(8,128)(2,1)} %join_plane.3.refs_0_.refs_1_.refs_5_, bf16[256,5120]{1,0:T(8,128)(2,1)} %copy-done, bf16[384,5120]{1,0:T(8,128)(2,1)} %copy-done.1, ...), custom_call_target="tpu_custom_call" | custom-call | flops 1 | bytes 1 | tf_op jit(solution)/shard_map/shadow_grads/pallas_call | solution.py:196
  219.5 4.2 %collective-permute-done.29.refs_1_ = bf16[256,1280]{1,0:T(8,128)(2,1)} collective-permute-done((bf16[256,1280]{1,0:T(8,128)(2,1)}, bf16[256,1280]{1,0:T(8,128)(2,1)}, u32[]{:S(2)}, u32[]{:S(2)}) %collective-permute-start.29) | collective-permute-done | bytes 655392 | tf_op jit(solution)/shard_map/ppermute | solution.py:734
  225.7 3.7 %collective-permute-start.32 = (bf16[128,1280]{1,0:T(8,128)(2,1)S(1)}, bf16[128,1280]{1,0:T(8,128)(2,1)S(1)}, u32[]{:S(2)}, u32[]{:S(2)}) collective-permute-start(bf16[128,1280]{1,0:T(8,128)(2,1)S(1)} %get-tuple-element.150.refs_5_), channel_id=1, source_target_pairs={{0,2},{1,3},{2,0},{3,1},{4,6},{5,7},{6,4},{7,5},{8,10},{9,11},{10,... | collective-permute-start | bytes 983048 | tf_op jit(solution)/shard_map/ppermute | solution.py:884
  231.9 9.1 %down_grad.1.refs_5_ = bf16[384,5120]{1,0:T(8,128)(2,1)} custom-call(s32[1]{0:T(128)} %constant.69.clone.1.column_ref, bf16[384,5120]{1,0:T(8,128)(2,1)} %join_plane.5.refs_0_.refs_4_, bf16[256,5120]{1,0:T(8,128)(2,1)} %join_plane.3.refs_0_.refs_1_.refs_5_, bf16[256,5120]{1,0:T(8,128)(2,1)} %copy-done, bf16[384,5120]{1,0:T(8,128)(2,1)} %copy-done.2, ...), custom_call_target="tpu_custom_call" | custom-call | flops 1 | bytes 1 | tf_op jit(solution)/shard_map/down_grad/pallas_call | solution.py:196
  246.5 12.9 %input_grads.1 = (bf16[5120,384]{1,0:T(8,128)(2,1)}, bf16[5120,384]{1,0:T(8,128)(2,1)}) custom-call(s32[1]{0:T(128)} %constant.69.clone.1.column_ref, bf16[384,5120]{1,0:T(8,128)(2,1)} %join_plane.4.refs_0_, bf16[256,5120]{1,0:T(8,128)(2,1)} %join_plane.3.refs_0_.refs_1_.refs_5_, bf16[256,5120]{1,0:T(8,128)(2,1)} %copy-done, bf16[384,5120]{1,0:T(8,128)(2,1)} %copy-done.1, ...), custom_call_target="tpu_custom_call" | custom-call | flops 1 | bytes 1 | tf_op jit(solution)/shard_map/input_grads/pallas_call | solution.py:196
  265.5 22.2 %collective-permute-done.37 = bf16[128,1280]{1,0:T(8,128)(2,1)S(1)} collective-permute-done((bf16[128,1280]{1,0:T(8,128)(2,1)S(1)}, bf16[128,1280]{1,0:T(8,128)(2,1)S(1)}, u32[]{:S(2)}, u32[]{:S(2)}) %collective-permute-start.37) | collective-permute-done | bytes 327712 | tf_op jit(solution)/shard_map/ppermute | solution.py:884
  (177 shorter events, 99.0 us)
Async XLA Ops:
  2.6 16.8 %collective-permute-start = (bf16[256,1280]{1,0:T(8,128)(2,1)}, bf16[256,1280]{1,0:T(8,128)(2,1)S(1)}, u32[]{:S(2)}, u32[]{:S(2)}) collective-permute-start(bf16[256,1280]{1,0:T(8,128)(2,1)} %stack_pieces.3.refs_0_), channel_id=1, source_target_pairs={{0,8},{8,0},{16,24},{24,16},{1,9},{9,1},{17,25},{25,17},{2,10},{10... | collective-permute-start | bytes 1966088 | tf_op jit(solution)/shard_map/ppermute | solution.py:734
  7.2 23.5 %collective-permute-start.5 = (bf16[128,1280]{1,0:T(8,128)(2,1)}, bf16[128,1280]{1,0:T(8,128)(2,1)S(1)}, u32[]{:S(2)}, u32[]{:S(2)}) collective-permute-start(bf16[128,1280]{1,0:T(8,128)(2,1)} %refs_0_.1), channel_id=1, source_target_pairs={{0,4},{1,5},{2,6},{3,7},{4,0},{5,1},{6,2},{7,3},{8,12},{9,13},{10,... | collective-permute-start | bytes 983048 | tf_op jit(solution)/shard_map/ppermute | solution.py:725
  7.5 29.5 %collective-permute-start.6 = (bf16[128,1280]{1,0:T(8,128)(2,1)}, bf16[128,1280]{1,0:T(8,128)(2,1)S(1)}, u32[]{:S(2)}, u32[]{:S(2)}) collective-permute-start(bf16[128,1280]{1,0:T(8,128)(2,1)} %refs_0_.1), channel_id=1, source_target_pairs={{0,6},{1,7},{2,4},{3,5},{4,2},{5,3},{6,0},{7,1},{8,14},{9,15},{10,... | collective-permute-start | bytes 983048 | tf_op jit(solution)/shard_map/ppermute | solution.py:725
  48.4 33.6 %collective-permute-start.8 = (bf16[384,1280]{1,0:T(8,128)(2,1)}, bf16[384,1280]{1,0:T(8,128)(2,1)}, u32[]{:S(2)}, u32[]{:S(2)}) collective-permute-start(bf16[384,1280]{1,0:T(8,128)(2,1)} %stack_pieces.4.refs_0_), channel_id=1, source_target_pairs={{0,8},{8,0},{16,24},{24,16},{1,9},{9,1},{17,25},{25,17},{2,10},{10... | collective-permute-start | bytes 2949128 | tf_op jit(solution)/shard_map/ppermute | solution.py:734
  48.9 33.1 %collective-permute-start.9 = (bf16[384,1280]{1,0:T(8,128)(2,1)}, bf16[384,1280]{1,0:T(8,128)(2,1)}, u32[]{:S(2)}, u32[]{:S(2)}) collective-permute-start(bf16[384,1280]{1,0:T(8,128)(2,1)} %stack_pieces.4.refs_0_), channel_id=1, source_target_pairs={{0,16},{8,24},{16,0},{24,8},{1,17},{9,25},{17,1},{25,9},{2,18},{10... | collective-permute-start | bytes 2949128 | tf_op jit(solution)/shard_map/ppermute | solution.py:734
  52.3 29.7 %collective-permute-start.11 = (bf16[1,2,160,640]{3,2,1,0:T(8,128)(2,1)}, bf16[1,2,160,640]{3,2,1,0:T(8,128)(2,1)S(1)}, u32[]{:S(2)}, u32[]{:S(2)}) collective-permute-start(bf16[1,2,160,640]{3,2,1,0:T(8,128)(2,1)} %get-tuple-element.158), channel_id=1, source_target_pairs={{0,6},{1,7},{2,4},{3,5},{4,2},{5,3},{6,0},{7,1},{8,14},{9,15},{10,... | collective-permute-start | bytes 1228808 | tf_op jit(solution)/shard_map/ppermute | solution.py:760
  52.7 29.2 %collective-permute-start.13 = (bf16[128,1280]{1,0:T(8,128)(2,1)}, bf16[128,1280]{1,0:T(8,128)(2,1)S(1)}, u32[]{:S(2)}, u32[]{:S(2)}) collective-permute-start(bf16[128,1280]{1,0:T(8,128)(2,1)} %refs_1_.1), channel_id=1, source_target_pairs={{0,4},{1,5},{2,6},{3,7},{4,0},{5,1},{6,2},{7,3},{8,12},{9,13},{10,... | collective-permute-start | bytes 983048 | tf_op jit(solution)/shard_map/ppermute | solution.py:725
  83.9 20.6 %collective-permute-start.14 = (bf16[192,1280]{1,0:T(8,128)(2,1)S(1)}, bf16[192,1280]{1,0:T(8,128)(2,1)S(1)}, u32[]{:S(2)}, u32[]{:S(2)}) collective-permute-start(bf16[192,1280]{1,0:T(8,128)(2,1)S(1)} %slice.88), channel_id=1, source_target_pairs={{0,16},{8,24},{16,0},{24,8},{1,17},{9,25},{17,1},{25,9},{2,18},{10... | collective-permute-start | bytes 1474568 | tf_op jit(solution)/shard_map/ppermute | solution.py:740
  86.6 17.9 %collective-permute-start.15 = (bf16[192,1280]{1,0:T(8,128)(2,1)S(1)}, bf16[192,1280]{1,0:T(8,128)(2,1)S(1)}, u32[]{:S(2)}, u32[]{:S(2)}) collective-permute-start(bf16[192,1280]{1,0:T(8,128)(2,1)S(1)} %slice.89), channel_id=1, source_target_pairs={{0,8},{8,0},{16,24},{24,16},{1,9},{9,1},{17,25},{25,17},{2,10},{10... | collective-permute-start | bytes 1474568 | tf_op jit(solution)/shard_map/ppermute | solution.py:740
  87.4 17.2 %collective-permute-start.16 = (bf16[128,1280]{1,0:T(8,128)(2,1)}, bf16[128,1280]{1,0:T(8,128)(2,1)S(1)}, u32[]{:S(2)}, u32[]{:S(2)}) collective-permute-start(bf16[128,1280]{1,0:T(8,128)(2,1)} %refs_1_.1), channel_id=1, source_target_pairs={{0,6},{1,7},{2,4},{3,5},{4,2},{5,3},{6,0},{7,1},{8,14},{9,15},{10,... | collective-permute-start | bytes 983048 | tf_op jit(solution)/shard_map/ppermute | solution.py:725
  113.0 48.7 %collective-permute-start.22 = (bf16[384,1280]{1,0:T(8,128)(2,1)}, bf16[384,1280]{1,0:T(8,128)(2,1)}, u32[]{:S(2)}, u32[]{:S(2)}) collective-permute-start(bf16[384,1280]{1,0:T(8,128)(2,1)} %stack_pieces.5.refs_5_.refs_0_), channel_id=1, source_target_pairs={{0,8},{8,0},{16,24},{24,16},{1,9},{9,1},{17,25},{25,17},{2,10},{10... | collective-permute-start | bytes 2949128 | tf_op jit(solution)/shard_map/ppermute | solution.py:734
  114.4 47.4 %collective-permute-start.23 = (bf16[384,1280]{1,0:T(8,128)(2,1)}, bf16[384,1280]{1,0:T(8,128)(2,1)}, u32[]{:S(2)}, u32[]{:S(2)}) collective-permute-start(bf16[384,1280]{1,0:T(8,128)(2,1)} %stack_pieces.5.refs_5_.refs_0_), channel_id=1, source_target_pairs={{0,16},{8,24},{16,0},{24,8},{1,17},{9,25},{17,1},{25,9},{2,18},{10... | collective-permute-start | bytes 2949128 | tf_op jit(solution)/shard_map/ppermute | solution.py:734
  114.8 47.0 %collective-permute-start.24 = (bf16[384,1280]{1,0:T(8,128)(2,1)}, bf16[384,1280]{1,0:T(8,128)(2,1)}, u32[]{:S(2)}, u32[]{:S(2)}) collective-permute-start(bf16[384,1280]{1,0:T(8,128)(2,1)} %stack_pieces.5.refs_5_.refs_0_), channel_id=1, source_target_pairs={{0,24},{8,16},{16,8},{24,0},{1,25},{9,17},{17,9},{25,1},{2,26},{10... | collective-permute-start | bytes 2949128 | tf_op jit(solution)/shard_map/ppermute | solution.py:734
  116.5 16.9 %collective-permute-start.18 = (bf16[1,2,160,640]{3,2,1,0:T(8,128)(2,1)}, bf16[1,2,160,640]{3,2,1,0:T(8,128)(2,1)}, u32[]{:S(2)}, u32[]{:S(2)}) collective-permute-start(bf16[1,2,160,640]{3,2,1,0:T(8,128)(2,1)} %get-tuple-element.97), channel_id=1, source_target_pairs={{0,2},{1,3},{2,0},{3,1},{4,6},{5,7},{6,4},{7,5},{8,10},{9,11},{10,... | collective-permute-start | bytes 1228808 | tf_op jit(solution)/shard_map/ppermute | solution.py:760
  120.0 18.4 %collective-permute-start.19 = (bf16[1,2,160,640]{3,2,1,0:T(8,128)(2,1)}, bf16[1,2,160,640]{3,2,1,0:T(8,128)(2,1)}, u32[]{:S(2)}, u32[]{:S(2)}) collective-permute-start(bf16[1,2,160,640]{3,2,1,0:T(8,128)(2,1)} %get-tuple-element.98), channel_id=1, source_target_pairs={{0,4},{1,5},{2,6},{3,7},{4,0},{5,1},{6,2},{7,3},{8,12},{9,13},{10,... | collective-permute-start | bytes 1228808 | tf_op jit(solution)/shard_map/ppermute | solution.py:760
  166.5 28.2 %collective-permute-start.31 = (bf16[384,5120]{1,0:T(8,128)(2,1)}, bf16[384,5120]{1,0:T(8,128)(2,1)S(1)}, u32[]{:S(2)}, u32[]{:S(2)}) collective-permute-start(bf16[384,5120]{1,0:T(8,128)(2,1)} %join_plane.5.refs_0_.refs_4_), channel_id=1, source_target_pairs={{0,1},{1,0},{2,3},{3,2},{4,5},{5,4},{6,7},{7,6},{8,9},{9,8},{10,11... | collective-permute-start | bytes 11796488 | tf_op jit(solution)/shard_map/ppermute | solution.py:729
  191.2 28.0 %collective-permute-start.28 = (bf16[256,1280]{1,0:T(8,128)(2,1)}, bf16[256,1280]{1,0:T(8,128)(2,1)}, u32[]{:S(2)}, u32[]{:S(2)}) collective-permute-start(bf16[256,1280]{1,0:T(8,128)(2,1)} %get-tuple-element.124.refs_8_), channel_id=1, source_target_pairs={{0,8},{8,0},{16,24},{24,16},{1,9},{9,1},{17,25},{25,17},{2,10},{10... | collective-permute-start | bytes 1966088 | tf_op jit(solution)/shard_map/ppermute | solution.py:734
  192.6 31.1 %collective-permute-start.29 = (bf16[256,1280]{1,0:T(8,128)(2,1)}, bf16[256,1280]{1,0:T(8,128)(2,1)}, u32[]{:S(2)}, u32[]{:S(2)}) collective-permute-start(bf16[256,1280]{1,0:T(8,128)(2,1)} %get-tuple-element.125), channel_id=1, source_target_pairs={{0,16},{8,24},{16,0},{24,8},{1,17},{9,25},{17,1},{25,9},{2,18},{10... | collective-permute-start | bytes 1966088 | tf_op jit(solution)/shard_map/ppermute | solution.py:734
  192.9 30.9 %collective-permute-start.30 = (bf16[256,1280]{1,0:T(8,128)(2,1)}, bf16[256,1280]{1,0:T(8,128)(2,1)}, u32[]{:S(2)}, u32[]{:S(2)}) collective-permute-start(bf16[256,1280]{1,0:T(8,128)(2,1)} %get-tuple-element.126), channel_id=1, source_target_pairs={{0,24},{8,16},{16,8},{24,0},{1,25},{9,17},{17,9},{25,1},{2,26},{10... | collective-permute-start | bytes 1966088 | tf_op jit(solution)/shard_map/ppermute | solution.py:734
  217.8 41.6 %collective-permute-start.25 = (bf16[256,1280]{1,0:T(8,128)(2,1)}, bf16[256,1280]{1,0:T(8,128)(2,1)S(1)}, u32[]{:S(2)}, u32[]{:S(2)}) collective-permute-start(bf16[256,1280]{1,0:T(8,128)(2,1)} %get-tuple-element.120.refs_9_), channel_id=1, source_target_pairs={{0,8},{8,0},{16,24},{24,16},{1,9},{9,1},{17,25},{25,17},{2,10},{10... | collective-permute-start | bytes 1966088 | tf_op jit(solution)/shard_map/ppermute | solution.py:734
  219.2 40.3 %collective-permute-start.26 = (bf16[256,1280]{1,0:T(8,128)(2,1)}, bf16[256,1280]{1,0:T(8,128)(2,1)S(1)}, u32[]{:S(2)}, u32[]{:S(2)}) collective-permute-start(bf16[256,1280]{1,0:T(8,128)(2,1)} %get-tuple-element.121), channel_id=1, source_target_pairs={{0,16},{8,24},{16,0},{24,8},{1,17},{9,25},{17,1},{25,9},{2,18},{10... | collective-permute-start | bytes 1966088 | tf_op jit(solution)/shard_map/ppermute | solution.py:734
  223.7 35.8 %collective-permute-start.27 = (bf16[256,1280]{1,0:T(8,128)(2,1)}, bf16[256,1280]{1,0:T(8,128)(2,1)S(1)}, u32[]{:S(2)}, u32[]{:S(2)}) collective-permute-start(bf16[256,1280]{1,0:T(8,128)(2,1)} %get-tuple-element.122), channel_id=1, source_target_pairs={{0,24},{8,16},{16,8},{24,0},{1,25},{9,17},{17,9},{25,1},{2,26},{10... | collective-permute-start | bytes 1966088 | tf_op jit(solution)/shard_map/ppermute | solution.py:734
  263.4 24.3 %collective-permute-start.37 = (bf16[128,1280]{1,0:T(8,128)(2,1)S(1)}, bf16[128,1280]{1,0:T(8,128)(2,1)S(1)}, u32[]{:S(2)}, u32[]{:S(2)}) collective-permute-start(bf16[128,1280]{1,0:T(8,128)(2,1)S(1)} %add_convert_fusion.1), channel_id=1, source_target_pairs={{0,6},{1,7},{2,4},{3,5},{4,2},{5,3},{6,0},{7,1},{8,14},{9,15},{10,... | collective-permute-start | bytes 983048 | tf_op jit(solution)/shard_map/ppermute | solution.py:884
  263.8 28.9 %collective-permute-start.38 = (bf16[1,2,144,640]{3,2,1,0:T(8,128)(2,1)}, bf16[1,2,144,640]{3,2,1,0:T(8,128)(2,1)S(1)}, u32[]{:S(2)}, u32[]{:S(2)}) collective-permute-start(bf16[1,2,144,640]{3,2,1,0:T(8,128)(2,1)} %get-tuple-element.145), channel_id=1, source_target_pairs={{0,6},{1,7},{2,4},{3,5},{4,2},{5,3},{6,0},{7,1},{8,14},{9,15},{10,... | collective-permute-start | bytes 1105928 | tf_op jit(solution)/shard_map/ppermute | solution.py:760
  (50 other events, 354.7 us)
